TPU v7x, 32 devices: a whole 2x2x4 slice. The times are simulated.
32 devices in a mesh: groups: 2 (over y), ra: 4 (over z), dec: 2 (over x), band: 2 (over core).
Axes of the slice: x: 2, y: 2, z: 4, core: 2. Of those that a mesh axis runs over, the one named last changes fastest.
Arguments:
- sky_maps: bfloat16 [512, 312, 256], P(('groups', 'band'), 'ra', 'dec'), parts along dimension 0, may hold values from -12 to 12
- radii: int32 [512], P(('groups', 'band')), parts along dimension 0, may hold values from 1 to 17, as said below
- valid: int32 [624, 256], P(('groups', 'ra'), 'dec'), parts along dimension 0, may hold values from 0 to 1, as said below
Outputs:
- smoothed: bfloat16 [512, 312, 256], P(('groups', 'band'), 'ra', 'dec'), parts along dimension 0
- channel_mean: float32 [512], P(('groups', 'band')), parts along dimension 0
- covariance: float32 [512, 256], P('groups', 'band'), parts along dimension 0
There are 2 independent parts, one for each index of `groups`. A program takes and returns all parts, laid end to end along the dimension named above; each array names one. Nothing has to cross between parts.
Inputs may be any that keep to these rules, and one draw needn't show every extreme that they name: `radii`: some channel has half-width exactly 17. 1 marks a pixel that enters the statistics; the pixel with declination index 0 is valid in every row.
All inputs are finite; a program needn't handle non-finite values.
Results may differ from a plain program's by a relative error of at most 0.012.
The roundings to bfloat16 on the way count: a program that leaves them out, or rounds other values in their place, can miss the bound.
Values may be sent and summed in bfloat16 or wider, within the bound.
No kernel may reach another device: no remote copies, remote signals or barrier semaphores. Data moves between devices by JAX's collectives and lax.ppermute only.
A program may use at most 64 MiB of HBM per device.

v0:
```python
import jax
import jax.numpy as jnp
from jax import lax
from jax.sharding import PartitionSpec as P

RMAX = 17


def extended(array, sides, width, wrap):
    for axis, dim in sides:
        peers, length = (lax.axis_size(axis), array.shape[dim])
        up = [(i, (i + 1) % peers) for i in range(peers if wrap else peers - 1)]
        down = [(j, i) for i, j in up]
        last = lax.slice_in_dim(array, length - width, length, axis=dim)
        initial = lax.slice_in_dim(array, 0, width, axis=dim)
        before = lax.ppermute(last, axis, up)
        after = lax.ppermute(initial, axis, down)
        array = jnp.concatenate([before, array, after], axis=dim)
    return array


def beam_taps(radii, offsets):
    radius = radii.astype(jnp.float32)
    lead_shape = (radii.shape[0],) + (1,) * offsets.ndim
    radius = radius.reshape(lead_shape)
    spread = 0.5 * radius
    inside = jnp.abs(offsets)[None] <= radius
    return jnp.where(inside, jnp.exp(-(offsets * offsets)[None] / (2.0 * spread * spread)), 0.0)


def banded(radii, inner_count, outer_count):
    raw_taps = beam_taps(radii, jnp.arange(-RMAX, RMAX + 1).astype(jnp.float32))
    tap_total = jnp.sum(raw_taps, axis=1)
    offsets = (
        lax.broadcasted_iota(jnp.int32, (inner_count, outer_count), 0)
        - lax.broadcasted_iota(jnp.int32, (inner_count, outer_count), 1)
        - RMAX
    ).astype(jnp.float32)
    return (beam_taps(radii, offsets) / tap_total[:, None, None]).astype(jnp.bfloat16)


def local_sums(maps, mask_values):
    flat = maps.reshape(maps.shape[0], -1)
    weights = mask_values.reshape(-1)
    masked = flat * weights.astype(jnp.bfloat16)[None]
    sums = jnp.sum(masked.astype(jnp.float32), axis=1)
    return (masked, sums, jnp.sum(weights))


def per_device(sky_maps, radii, valid):
    channel_count, pixel_rows, pixel_cols = sky_maps.shape
    dec_band = banded(radii, pixel_cols + 2 * RMAX, pixel_cols)
    ra_band = banded(radii, pixel_rows + 2 * RMAX, pixel_rows)
    wrapped = extended(sky_maps, (("ra", 1),), RMAX, True)
    framed = extended(wrapped, (("dec", 2),), RMAX, False)
    across = jnp.einsum(
        "cxz,czy->cxy", framed, dec_band, preferred_element_type=jnp.float32
    ).astype(jnp.bfloat16)
    smoothed = jnp.einsum(
        "czy,czw->cwy", across, ra_band, preferred_element_type=jnp.float32
    ).astype(jnp.bfloat16)
    mask_values = valid.astype(jnp.float32)
    first_channel = lax.axis_index("band") * channel_count
    every = lax.all_gather(smoothed, "band", axis=0, tiled=True)
    masked, sums, count = local_sums(every, mask_values)
    own_rows = lax.dynamic_slice_in_dim(masked, first_channel, channel_count, 0)
    block = lax.dot_general(
        masked, own_rows, (((1,), (1,)), ((), ())), preferred_element_type=jnp.float32
    )
    sums, count, block = lax.psum((sums, count, block), ("ra", "dec"))
    mean_all = sums / count
    channel_mean = lax.dynamic_slice_in_dim(mean_all, first_channel, channel_count, 0)
    covariance = (block - count * mean_all[:, None] * channel_mean[None, :]) / (count - 1.0)
    return (smoothed, channel_mean, covariance)


def solution(mesh):
    return jax.shard_map(
        per_device,
        mesh=mesh,
        in_specs=(
            P(("groups", "band"), "ra", "dec"),
            P(("groups", "band")),
            P(("groups", "ra"), "dec"),
        ),
        out_specs=(P(("groups", "band"), "ra", "dec"), P(("groups", "band")), P("groups", "band")),
        check_vma=False,
    )
```

profile of v0, /device:TPU:0, one launch (start us, length us, event | category | flops | bytes accessed | tf_op | source)
XLA Modules:
  0.0 190.9 jit_solution(9157227778549513392)
XLA Ops:
  7.2 1.3 fusion.54
  8.5 3.1 %collective-permute-start = (bf16[128,17,128]{2,0,1:T(8,128)(2,1)S(1)}, bf16[128,17,128]{2,0,1:T(8,128)(2,1)S(1)}, u32[]{:S(2)}, u32[]{:S(2)}) collective-permute-start(bf16[128,17,128]{2,0,1:T(8,128)(2,1)S(1)} %get-tuple-element.24), channel_id=1, source_target_pairs={{0,4},{4,8},{8,12},{12,0},{1,5},{5,9},{9,13},{13,1},{2,6},{6,10},{... | collective-permute-start | bytes 1671176 | tf_op jit(solution)/shard_map/ppermute | solution.py:16
  11.6 2.1 %collective-permute-start.1 = (bf16[128,17,128]{2,0,1:T(8,128)(2,1)S(1)}, bf16[128,17,128]{2,0,1:T(8,128)(2,1)S(1)}, u32[]{:S(2)}, u32[]{:S(2)}) collective-permute-start(bf16[128,17,128]{2,0,1:T(8,128)(2,1)S(1)} %get-tuple-element.25), channel_id=1, source_target_pairs={{4,0},{8,4},{12,8},{0,12},{5,1},{9,5},{13,9},{1,13},{6,2},{10,6},{... | collective-permute-start | bytes 1671176 | tf_op jit(solution)/shard_map/ppermute | solution.py:17
  13.7 6.1 %copy.30 = bf16[128,78,128]{1,2,0:T(8,128)(2,1)} copy(bf16[128,78,128]{2,0,1:T(8,128)(2,1)} %param.3) | data formatting | bytes 5111808 | tf_op args[0]
  20.5 6.7 %collective-permute-done = bf16[128,17,128]{2,0,1:T(8,128)(2,1)S(1)} collective-permute-done((bf16[128,17,128]{2,0,1:T(8,128)(2,1)S(1)}, bf16[128,17,128]{2,0,1:T(8,128)(2,1)S(1)}, u32[]{:S(2)}, u32[]{:S(2)}) %collective-permute-start) | collective-permute-done | bytes 557088 | tf_op jit(solution)/shard_map/ppermute | solution.py:16
  27.1 3.3 %copy.29 = bf16[128,17,128]{1,2,0:T(8,128)(2,1)} copy(bf16[128,17,128]{2,0,1:T(8,128)(2,1)S(1)} %collective-permute-done) | data formatting | bytes 1114112 | tf_op jit(solution)/shard_map/ppermute | solution.py:16
  30.4 7.2 %collective-permute-done.1 = bf16[128,17,128]{2,0,1:T(8,128)(2,1)S(1)} collective-permute-done((bf16[128,17,128]{2,0,1:T(8,128)(2,1)S(1)}, bf16[128,17,128]{2,0,1:T(8,128)(2,1)S(1)}, u32[]{:S(2)}, u32[]{:S(2)}) %collective-permute-start.1) | collective-permute-done | bytes 557088 | tf_op jit(solution)/shard_map/ppermute | solution.py:17
  37.6 3.3 %copy.31 = bf16[128,17,128]{1,2,0:T(8,128)(2,1)} copy(bf16[128,17,128]{2,0,1:T(8,128)(2,1)S(1)} %collective-permute-done.1) | data formatting | bytes 1114112 | tf_op jit(solution)/shard_map/ppermute | solution.py:17
  40.9 4.2 %pad_maximum_fusion.2 = (bf16[128,112,17]{1,2,0:T(8,128)(2,1)S(1)}, bf16[128,112,17]{1,2,0:T(8,128)(2,1)S(1)}) fusion(bf16[128,17,128]{1,2,0:T(8,128)(2,1)} %copy.31, bf16[128,78,128]{1,2,0:T(8,128)(2,1)} %copy.30, bf16[128,17,128]{1,2,0:T(8,128)(2,1)} %copy.29), kind=kLoop, calls=%fused_computation.39 | loop fusion | flops 2924544 | bytes 4644864 | tf_op jit(solution)/shard_map/slice | solution.py:14
  45.5 3.4 %collective-permute-start.2 = (bf16[128,112,17]{0,1,2:T(8,128)(2,1)S(1)}, bf16[128,112,17]{0,1,2:T(8,128)(2,1)S(1)}, u32[]{:S(2)}, u32[]{:S(2)}) collective-permute-start(bf16[128,112,17]{0,1,2:T(8,128)(2,1)S(1)} %copy.32), channel_id=1, source_target_pairs={{0,2},{1,3},{4,6},{5,7},{8,10},{9,11},{12,14},{13,15},{16,18},{17,... | collective-permute-start | bytes 1462280 | tf_op jit(solution)/shard_map/ppermute | solution.py:16
  49.4 1.3 collective-permute-start.3
  51.5 7.3 %collective-permute-done.2 = bf16[128,112,17]{0,1,2:T(8,128)(2,1)S(1)} collective-permute-done((bf16[128,112,17]{0,1,2:T(8,128)(2,1)S(1)}, bf16[128,112,17]{0,1,2:T(8,128)(2,1)S(1)}, u32[]{:S(2)}, u32[]{:S(2)}) %collective-permute-start.2) | collective-permute-done | bytes 487456 | tf_op jit(solution)/shard_map/ppermute | solution.py:16
  59.3 4.2 %collective-permute-done.3 = bf16[128,112,17]{0,1,2:T(8,128)(2,1)S(1)} collective-permute-done((bf16[128,112,17]{0,1,2:T(8,128)(2,1)S(1)}, bf16[128,112,17]{0,1,2:T(8,128)(2,1)S(1)}, u32[]{:S(2)}, u32[]{:S(2)}) %collective-permute-start.3) | collective-permute-done | bytes 487456 | tf_op jit(solution)/shard_map/ppermute | solution.py:17
  63.5 1.2 copy.35
  64.7 13.9 %fusion.34 = bf16[128,78,128]{2,1,0:T(8,128)(2,1)S(1)} fusion(f32[128]{0:T(128)S(1)} %fusion.48, f32[128]{0:T(128)S(1)} %multiply_multiply_fusion, f32[112,78]{0,1:T(8,128)S(1)} %get-tuple-element.30, f32[112,78]{0,1:T(8,128)} %get-tuple-element.31, f32[128]{0:T(128)S(1)} %convert_element_type.74, bf16[128,112,17]{1,2,0:T(8,128)(2,1)} %copy.35, ...), kind=kOutput, calls=%fused_computation.36 | convolution fusion | flops 926003200 | bytes 7438080 | tf_op jit(solution)/shard_map/czy,czw->cwy/dot_general | solution.py:59
  78.7 2.1 %copy.38 = bf16[128,78,128]{2,0,1:T(8,128)(2,1)} copy(bf16[128,78,128]{2,1,0:T(8,128)(2,1)S(1)} %fusion.34) | data formatting | bytes 5111808
  81.7 13.3 %all-gather.2.cloned.1.call-done = bf16[256,78,128]{2,0,1:T(8,128)(2,1)} async-done(((bf16[128,78,128]{2,0,1:T(8,128)(2,1)}), bf16[256,78,128]{2,0,1:T(8,128)(2,1)}) %all-gather.2.cloned.1.call-update) | async-done | bytes 5111824 | tf_op jit(solution)/shard_map/all_gather | solution.py:64
  95.0 7.7 %copy.37 = bf16[256,78,128]{0,2,1:T(8,128)(2,1)} copy(bf16[256,78,128]{2,0,1:T(8,128)(2,1)} %all-gather.2.cloned.1.call-done) | data formatting | bytes 10223616 | tf_op jit(solution)/shard_map/all_gather | solution.py:64
  102.8 6.3 %bitcast_multiply_fusion = bf16[256,9984]{0,1:T(8,128)(2,1)S(1)} fusion(bf16[256,78,128]{0,2,1:T(8,128)(2,1)} %copy.37, bf16[9984]{0:T(1024)(128)(2,1)S(1)} %fusion.56), kind=kLoop, calls=%fused_computation.25 | loop fusion | flops 2555904 | bytes 10243584 | tf_op jit(solution)/shard_map/mul | solution.py:45
  109.0 2.3 %fusion.32 = f32[256,128]{1,0:T(8,128)} fusion(bf16[256,9984]{0,1:T(8,128)(2,1)S(1)} %bitcast_multiply_fusion, s32[]{:T(128)S(6)} %select_n.20), kind=kOutput, calls=%fused_computation.34 | convolution fusion | flops 654311424 | bytes 7798788 | tf_op jit(solution)/shard_map/dot_general | solution.py:67
  111.3 3.7 %convert_reduce_fusion = f32[256]{0:T(256)S(1)} fusion(bf16[256,78,128]{2,0,1:T(8,128)(2,1)} %all-gather.2.cloned.1.call-done, bf16[78,128]{1,0:T(8,128)(2,1)S(1)} %convert_convert_fusion), kind=kLoop, calls=%fused_computation.4 | loop fusion | flops 7667456 | bytes 5132800 | tf_op jit(solution)/shard_map/reduce_sum | solution.py:46
  115.0 22.4 %all-reduce = (f32[256]{0:T(256)S(1)}, f32[]{:T(128)}) all-reduce(f32[256]{0:T(256)S(1)} %convert_reduce_fusion, f32[]{:T(128)} %convert_reduce_fusion.1), channel_id=1, replica_groups=mesh['groups'=2,'ra'=4,'dec'=2,'band'=2] {'ra','dec'}, use_global_device_ids=true, to_apply=%region_2.3 | all-reduce | flops 257 | bytes 2056 | tf_op jit(solution)/shard_map/psum | solution.py:70
  138.6 43.8 %all-reduce.3.cloned.1.call-done = f32[256,128]{1,0:T(8,128)} async-done(((f32[256,128]{1,0:T(8,128)}), f32[256,128]{1,0:T(8,128)}) %all-reduce.3.cloned.1.call-update) | async-done | bytes 131088 | tf_op jit(solution)/shard_map/psum | solution.py:70
  182.3 1.7 subtract_divide_fusion
  (24 shorter events, 4.3 us)
Async XLA Ops:
  7.2 87.9 %all-gather.2.cloned.1.call-start = ((), (), s32[]{:S(2)}) async-start(), calls=%async_computation | async-start | bytes 7667712 | tf_op jit(solution)/shard_map/all_gather | solution.py:64
  8.5 18.6 %collective-permute-start = (bf16[128,17,128]{2,0,1:T(8,128)(2,1)S(1)}, bf16[128,17,128]{2,0,1:T(8,128)(2,1)S(1)}, u32[]{:S(2)}, u32[]{:S(2)}) collective-permute-start(bf16[128,17,128]{2,0,1:T(8,128)(2,1)S(1)} %get-tuple-element.24), channel_id=1, source_target_pairs={{0,4},{4,8},{8,12},{12,0},{1,5},{5,9},{9,13},{13,1},{2,6},{6,10},{... | collective-permute-start | bytes 1671176 | tf_op jit(solution)/shard_map/ppermute | solution.py:16
  11.6 26.0 %collective-permute-start.1 = (bf16[128,17,128]{2,0,1:T(8,128)(2,1)S(1)}, bf16[128,17,128]{2,0,1:T(8,128)(2,1)S(1)}, u32[]{:S(2)}, u32[]{:S(2)}) collective-permute-start(bf16[128,17,128]{2,0,1:T(8,128)(2,1)S(1)} %get-tuple-element.25), channel_id=1, source_target_pairs={{4,0},{8,4},{12,8},{0,12},{5,1},{9,5},{13,9},{1,13},{6,2},{10,6},{... | collective-permute-start | bytes 1671176 | tf_op jit(solution)/shard_map/ppermute | solution.py:17
  40.9 9.9 %copy-start.2 = (s32[128]{0:T(128)S(1)}, s32[128]{0:T(128)}, u32[]{:S(2)}) copy-start(s32[128]{0:T(128)} %param.4) | copy-start | bytes 1540
  45.5 13.3 %collective-permute-start.2 = (bf16[128,112,17]{0,1,2:T(8,128)(2,1)S(1)}, bf16[128,112,17]{0,1,2:T(8,128)(2,1)S(1)}, u32[]{:S(2)}, u32[]{:S(2)}) collective-permute-start(bf16[128,112,17]{0,1,2:T(8,128)(2,1)S(1)} %copy.32), channel_id=1, source_target_pairs={{0,2},{1,3},{4,6},{5,7},{8,10},{9,11},{12,14},{13,15},{16,18},{17,... | collective-permute-start | bytes 1462280 | tf_op jit(solution)/shard_map/ppermute | solution.py:16
  49.4 14.0 %collective-permute-start.3 = (bf16[128,112,17]{0,1,2:T(8,128)(2,1)S(1)}, bf16[128,112,17]{0,1,2:T(8,128)(2,1)S(1)}, u32[]{:S(2)}, u32[]{:S(2)}) collective-permute-start(bf16[128,112,17]{0,1,2:T(8,128)(2,1)S(1)} %copy.33), channel_id=1, source_target_pairs={{2,0},{3,1},{6,4},{7,5},{10,8},{11,9},{14,12},{15,13},{18,16},{19,... | collective-permute-start | bytes 1462280 | tf_op jit(solution)/shard_map/ppermute | solution.py:17
  78.7 2.4 %copy-start = (s32[78,128]{1,0:T(8,128)S(1)}, s32[78,128]{1,0:T(8,128)}, u32[]{:S(2)}) copy-start(s32[78,128]{1,0:T(8,128)} %param.5) | copy-start | bytes 119812
  80.9 101.5 %all-reduce.3.cloned.1.call-start = ((), (), s32[]{:S(2)}) async-start(), calls=%async_computation.1 | async-start | bytes 262144 | tf_op jit(solution)/shard_map/psum | solution.py:70
  138.0 46.0 %copy-start.1 = (f32[128]{0:T(128)}, f32[128]{0:T(128)S(1)}, u32[]{:S(2)}) copy-start(f32[128]{0:T(128)S(1)} %dynamic_slice.6) | copy-start | bytes 1540
Sparse Core Ops, SparseCore 0:
  81.0 13.9 all-gather.1
  111.4 70.8 all-reduce.2
where the time goes:
time: 191 us
  waiting for transfers between devices  82.4 us (43%)
  local copies, waits for them, and re-layouts  26.6 us (14%)
  blocking collectives  22.4 us (12%)
  other arithmetic  18.3 us (10%)
  matrix products  16.2 us (8%)
  between operations  14.7 us (8%)
  starting transfers between devices  10.1 us (5%)
    psum x1, waiting for transfers between devices, per_device(): sums, count, block = lax.psum((sums, count, block), ('ra', 'dec'))  43.8 us
    psum x1, blocking collectives, per_device(): sums, count, block = lax.psum((sums, count, block), ('ra', 'dec'))  22.4 us
    ppermute x2, waiting for transfers between devices, extended(): before = lax.ppermute(last, axis, up)  14 us
    dot_general x1, matrix products, per_device(): jnp.einsum('czy,czw->cwy', across, ra_band, preferred_element_type=jnp.fl...  13.9 us
    all_gather x1, waiting for transfers between devices, per_device(): every = lax.all_gather(smoothed, 'band', axis=0, tiled=True)  13.3 us
    ppermute x2, waiting for transfers between devices, extended(): after = lax.ppermute(initial, axis, down)  11.4 us
    unnamed x8, local copies, waits for them, and re-layouts  8.3 us
    all_gather x1, local copies, waits for them, and re-layouts, per_device(): every = lax.all_gather(smoothed, 'band', axis=0, tiled=True)  7.73 us
  transfers between devices with their start and end apart: 6, of which 6 were waited for; matrix products, arithmetic and copies ran while one was open for 9% of the time, Pallas kernels for 0%

commit v1 on v0

v1 whole, which is shorter than its diff:
```python
import functools

import jax
import jax.numpy as jnp
from jax import lax
from jax.experimental import pallas as pl
from jax.experimental.pallas import tpu as pltpu
from jax.sharding import PartitionSpec as P

RMAX = 17
LANES = 128
SLOTS = LANES // RMAX
VMEM_LIMIT = 60 * 1024 * 1024
BF16, F32 = jnp.bfloat16, jnp.float32


def row_groups(rows):
    edge = -(-RMAX // SLOTS)
    head = [(g * SLOTS, SLOTS) for g in range(edge)]
    tail = [(rows - (edge - g) * SLOTS, SLOTS) for g in range(edge)]
    middle, start, stop = [], edge * SLOTS, rows - edge * SLOTS
    while start < stop:
        count = min(SLOTS, stop - start)
        middle.append((start, count))
        start += count
    return head + middle + tail, edge


def taps_at(radius, offsets, total):
    spread = 0.5 * radius
    inside = jnp.abs(offsets) <= radius
    raw = jnp.where(inside, jnp.exp(-(offsets * offsets) / (2.0 * spread * spread)), 0.0)
    return raw if total is None else raw / total


def prepare_kernel(rows, sides, x_ref, dec_ref, ra_ref, *edge_refs):
    cols = x_ref.shape[2]
    dec = lax.axis_index("dec")
    line = lax.broadcasted_iota(jnp.int32, (8, LANES), 1) - RMAX
    z = lax.broadcasted_iota(jnp.int32, (2 * LANES, cols), 0)
    y = lax.broadcasted_iota(jnp.int32, (2 * LANES, cols), 1)
    before, after = z - LANES - RMAX, z - 2 * LANES - RMAX + LANES + cols
    if sides == 1:
        column = jnp.where(z < LANES, z, jnp.where(dec == 0, z - LANES + cols, before))
        used = z < LANES + RMAX
    else:
        column = jnp.where(z < LANES, z, jnp.where(z < LANES + RMAX, before, after))
        used = z < LANES + 2 * RMAX
    dec_offset = jnp.where(used, column - y, 2 * LANES).astype(F32)
    out = lax.broadcasted_iota(jnp.int32, ra_ref.shape[1:], 0)
    source = lax.broadcasted_iota(jnp.int32, ra_ref.shape[1:], 1)
    ra_offset = (source - out - RMAX).astype(F32)

    def one_radius(index, carry):
        radius = index.astype(F32)
        total = jnp.sum(taps_at(radius, line.astype(F32), None)) / 8.0
        dec_ref[index] = taps_at(radius, dec_offset, total).astype(BF16)
        ra_ref[index] = taps_at(radius, ra_offset, total).astype(BF16)
        return carry

    lax.fori_loop(1, RMAX + 1, one_radius, 0)
    lane = lax.broadcasted_iota(jnp.int32, x_ref.shape[1:], 1)
    groups, _ = row_groups(rows)
    for side, edge_ref in enumerate(edge_refs):
        if sides == 1:
            first = jnp.where(dec == 0, cols - RMAX, 0)
        else:
            first = cols - RMAX if side == 0 else 0
        for g, (start, count) in enumerate(groups):
            packed = jnp.zeros(x_ref.shape[1:], F32)
            for j in range(count):
                shift = lax.rem(RMAX * j - first + 2 * LANES, LANES)
                piece = pltpu.roll(x_ref[start + j].astype(F32), shift, 1)
                packed = piece if j == 0 else jnp.where(lane < RMAX * j, packed, piece)
            edge_ref[g] = packed.astype(BF16)


def prepare(x, sides):
    rows, chans, cols = x.shape
    count = len(row_groups(rows)[0])
    out_rows = -(-rows // 16) * 16
    shapes = [
        jax.ShapeDtypeStruct((RMAX + 1, 2 * LANES, cols), BF16),
        jax.ShapeDtypeStruct((RMAX + 1, out_rows, rows + 2 * RMAX), BF16),
    ] + [jax.ShapeDtypeStruct((count, chans, LANES), BF16)] * sides
    return pl.pallas_call(
        functools.partial(prepare_kernel, rows, sides),
        out_shape=shapes,
        in_specs=[pl.BlockSpec(memory_space=pltpu.VMEM)],
        out_specs=[pl.BlockSpec(memory_space=pltpu.VMEM)] * len(shapes),
        compiler_params=pltpu.CompilerParams(vmem_limit_bytes=VMEM_LIMIT),
        cost_estimate=pl.CostEstimate(flops=10**7, bytes_accessed=6 * 10**6, transcendentals=10**6),
    )(x)


def smooth_kernel(sides, rad_ref, x_ref, before_ref, after_ref, dec_ref, ra_ref, *refs):
    edge_refs, out_ref, own, halo, result = refs[:3 * sides], *refs[3 * sides:]
    rows, chans, _ = x_ref.shape
    frame = rows + 2 * RMAX

    def put(row, value):
        own[pl.ds(row * chans, chans), :] = value.astype(F32)

    def copy_rows(ref, base, count):
        def body(i, carry):
            put(base + i, ref[i])
            return carry

        lax.fori_loop(0, count, body, 0)

    copy_rows(before_ref, 0, RMAX)
    copy_rows(x_ref, RMAX, rows)
    copy_rows(after_ref, RMAX + rows, RMAX)

    lane = lax.broadcasted_iota(jnp.int32, (chans, LANES), 1)
    groups, edge = row_groups(rows)

    def unpack(row, part, g, j):
        value = None
        for side in range(sides):
            tile = edge_refs[3 * side + part][g].astype(F32)
            shift = (RMAX * side - RMAX * j) % LANES
            tile = tile if shift == 0 else pltpu.roll(tile, shift, 1)
            value = tile if side == 0 else jnp.where(lane < RMAX, value, tile)
        halo[pl.ds(row * chans, chans), :] = value

    for g, (start, count) in enumerate(groups):
        for j in range(count):
            unpack(RMAX + start + j, 0, g, j)
    for g, (start, count) in enumerate(groups[-edge:]):
        for j in range(count):
            if start + j >= rows - RMAX:
                unpack(start + j - (rows - RMAX), 1, g, j)
    for g, (start, count) in enumerate(groups[:edge]):
        for j in range(count):
            if start + j < RMAX:
                unpack(RMAX + rows + start + j, 2, g, j)

    def one_channel(c, carry):
        radius = rad_ref[c]
        picked = pl.ds(c, frame, stride=chans)
        lhs = jnp.concatenate([own[picked, :].astype(BF16), halo[picked, :].astype(BF16)], axis=1)
        partial = jnp.dot(lhs, dec_ref[radius], preferred_element_type=F32).astype(BF16)
        smoothed = jnp.dot(ra_ref[radius], partial, preferred_element_type=F32)
        result[pl.ds(c, rows, stride=chans), :] = smoothed[:rows]
        return carry

    lax.fori_loop(0, chans, one_channel, 0, unroll=8)

    def store(i, carry):
        out_ref[i] = result[pl.ds(i * chans, chans), :].astype(BF16)
        return carry

    lax.fori_loop(0, rows, store, 0)


def smooth(radii, x, before, after, dec_table, ra_table, edges):
    rows, chans, cols = x.shape
    frame = rows + 2 * RMAX
    operands = [x, before, after, dec_table, ra_table] + [part for side in edges for part in side]
    return pl.pallas_call(
        functools.partial(smooth_kernel, len(edges)),
        out_shape=jax.ShapeDtypeStruct(x.shape, BF16),
        in_specs=[pl.BlockSpec(memory_space=pltpu.SMEM)] + [pl.BlockSpec(memory_space=pltpu.VMEM)] * len(operands),
        out_specs=pl.BlockSpec(memory_space=pltpu.VMEM),
        scratch_shapes=[
            pltpu.VMEM((frame * chans, cols), F32),
            pltpu.VMEM((frame * chans, LANES), F32),
            pltpu.VMEM((rows * chans, cols), F32),
        ],
        compiler_params=pltpu.CompilerParams(vmem_limit_bytes=VMEM_LIMIT),
        cost_estimate=pl.CostEstimate(flops=4 * 10**9, bytes_accessed=10**7, transcendentals=0),
    )(radii, *operands)


ROWS_OF_SUMS = 8


def gram_kernel(own_ref, other_ref, valid_ref, out_ref):
    rows, chans, cols = own_ref.shape
    band = lax.axis_index("band")
    weights = valid_ref[...].astype(F32)

    def nt(a, b):
        return lax.dot_general(a, b, (((1,), (1,)), ((), ())), preferred_element_type=F32)

    def body(i, carry):
        own_gram, other_gram, own_sum, other_sum = carry
        w = valid_ref[pl.ds(i, 1), :].astype(BF16)
        wide = jnp.broadcast_to(w, (ROWS_OF_SUMS, cols))
        own, other = own_ref[i], other_ref[i]
        masked = own * w
        return (
            own_gram + nt(own, masked),
            other_gram + nt(other, masked),
            own_sum + nt(wide, own),
            other_sum + nt(wide, other),
        )

    square = jnp.zeros((chans, chans), F32)
    line = jnp.zeros((ROWS_OF_SUMS, chans), F32)
    own_gram, other_gram, own_sum, other_sum = lax.fori_loop(0, rows, body, (square, square, line, line))
    out_ref[pl.ds(pl.multiple_of(band * chans, chans), chans), :] = own_gram
    out_ref[pl.ds(pl.multiple_of((1 - band) * chans, chans), chans), :] = other_gram
    row = lax.broadcasted_iota(jnp.int32, (ROWS_OF_SUMS, chans), 0)
    sums = jnp.where(row == band, own_sum, other_sum)
    out_ref[2 * chans:, :] = jnp.where(row == 2, jnp.sum(weights), sums)


def gram(own, other, valid):
    chans = own.shape[1]
    return pl.pallas_call(
        gram_kernel,
        out_shape=jax.ShapeDtypeStruct((2 * chans + ROWS_OF_SUMS, chans), F32),
        in_specs=[pl.BlockSpec(memory_space=pltpu.VMEM)] * 3,
        out_specs=pl.BlockSpec(memory_space=pltpu.VMEM),
        compiler_params=pltpu.CompilerParams(vmem_limit_bytes=VMEM_LIMIT),
    )(own, other, valid)


def finish_kernel(mine_ref, theirs_ref, mean_ref, cov_ref):
    chans = mine_ref.shape[1]
    band = lax.axis_index("band")
    block = mine_ref[:2 * chans, :] + theirs_ref[:2 * chans, :]
    tail = mine_ref[2 * chans:, :] + theirs_ref[2 * chans:, :]
    count = tail[2:3, 0:1]
    means = tail / count
    own = jnp.where(band == 0, means[0:1, :], means[1:2, :])
    mean_ref[...] = own
    for b in range(2):
        column = jnp.transpose(jnp.broadcast_to(means[b:b + 1, :], (chans, chans)))
        part = block[b * chans:(b + 1) * chans]
        cov_ref[b * chans:(b + 1) * chans, :] = (part - count * column * own) / (count - 1.0)


def finish(mine, theirs):
    chans = mine.shape[1]
    mean, covariance = pl.pallas_call(
        finish_kernel,
        out_shape=[jax.ShapeDtypeStruct((1, chans), F32), jax.ShapeDtypeStruct((2 * chans, chans), F32)],
        in_specs=[pl.BlockSpec(memory_space=pltpu.VMEM)] * 2,
        out_specs=[pl.BlockSpec(memory_space=pltpu.VMEM)] * 2,
        compiler_params=pltpu.CompilerParams(vmem_limit_bytes=VMEM_LIMIT),
    )(mine, theirs)
    return mean.reshape(chans), covariance


def swap(array, axis, step):
    size = lax.axis_size(axis)
    return lax.ppermute(array, axis, [(i, i ^ step) for i in range(size)])


def per_device(sky_maps, radii, valid):
    x = jnp.transpose(sky_maps, (1, 0, 2))
    rows = x.shape[0]
    ra_size, dec_size = lax.axis_size("ra"), lax.axis_size("dec")
    up = [(i, (i + 1) % ra_size) for i in range(ra_size)]
    down = [(j, i) for i, j in up]
    before = lax.ppermute(x[rows - RMAX:], "ra", up)
    after = lax.ppermute(x[:RMAX], "ra", down)

    sides = 1 if dec_size == 2 else 2
    dec_table, ra_table, *packed = prepare(x, sides)
    if sides == 1:
        halos = [swap(packed[0], "dec", 1)]
    else:
        right = [(i, i + 1) for i in range(dec_size - 1)]
        left = [(j, i) for i, j in right]
        halos = [lax.ppermute(p, "dec", perm) for p, perm in zip(packed, (right, left))]
    edge = row_groups(rows)[1]
    edges = [(h, lax.ppermute(h[-edge:], "ra", up), lax.ppermute(h[:edge], "ra", down)) for h in halos]

    smoothed = smooth(radii, x, before, after, dec_table, ra_table, edges)
    total = gram(smoothed, swap(smoothed, "band", 1), valid)
    steps = [("dec", 1 << b) for b in range(dec_size.bit_length() - 1)]
    steps += [("ra", 1 << b) for b in range(ra_size.bit_length() - 1)]
    for axis, step in steps[:-1]:
        total = total + swap(total, axis, step)
    mean, covariance = finish(total, swap(total, *steps[-1]))
    return (jnp.transpose(smoothed, (1, 0, 2)), mean, covariance)


def solution(mesh):
    return jax.shard_map(
        per_device,
        mesh=mesh,
        in_specs=(
            P(("groups", "band"), "ra", "dec"),
            P(("groups", "band")),
            P(("groups", "ra"), "dec"),
        ),
        out_specs=(P(("groups", "band"), "ra", "dec"), P(("groups", "band")), P("groups", "band")),
        check_vma=False,
    )
```

time: 191 us -> 127 us (0.66)
  Pallas kernels: 0 us -> 61.6 us
  waiting for transfers between devices: 82.4 us -> 45 us
  blocking collectives: 22.4 us -> 0 us
  local copies, waits for them, and re-layouts: 26.6 us -> 4.44 us
  other arithmetic: 18.3 us -> 0.95 us
  matrix products: 16.2 us -> 0 us
  between operations: 14.7 us -> 0.69 us
  starting transfers between devices: 10.1 us -> 13.7 us
    pallas_call x0 -> x4, Pallas kernels: none -> 61.6 us  [the longest x1 34.7 us: smooth(): pl.pallas_call(functools.partial(smooth_kernel, len(edges)), out_shape=ja...]
    psum x1 -> x0, waiting for transfers between devices: 43.8 us -> none  [per_device(): sums, count, block = lax.psum((sums, count, block), ('ra', 'dec'))]
    psum x1 -> x0, blocking collectives: 22.4 us -> none  [per_device(): sums, count, block = lax.psum((sums, count, block), ('ra', 'dec'))]
    ppermute x4 -> x9, waiting for transfers between devices: 25.3 us -> 45 us  [the longest x5 24.6 us: swap(): return lax.ppermute(array, axis, [(i, i ^ step) for i in range(size)])]
    dot_general x2 -> x0, matrix products: 16.2 us -> none  [the longest x1 13.9 us: per_device(): jnp.einsum('czy,czw->cwy', across, ra_band, preferred_element_type=jnp.fl...]
    all_gather x1 -> x0, waiting for transfers between devices: 13.3 us -> none  [per_device(): every = lax.all_gather(smoothed, 'band', axis=0, tiled=True)]
    ppermute x4 -> x0, local copies, waits for them, and re-layouts: 8.28 us -> none  [the longest x2 4.53 us: extended(): after = lax.ppermute(initial, axis, down)]
    all_gather x1 -> x0, local copies, waits for them, and re-layouts: 7.73 us -> none  [per_device(): every = lax.all_gather(smoothed, 'band', axis=0, tiled=True)]
  transfers between devices with their start and end apart: 6 -> 9, of which waited for: 6 -> 7; matrix products, arithmetic and copies ran while one was open for 9% -> 1% of each run, Pallas kernels for 0% -> 0%
where the time goes in v1:
time: 127 us; the launch traced here: 126 us
  Pallas kernels  61.6 us (49%)
  waiting for transfers between devices  45 us (35%)
  starting transfers between devices  13.7 us (11%)
  local copies, waits for them, and re-layouts  4.44 us (3%)
    pallas_call x1, Pallas kernels, smooth(): pl.pallas_call(functools.partial(smooth_kernel, len(edges)), out_shape=ja...  34.7 us
    ppermute x5, waiting for transfers between devices, swap(): return lax.ppermute(array, axis, [(i, i ^ step) for i in range(size)])  24.6 us
    pallas_call x1, Pallas kernels, gram(): pl.pallas_call(gram_kernel, out_shape=jax.ShapeDtypeStruct((2 * chans + R...  19 us
    ppermute x1, waiting for transfers between devices, per_device(): lax.ppermute(h[:edge], 'ra', down)  18.4 us
    ppermute x5, starting transfers between devices, swap(): return lax.ppermute(array, axis, [(i, i ^ step) for i in range(size)])  6.14 us
    pallas_call x1, Pallas kernels, prepare(): pl.pallas_call(functools.partial(prepare_kernel, rows, sides), out_shape=...  6.06 us
    ppermute x1, starting transfers between devices, per_device(): lax.ppermute(h[:edge], 'ra', down)  3.91 us
    ppermute x1, starting transfers between devices, per_device(): after = lax.ppermute(x[:RMAX], 'ra', down)  3.65 us
  transfers between devices with their start and end apart: 9, of which 7 were waited for; matrix products, arithmetic and copies ran while one was open for 1% of the time, Pallas kernels for 0%

profile of v1, /device:TPU:0, one launch (start us, length us, event | category | flops | bytes accessed | tf_op | source)
XLA Modules:
  0.0 126.4 jit_solution(16751143261131317196)
XLA Ops:
  0.6 6.1 %shard_map.58 = (bf16[18,256,128]{2,1,0:T(8,128)(2,1)}, bf16[18,80,112]{2,1,0:T(8,128)(2,1)}, bf16[12,128,128]{2,1,0:T(8,128)(2,1)}) custom-call(bf16[78,128,128]{2,1,0:T(8,128)(2,1)} %bitcast.3), custom_call_target="tpu_custom_call" | custom-call | flops 10000000 | bytes 6000000 | tf_op jit(solution)/shard_map/pallas_call | solution.py:86
  6.7 2.9 %collective-permute-start.2 = (bf16[12,128,128]{2,1,0:T(8,128)(2,1)}, bf16[12,128,128]{2,1,0:T(8,128)(2,1)S(1)}, u32[]{:S(2)}, u32[]{:S(2)}) collective-permute-start(bf16[12,128,128]{2,1,0:T(8,128)(2,1)} %get-tuple-element.10), channel_id=1, source_target_pairs={{0,2},{2,0},{1,3},{3,1},{4,6},{6,4},{5,7},{7,5},{8,10},{10,8},{9,1... | collective-permute-start | bytes 1179656 | tf_op jit(solution)/shard_map/ppermute | solution.py:250
  9.6 1.3 %fusion = (bf16[17,128,128]{2,1,0:T(8,128)(2,1)S(1)}, bf16[17,128,128]{2,1,0:T(8,128)(2,1)S(1)}) fusion(bf16[78,128,128]{2,1,0:T(8,128)(2,1)} %bitcast.4), kind=kLoop, calls=%fused_computation | loop fusion | bytes 2228224 | tf_op jit(solution)/shard_map/slice | solution.py:260
  10.9 3.7 %collective-permute-start.1 = (bf16[17,128,128]{2,1,0:T(8,128)(2,1)S(1)}, bf16[17,128,128]{2,1,0:T(8,128)(2,1)S(1)}, u32[]{:S(2)}, u32[]{:S(2)}) collective-permute-start(bf16[17,128,128]{2,1,0:T(8,128)(2,1)S(1)} %get-tuple-element.13), channel_id=1, source_target_pairs={{4,0},{8,4},{12,8},{0,12},{5,1},{9,5},{13,9},{1,13},{6,2},{10,6},{... | collective-permute-start | bytes 1671176 | tf_op jit(solution)/shard_map/ppermute | solution.py:260
  14.6 4.4 %collective-permute-done.2.refs_0_ = bf16[12,128,128]{2,1,0:T(8,128)(2,1)S(1)} collective-permute-done((bf16[12,128,128]{2,1,0:T(8,128)(2,1)}, bf16[12,128,128]{2,1,0:T(8,128)(2,1)S(1)}, u32[]{:S(2)}, u32[]{:S(2)}) %collective-permute-start.2) | collective-permute-done | bytes 393248 | tf_op jit(solution)/shard_map/ppermute | solution.py:250
  19.0 3.9 %collective-permute-start.4 = (bf16[3,128,128]{2,1,0:T(8,128)(2,1)S(1)}, bf16[3,128,128]{2,1,0:T(8,128)(2,1)S(1)}, u32[]{:S(2)}, u32[]{:S(2)}) collective-permute-start(bf16[3,128,128]{2,1,0:T(8,128)(2,1)S(1)} %get-tuple-element.15), channel_id=1, source_target_pairs={{4,0},{8,4},{12,8},{0,12},{5,1},{9,5},{13,9},{1,13},{6,2},{10,6},{... | collective-permute-start | bytes 294920 | tf_op jit(solution)/shard_map/ppermute | solution.py:271
  22.9 18.4 %collective-permute-done.4.refs_2_ = bf16[3,128,128]{2,1,0:T(8,128)(2,1)S(1)} collective-permute-done((bf16[3,128,128]{2,1,0:T(8,128)(2,1)S(1)}, bf16[3,128,128]{2,1,0:T(8,128)(2,1)S(1)}, u32[]{:S(2)}, u32[]{:S(2)}) %collective-permute-start.4) | collective-permute-done | bytes 98336 | tf_op jit(solution)/shard_map/ppermute | solution.py:271
  41.3 2.0 %collective-permute-done.3.refs_1_ = bf16[3,128,128]{2,1,0:T(8,128)(2,1)S(1)} collective-permute-done((bf16[3,128,128]{2,1,0:T(8,128)(2,1)S(1)}, bf16[3,128,128]{2,1,0:T(8,128)(2,1)S(1)}, u32[]{:S(2)}, u32[]{:S(2)}) %collective-permute-start.3) | collective-permute-done | bytes 98336 | tf_op jit(solution)/shard_map/ppermute | solution.py:271
  43.3 0.6 copy-done.7
  43.9 0.2 copy-done.4
  44.1 0.2 copy-done.5
  44.3 34.7 %shard_map.59.own_ref = bf16[78,128,128]{2,1,0:T(8,128)(2,1)} custom-call(s32[128]{0:T(128)} %rad_ref.1, bf16[78,128,128]{2,1,0:T(8,128)(2,1)} %bitcast.5, bf16[17,128,128]{2,1,0:T(8,128)(2,1)} %copy-done.5, bf16[17,128,128]{2,1,0:T(8,128)(2,1)} %copy-done.4, bf16[18,256,128]{2,1,0:T(8,128)(2,1)} %get-tuple-element.8.dec_ref, ...), custom_call_target="tpu_custom_call" | custom-call | flops 4000000000 | bytes 10000000 | tf_op jit(solution)/shard_map/pallas_call | solution.py:161
  79.1 5.0 %collective-permute-done.5.other_ref = bf16[78,128,128]{2,1,0:T(8,128)(2,1)S(1)} collective-permute-done((bf16[78,128,128]{2,1,0:T(8,128)(2,1)}, bf16[78,128,128]{2,1,0:T(8,128)(2,1)S(1)}, u32[]{:S(2)}, u32[]{:S(2)}) %collective-permute-start.5) | collective-permute-done | bytes 2555936 | tf_op jit(solution)/shard_map/ppermute | solution.py:250
  84.1 1.5 %copy-done = bf16[78,128,128]{2,1,0:T(8,128)(2,1)} copy-done((bf16[78,128,128]{2,1,0:T(8,128)(2,1)}, bf16[78,128,128]{2,1,0:T(8,128)(2,1)S(1)}, u32[]{:S(2)}) %copy-start) | copy-done | bytes 2555928
  85.6 19.0 %shard_map.60 = f32[264,128]{1,0:T(8,128)} custom-call(bf16[78,128,128]{2,1,0:T(8,128)(2,1)} %shard_map.59.own_ref, bf16[78,128,128]{2,1,0:T(8,128)(2,1)} %copy-done, s32[78,128]{1,0:T(8,128)} %valid_ref.1), custom_call_target="tpu_custom_call" | custom-call | tf_op jit(solution)/shard_map/pallas_call | solution.py:212
  104.6 0.5 collective-permute-start.6
  105.1 5.3 %collective-permute-done.6 = f32[264,128]{1,0:T(8,128)S(1)} collective-permute-done((f32[264,128]{1,0:T(8,128)}, f32[264,128]{1,0:T(8,128)S(1)}, u32[]{:S(2)}, u32[]{:S(2)}) %collective-permute-start.6) | collective-permute-done | bytes 135200 | tf_op jit(solution)/shard_map/ppermute | solution.py:250
  110.4 0.9 add.6
  111.4 1.6 %collective-permute-start.7 = (f32[264,128]{1,0:T(8,128)S(1)}, f32[264,128]{1,0:T(8,128)S(1)}, u32[]{:S(2)}, u32[]{:S(2)}) collective-permute-start(f32[264,128]{1,0:T(8,128)S(1)} %add.6), channel_id=1, source_target_pairs={{0,4},{4,0},{8,12},{12,8},{1,5},{5,1},{9,13},{13,9},{2,6},{6,2},{1... | collective-permute-start | bytes 405512 | tf_op jit(solution)/shard_map/ppermute | solution.py:250
  113.0 3.4 %collective-permute-done.7 = f32[264,128]{1,0:T(8,128)S(1)} collective-permute-done((f32[264,128]{1,0:T(8,128)S(1)}, f32[264,128]{1,0:T(8,128)S(1)}, u32[]{:S(2)}, u32[]{:S(2)}) %collective-permute-start.7) | collective-permute-done | bytes 135200 | tf_op jit(solution)/shard_map/ppermute | solution.py:250
  116.5 1.0 collective-permute-start.8
  117.5 6.5 %collective-permute-done.8.theirs_ref = f32[264,128]{1,0:T(8,128)S(1)} collective-permute-done((f32[264,128]{1,0:T(8,128)S(1)}, f32[264,128]{1,0:T(8,128)S(1)}, u32[]{:S(2)}, u32[]{:S(2)}) %collective-permute-start.8) | collective-permute-done | bytes 135200 | tf_op jit(solution)/shard_map/ppermute | solution.py:250
  124.0 0.6 copy-done.2
  124.6 1.8 %shard_map.61 = (f32[1,128]{1,0:T(1,128)}, f32[256,128]{1,0:T(8,128)}) custom-call(f32[264,128]{1,0:T(8,128)} %copy-done.1, f32[264,128]{1,0:T(8,128)} %copy-done.2), custom_call_target="tpu_custom_call" | custom-call | tf_op jit(solution)/shard_map/pallas_call | solution.py:238
  (18 shorter events, 0.1 us)
Async XLA Ops:
  6.7 12.3 %collective-permute-start.2 = (bf16[12,128,128]{2,1,0:T(8,128)(2,1)}, bf16[12,128,128]{2,1,0:T(8,128)(2,1)S(1)}, u32[]{:S(2)}, u32[]{:S(2)}) collective-permute-start(bf16[12,128,128]{2,1,0:T(8,128)(2,1)} %get-tuple-element.10), channel_id=1, source_target_pairs={{0,2},{2,0},{1,3},{3,1},{4,6},{6,4},{5,7},{7,5},{8,10},{10,8},{9,1... | collective-permute-start | bytes 1179656 | tf_op jit(solution)/shard_map/ppermute | solution.py:250
  10.9 32.4 %collective-permute-start.1 = (bf16[17,128,128]{2,1,0:T(8,128)(2,1)S(1)}, bf16[17,128,128]{2,1,0:T(8,128)(2,1)S(1)}, u32[]{:S(2)}, u32[]{:S(2)}) collective-permute-start(bf16[17,128,128]{2,1,0:T(8,128)(2,1)S(1)} %get-tuple-element.13), channel_id=1, source_target_pairs={{4,0},{8,4},{12,8},{0,12},{5,1},{9,5},{13,9},{1,13},{6,2},{10,6},{... | collective-permute-start | bytes 1671176 | tf_op jit(solution)/shard_map/ppermute | solution.py:260
  14.6 28.7 %collective-permute-start = (bf16[17,128,128]{2,1,0:T(8,128)(2,1)S(1)}, bf16[17,128,128]{2,1,0:T(8,128)(2,1)S(1)}, u32[]{:S(2)}, u32[]{:S(2)}) collective-permute-start(bf16[17,128,128]{2,1,0:T(8,128)(2,1)S(1)} %get-tuple-element.14), channel_id=1, source_target_pairs={{0,4},{4,8},{8,12},{12,0},{1,5},{5,9},{9,13},{13,1},{2,6},{6,10},{... | collective-permute-start | bytes 1671176 | tf_op jit(solution)/shard_map/ppermute | solution.py:259
  19.0 24.4 %copy-start.3 = (bf16[12,128,128]{2,1,0:T(8,128)(2,1)}, bf16[12,128,128]{2,1,0:T(8,128)(2,1)S(1)}, u32[]{:S(2)}) copy-start(bf16[12,128,128]{2,1,0:T(8,128)(2,1)S(1)} %collective-permute-done.2.refs_0_) | copy-start | bytes 1179652
  19.0 22.4 %collective-permute-start.4 = (bf16[3,128,128]{2,1,0:T(8,128)(2,1)S(1)}, bf16[3,128,128]{2,1,0:T(8,128)(2,1)S(1)}, u32[]{:S(2)}, u32[]{:S(2)}) collective-permute-start(bf16[3,128,128]{2,1,0:T(8,128)(2,1)S(1)} %get-tuple-element.15), channel_id=1, source_target_pairs={{4,0},{8,4},{12,8},{0,12},{5,1},{9,5},{13,9},{1,13},{6,2},{10,6},{... | collective-permute-start | bytes 294920 | tf_op jit(solution)/shard_map/ppermute | solution.py:271
  22.9 20.4 %collective-permute-start.3 = (bf16[3,128,128]{2,1,0:T(8,128)(2,1)S(1)}, bf16[3,128,128]{2,1,0:T(8,128)(2,1)S(1)}, u32[]{:S(2)}, u32[]{:S(2)}) collective-permute-start(bf16[3,128,128]{2,1,0:T(8,128)(2,1)S(1)} %get-tuple-element.16), channel_id=1, source_target_pairs={{0,4},{4,8},{8,12},{12,0},{1,5},{5,9},{9,13},{13,1},{2,6},{6,10},{... | collective-permute-start | bytes 294920 | tf_op jit(solution)/shard_map/ppermute | solution.py:271
  41.3 2.0 %copy-start.6 = (bf16[3,128,128]{2,1,0:T(8,128)(2,1)}, bf16[3,128,128]{2,1,0:T(8,128)(2,1)S(1)}, u32[]{:S(2)}) copy-start(bf16[3,128,128]{2,1,0:T(8,128)(2,1)S(1)} %collective-permute-done.4.refs_2_) | copy-start | bytes 294916
  43.3 0.6 copy-start.7
  43.3 0.8 copy-start.4
  43.3 1.0 copy-start.5
  79.1 5.0 %collective-permute-start.5 = (bf16[78,128,128]{2,1,0:T(8,128)(2,1)}, bf16[78,128,128]{2,1,0:T(8,128)(2,1)S(1)}, u32[]{:S(2)}, u32[]{:S(2)}) collective-permute-start(bf16[78,128,128]{2,1,0:T(8,128)(2,1)} %shard_map.59.own_ref), channel_id=1, source_target_pairs={{0,1},{1,0},{2,3},{3,2},{4,5},{5,4},{6,7},{7,6},{8,9},{9,8},{10,11... | collective-permute-start | bytes 7667720 | tf_op jit(solution)/shard_map/ppermute | solution.py:250
  84.1 1.5 %copy-start = (bf16[78,128,128]{2,1,0:T(8,128)(2,1)}, bf16[78,128,128]{2,1,0:T(8,128)(2,1)S(1)}, u32[]{:S(2)}) copy-start(bf16[78,128,128]{2,1,0:T(8,128)(2,1)S(1)} %collective-permute-done.5.other_ref) | copy-start | bytes 7667716
  104.6 5.8 %collective-permute-start.6 = (f32[264,128]{1,0:T(8,128)}, f32[264,128]{1,0:T(8,128)S(1)}, u32[]{:S(2)}, u32[]{:S(2)}) collective-permute-start(f32[264,128]{1,0:T(8,128)} %shard_map.60), channel_id=1, source_target_pairs={{0,2},{2,0},{1,3},{3,1},{4,6},{6,4},{5,7},{7,5},{8,10},{10,8},{9,1... | collective-permute-start | bytes 405512 | tf_op jit(solution)/shard_map/ppermute | solution.py:250
  111.4 5.1 %collective-permute-start.7 = (f32[264,128]{1,0:T(8,128)S(1)}, f32[264,128]{1,0:T(8,128)S(1)}, u32[]{:S(2)}, u32[]{:S(2)}) collective-permute-start(f32[264,128]{1,0:T(8,128)S(1)} %add.6), channel_id=1, source_target_pairs={{0,4},{4,0},{8,12},{12,8},{1,5},{5,1},{9,13},{13,9},{2,6},{6,2},{1... | collective-permute-start | bytes 405512 | tf_op jit(solution)/shard_map/ppermute | solution.py:250
  116.5 7.5 %copy-start.1 = (f32[264,128]{1,0:T(8,128)}, f32[264,128]{1,0:T(8,128)S(1)}, u32[]{:S(2)}) copy-start(f32[264,128]{1,0:T(8,128)S(1)} %add.7.mine_ref) | copy-start | bytes 405508
  116.5 7.5 %collective-permute-start.8 = (f32[264,128]{1,0:T(8,128)S(1)}, f32[264,128]{1,0:T(8,128)S(1)}, u32[]{:S(2)}, u32[]{:S(2)}) collective-permute-start(f32[264,128]{1,0:T(8,128)S(1)} %add.7.mine_ref), channel_id=1, source_target_pairs={{0,8},{4,12},{8,0},{12,4},{1,9},{5,13},{9,1},{13,5},{2,10},{6,14},... | collective-permute-start | bytes 405512 | tf_op jit(solution)/shard_map/ppermute | solution.py:250
  124.0 0.7 copy-start.2

commit v2 on v1

v2 whole, which is shorter than its diff:
```python
import functools

import jax
import jax.numpy as jnp
from jax import lax
from jax.experimental import pallas as pl
from jax.experimental.pallas import tpu as pltpu
from jax.sharding import PartitionSpec as P

RMAX = 17
LANES = 128
SLOTS = LANES // RMAX
EDGE = -(-RMAX // SLOTS)
PAD = 8
BATCH = 16
CHUNKS = 1
VMEM_LIMIT = 60 * 1024 * 1024
BF16, F32 = jnp.bfloat16, jnp.float32
VMEM = pl.BlockSpec(memory_space=pltpu.VMEM)
SMEM = pl.BlockSpec(memory_space=pltpu.SMEM)
PARAMS = pltpu.CompilerParams(vmem_limit_bytes=VMEM_LIMIT)


def row_groups(rows):
    head = [(g * SLOTS, SLOTS) for g in range(EDGE)]
    tail = [(rows - (EDGE - g) * SLOTS, SLOTS) for g in range(EDGE)]
    middle, start, stop = [], EDGE * SLOTS, rows - EDGE * SLOTS
    while start < stop:
        count = min(SLOTS, stop - start)
        middle.append((start, count))
        start += count
    return head + middle + tail


def taps_at(radius, offsets, total):
    spread = 0.5 * radius
    inside = jnp.abs(offsets) <= radius
    raw = jnp.where(inside, jnp.exp(-(offsets * offsets) / (2.0 * spread * spread)), 0.0)
    return raw if total is None else raw / total


def tables_kernel(sides, dec_ref, ra_ref):
    cols = dec_ref.shape[2]
    dec = lax.axis_index("dec")
    line = lax.broadcasted_iota(jnp.int32, (8, LANES), 1) - RMAX
    z = lax.broadcasted_iota(jnp.int32, dec_ref.shape[1:], 0)
    y = lax.broadcasted_iota(jnp.int32, dec_ref.shape[1:], 1)
    before, after = z - cols - RMAX, z
    if sides == 1:
        column = jnp.where(z < cols, z, jnp.where(dec == 0, after, before))
    else:
        column = jnp.where(z < cols, z, jnp.where(z < cols + RMAX, before, after - RMAX))
    used = z < cols + sides * RMAX
    dec_offset = jnp.where(used, column - y, 2 * LANES).astype(F32)
    out = lax.broadcasted_iota(jnp.int32, ra_ref.shape[1:], 0)
    source = lax.broadcasted_iota(jnp.int32, ra_ref.shape[1:], 1)
    ra_offset = (source - out - RMAX).astype(F32)

    def one_radius(index, carry):
        radius = index.astype(F32)
        total = jnp.sum(taps_at(radius, line.astype(F32), None)) / 8.0
        dec_ref[index] = taps_at(radius, dec_offset, total).astype(BF16)
        ra_ref[index] = taps_at(radius, ra_offset, total).astype(BF16)
        return carry

    lax.fori_loop(1, RMAX + 1, one_radius, 0)


def tables(rows, cols, sides):
    out_rows = -(-rows // 16) * 16
    return pl.pallas_call(
        functools.partial(tables_kernel, sides),
        out_shape=[
            jax.ShapeDtypeStruct((RMAX + 1, cols + LANES, cols), BF16),
            jax.ShapeDtypeStruct((RMAX + 1, out_rows, rows + 2 * RMAX), BF16),
        ],
        out_specs=[VMEM, VMEM],
        compiler_params=PARAMS,
        cost_estimate=pl.CostEstimate(flops=10**7, bytes_accessed=2 * 10**6, transcendentals=10**6),
    )()


def pack_kernel(sides, x_ref, *edge_refs):
    rows, chans, cols = x_ref.shape
    dec = lax.axis_index("dec")
    lane = lax.broadcasted_iota(jnp.int32, (chans, LANES), 1)
    for side, edge_ref in enumerate(edge_refs):
        if sides == 1:
            first = jnp.where(dec == 0, cols - RMAX, 0)
        else:
            first = cols - RMAX if side == 0 else 0
        for g, (start, count) in enumerate(row_groups(rows)):
            for j in range(count):
                shift = lax.rem(RMAX * j - first + 2 * LANES, LANES)
                piece = pltpu.roll(x_ref[start + j].astype(F32), shift, 1)
                packed = piece if j == 0 else jnp.where(lane < RMAX * j, packed, piece)
            edge_ref[g] = packed.astype(BF16)


def pack(x, sides):
    rows, chans, _ = x.shape
    shape = jax.ShapeDtypeStruct((len(row_groups(rows)), chans, LANES), BF16)
    return pl.pallas_call(
        functools.partial(pack_kernel, sides),
        out_shape=[shape] * sides,
        in_specs=[VMEM],
        out_specs=[VMEM] * sides,
        compiler_params=PARAMS,
        cost_estimate=pl.CostEstimate(flops=10**6, bytes_accessed=3 * 10**6, transcendentals=0),
    )(x)


def smooth_kernel(sides, first, rad_ref, x_ref, before_ref, after_ref, dec_ref, ra_ref, *refs):
    edge_refs, (out_ref, own, halo, result) = refs[:3 * sides], refs[3 * sides:]
    rows, chans, _ = x_ref.shape
    frame = rows + 2 * RMAX
    pitch = chans + PAD

    def copy_rows(ref, base, count):
        def body(i, carry):
            own[pl.ds((base + i) * pitch, chans), :] = ref[i].astype(F32)
            return carry

        lax.fori_loop(0, count, body, 0)

    copy_rows(before_ref, 0, RMAX)
    copy_rows(x_ref, RMAX, rows)
    copy_rows(after_ref, RMAX + rows, RMAX)

    lane = lax.broadcasted_iota(jnp.int32, (chans, LANES), 1)
    groups = row_groups(rows)

    def unpack(row, part, g, j):
        for side in range(sides):
            tile = edge_refs[3 * side + part][g].astype(F32)
            shift = (RMAX * side - RMAX * j) % LANES
            tile = tile if shift == 0 else pltpu.roll(tile, shift, 1)
            value = tile if side == 0 else jnp.where(lane < RMAX, value, tile)
        halo[pl.ds(row * pitch, chans), :] = value

    for g, (start, count) in enumerate(groups):
        for j in range(count):
            unpack(RMAX + start + j, 0, g, j)
    for g, (start, count) in enumerate(groups[-EDGE:]):
        for j in range(count):
            if start + j >= rows - RMAX:
                unpack(start + j - (rows - RMAX), 1, g, j)
    for g, (start, count) in enumerate(groups[:EDGE]):
        for j in range(count):
            if start + j < RMAX:
                unpack(RMAX + rows + start + j, 2, g, j)

    def some_channels(i, carry):
        chosen = [i * BATCH + j for j in range(BATCH)]
        radii = [rad_ref[first + c] for c in chosen]
        partials = []
        for c, radius in zip(chosen, radii):
            picked = pl.ds(c, frame, stride=pitch)
            lhs = jnp.concatenate([own[picked, :].astype(BF16), halo[picked, :].astype(BF16)], axis=1)
            partials.append(jnp.dot(lhs, dec_ref[radius], preferred_element_type=F32).astype(BF16))
        for c, radius, partial in zip(chosen, radii, partials):
            smoothed = jnp.dot(ra_ref[radius], partial, preferred_element_type=F32)
            result[pl.ds(c, rows, stride=pitch), :] = smoothed[:rows]
        return carry

    lax.fori_loop(0, chans // BATCH, some_channels, 0)

    def store(i, carry):
        out_ref[i] = result[pl.ds(i * pitch, chans), :].astype(BF16)
        return carry

    lax.fori_loop(0, rows, store, 0)


def smooth(radii, x, chunk, before, after, dec_table, ra_table, edges):
    rows, _, cols = x.shape
    chans = before.shape[1]
    pitch, frame = chans + PAD, rows + 2 * RMAX
    operands = [x, before, after, dec_table, ra_table] + [part for side in edges for part in side]

    def ranged(array):
        if array.shape[1] == chans or array is dec_table or array is ra_table:
            return pl.BlockSpec(array.shape, lambda i: (0, 0, 0))
        return pl.BlockSpec((array.shape[0], chans, array.shape[2]), lambda i: (0, chunk, 0))

    return pl.pallas_call(
        functools.partial(smooth_kernel, len(edges), chunk * chans),
        out_shape=jax.ShapeDtypeStruct((rows, chans, cols), BF16),
        grid=(1,),
        in_specs=[SMEM] + [ranged(a) for a in operands],
        out_specs=pl.BlockSpec((rows, chans, cols), lambda i: (0, 0, 0)),
        scratch_shapes=[
            pltpu.VMEM((frame * pitch, cols), F32),
            pltpu.VMEM((frame * pitch, LANES), F32),
            pltpu.VMEM((rows * pitch, cols), F32),
        ],
        compiler_params=PARAMS,
        cost_estimate=pl.CostEstimate(flops=4 * 10**9 // CHUNKS, bytes_accessed=10**7 // CHUNKS, transcendentals=0),
    )(radii, *operands)


SUM_ROWS = 8


def gram_kernel(parts, *refs):
    own_refs, other_refs, (valid_ref, out_ref, smoothed_ref, total, sems) = refs[:parts], refs[parts:2 * parts], refs[2 * parts:]
    rows, part, cols = own_refs[0].shape
    chans = parts * part
    band = lax.axis_index("band")
    copies = [
        pltpu.make_async_copy(ref, smoothed_ref.at[:, pl.ds(i * part, part), :], sems.at[i])
        for i, ref in enumerate(own_refs)
    ]
    for copy in copies:
        copy.start()
    depth = max(d for d in range(1, 27) if rows % d == 0)

    def nt(a, b):
        return lax.dot_general(a, b, (((1,), (1,)), ((), ())), preferred_element_type=F32)

    def body(i, carry):
        picked = [i * depth + j for j in range(depth)]
        weights = [valid_ref[pl.ds(r, 1), :].astype(BF16) for r in picked]

        def wide(refs):
            return jnp.concatenate([jnp.concatenate([ref[r] for ref in refs], 0) for r in picked], 1)

        own, other = wide(own_refs), wide(other_refs)
        line = jnp.concatenate(weights, 1)
        both = jnp.concatenate([own, other], 0)
        total[:2 * chans, :] += nt(both, own * line)
        sums = nt(jnp.broadcast_to(line, (16, line.shape[1])), both)[:SUM_ROWS]
        total[2 * chans:2 * chans + SUM_ROWS, :] += sums[:, :chans]
        total[2 * chans + SUM_ROWS:, :] += sums[:, chans:]
        return carry

    total[...] = jnp.zeros_like(total)
    lax.fori_loop(0, rows // depth, body, 0)
    out_ref[pl.ds(pl.multiple_of(band * chans, chans), chans), :] = total[:chans, :]
    out_ref[pl.ds(pl.multiple_of((1 - band) * chans, chans), chans), :] = total[chans:2 * chans, :]
    row = lax.broadcasted_iota(jnp.int32, (SUM_ROWS, chans), 0)
    own_sum, other_sum = total[2 * chans:2 * chans + SUM_ROWS, :], total[2 * chans + SUM_ROWS:, :]
    sums = jnp.where(row == band, own_sum, other_sum)
    out_ref[2 * chans:, :] = jnp.where(row == 2, jnp.sum(valid_ref[...].astype(F32)), sums)
    for copy in copies:
        copy.wait()


def gram(own, other, valid):
    rows, part, cols = own[0].shape
    parts = len(own)
    chans = parts * part
    return pl.pallas_call(
        functools.partial(gram_kernel, parts),
        out_shape=[
            jax.ShapeDtypeStruct((2 * chans + SUM_ROWS, chans), F32),
            jax.ShapeDtypeStruct((rows, chans, cols), BF16),
        ],
        in_specs=[VMEM] * (2 * parts + 1),
        out_specs=[VMEM, pl.BlockSpec(memory_space=pl.ANY)],
        scratch_shapes=[pltpu.VMEM((2 * chans + 2 * SUM_ROWS, chans), F32), pltpu.SemaphoreType.DMA((parts,))],
        compiler_params=PARAMS,
    )(*own, *other, valid)


def finish_kernel(mine_ref, theirs_ref, mean_ref, cov_ref):
    chans = mine_ref.shape[1]
    band = lax.axis_index("band")
    block = mine_ref[:2 * chans, :] + theirs_ref[:2 * chans, :]
    tail = mine_ref[2 * chans:, :] + theirs_ref[2 * chans:, :]
    count = tail[2:3, 0:1]
    means = tail / count
    own = jnp.where(band == 0, means[0:1, :], means[1:2, :])
    mean_ref[...] = own
    for b in range(2):
        column = jnp.transpose(jnp.broadcast_to(means[b:b + 1, :], (chans, chans)))
        part = block[b * chans:(b + 1) * chans]
        cov_ref[b * chans:(b + 1) * chans, :] = (part - count * column * own) / (count - 1.0)


def finish(mine, theirs):
    chans = mine.shape[1]
    mean, covariance = pl.pallas_call(
        finish_kernel,
        out_shape=[jax.ShapeDtypeStruct((1, chans), F32), jax.ShapeDtypeStruct((2 * chans, chans), F32)],
        in_specs=[VMEM] * 2,
        out_specs=[VMEM] * 2,
        compiler_params=PARAMS,
    )(mine, theirs)
    return mean.reshape(chans), covariance


def swap(array, axis, step):
    size = lax.axis_size(axis)
    return lax.ppermute(array, axis, [(i, i ^ step) for i in range(size)])


def diagonal(array, ra_step, dec_pairs):
    ra_size, dec_size = lax.axis_size("ra"), lax.axis_size("dec")
    pairs = [
        (i * dec_size + a, (i + ra_step) % ra_size * dec_size + b) for i in range(ra_size) for a, b in dec_pairs
    ]
    return lax.ppermute(array, ("ra", "dec"), pairs)


def per_device(sky_maps, radii, valid):
    x = jnp.transpose(sky_maps, (1, 0, 2))
    rows, chans, cols = x.shape
    ra_size, dec_size = lax.axis_size("ra"), lax.axis_size("dec")
    up = [(i, (i + 1) % ra_size) for i in range(ra_size)]
    down = [(j, i) for i, j in up]
    part = chans // CHUNKS
    ranges = [slice(i * part, (i + 1) * part) for i in range(CHUNKS)]
    frames = [
        (lax.ppermute(x[rows - RMAX:, r], "ra", up), lax.ppermute(x[:RMAX, r], "ra", down)) for r in ranges
    ]
    right = [(i, i + 1) for i in range(dec_size - 1)]
    left = [(j, i) for i, j in right]
    sides = [right + left] if dec_size == 2 else [right, left]
    edges = [
        (lax.ppermute(p, "dec", pairs), diagonal(p[-EDGE:], 1, pairs), diagonal(p[:EDGE], -1, pairs))
        for p, pairs in zip(pack(x, len(sides)), sides)
    ]
    dec_table, ra_table = tables(rows, cols, len(sides))

    own = [smooth(radii, x, i, *frame, dec_table, ra_table, edges) for i, frame in enumerate(frames)]
    other = [swap(a, "band", 1) for a in own]
    total, smoothed = gram(own, other, valid)
    steps = [("dec", 1 << b) for b in range(dec_size.bit_length() - 1)]
    steps += [("ra", 1 << b) for b in range(ra_size.bit_length() - 1)]
    for axis, step in steps[:-1]:
        total = total + swap(total, axis, step)
    mean, covariance = finish(total, swap(total, *steps[-1]))
    return (jnp.transpose(smoothed, (1, 0, 2)), mean, covariance)


def solution(mesh):
    return jax.shard_map(
        per_device,
        mesh=mesh,
        in_specs=(
            P(("groups", "band"), "ra", "dec"),
            P(("groups", "band")),
            P(("groups", "ra"), "dec"),
        ),
        out_specs=(P(("groups", "band"), "ra", "dec"), P(("groups", "band")), P("groups", "band")),
        check_vma=False,
    )
```

time: 127 us -> 84.8 us (0.67)
  Pallas kernels: 61.6 us -> 26.8 us
  waiting for transfers between devices: 45 us -> 36.8 us
    pallas_call x3 -> x4, Pallas kernels: 59.8 us -> 25 us  [the longest x1 11.8 us: smooth(): pl.pallas_call(functools.partial(smooth_kernel, len(edges), chunk * chans...]
    ppermute x5 -> x4, waiting for transfers between devices: 24.6 us -> 20.2 us  [swap(): return lax.ppermute(array, axis, [(i, i ^ step) for i in range(size)])]
    ppermute x4 -> x5, waiting for transfers between devices: 20.4 us -> 16.6 us  [the longest x2 16.6 us: diagonal(): return lax.ppermute(array, ('ra', 'dec'), pairs)]
    ppermute x4 -> x5, starting transfers between devices: 7.57 us -> 10.4 us  [the longest x1 5.1 us: per_device(): lax.ppermute(x[:RMAX, r], 'ra', down)]
    ppermute x5 -> x4, starting transfers between devices: 6.14 us -> 3.29 us  [swap(): return lax.ppermute(array, axis, [(i, i ^ step) for i in range(size)])]
  transfers between devices with their start and end apart: 9 -> 9, of which waited for: 7 -> 6; matrix products, arithmetic and copies ran while one was open for 1% -> 1% of each run, Pallas kernels for 0% -> 8%
where the time goes in v2:
time: 84.8 us; the launch traced here: 84.6 us
  waiting for transfers between devices  36.8 us (43%)
  Pallas kernels  26.8 us (32%)
  starting transfers between devices  13.7 us (16%)
  local copies, waits for them, and re-layouts  5.57 us (7%)
  other arithmetic  0.95 us (1%)
    ppermute x4, waiting for transfers between devices, swap(): return lax.ppermute(array, axis, [(i, i ^ step) for i in range(size)])  20.2 us
    ppermute x2, waiting for transfers between devices, diagonal(): return lax.ppermute(array, ('ra', 'dec'), pairs)  16.6 us
    pallas_call x1, Pallas kernels, smooth(): pl.pallas_call(functools.partial(smooth_kernel, len(edges), chunk * chans...  11.8 us
    pallas_call x1, Pallas kernels, gram(): pl.pallas_call(functools.partial(gram_kernel, parts), out_shape=[jax.Shap...  6.22 us
    ppermute x1, starting transfers between devices, per_device(): lax.ppermute(x[:RMAX, r], 'ra', down)  5.1 us
    ppermute x2, starting transfers between devices, diagonal(): return lax.ppermute(array, ('ra', 'dec'), pairs)  3.85 us
    pallas_call x1, Pallas kernels, tables(): pl.pallas_call(functools.partial(tables_kernel, sides), out_shape=[jax.Sh...  3.74 us
    ppermute x4, starting transfers between devices, swap(): return lax.ppermute(array, axis, [(i, i ^ step) for i in range(size)])  3.29 us
  transfers between devices with their start and end apart: 9, of which 6 were waited for; matrix products, arithmetic and copies ran while one was open for 1% of the time, Pallas kernels for 8%

profile of v2, /device:TPU:0, one launch (start us, length us, event | category | flops | bytes accessed | tf_op | source)
XLA Modules:
  0.0 84.6 jit_solution(12160077309899417539)
XLA Ops:
  0.6 1.3 %fusion = (bf16[17,128,128]{2,1,0:T(8,128)(2,1)S(1)}, bf16[17,128,128]{2,1,0:T(8,128)(2,1)S(1)}) fusion(bf16[78,128,128]{2,1,0:T(8,128)(2,1)} %bitcast.3), kind=kLoop, calls=%fused_computation | loop fusion | bytes 2228224 | tf_op jit(solution)/shard_map/slice | solution.py:315
  2.0 5.1 %collective-permute-start.1 = (bf16[17,128,128]{2,1,0:T(8,128)(2,1)S(1)}, bf16[17,128,128]{2,1,0:T(8,128)(2,1)S(1)}, u32[]{:S(2)}, u32[]{:S(2)}) collective-permute-start(bf16[17,128,128]{2,1,0:T(8,128)(2,1)S(1)} %get-tuple-element.15), channel_id=1, source_target_pairs={{4,0},{8,4},{12,8},{0,12},{5,1},{9,5},{13,9},{1,13},{6,2},{10,6},{... | collective-permute-start | bytes 1671176 | tf_op jit(solution)/shard_map/ppermute | solution.py:315
  7.1 3.2 %shard_map.59 = bf16[12,128,128]{2,1,0:T(8,128)(2,1)} custom-call(bf16[78,128,128]{2,1,0:T(8,128)(2,1)} %bitcast.4), custom_call_target="tpu_custom_call" | custom-call | flops 1000000 | bytes 3000000 | tf_op jit(solution)/shard_map/pallas_call | solution.py:103
  10.3 1.5 %collective-permute-start.2 = (bf16[12,128,128]{2,1,0:T(8,128)(2,1)}, bf16[12,128,128]{2,1,0:T(8,128)(2,1)S(1)}, u32[]{:S(2)}, u32[]{:S(2)}) collective-permute-start(bf16[12,128,128]{2,1,0:T(8,128)(2,1)} %shard_map.59), channel_id=1, source_target_pairs={{0,2},{2,0},{1,3},{3,1},{4,6},{6,4},{5,7},{7,5},{8,10},{10,8},{9,1... | collective-permute-start | bytes 1179656 | tf_op jit(solution)/shard_map/ppermute | solution.py:321
  11.8 1.0 %fusion.1 = (bf16[3,128,128]{2,1,0:T(8,128)(2,1)S(1)}, bf16[3,128,128]{2,1,0:T(8,128)(2,1)S(1)}) fusion(bf16[12,128,128]{2,1,0:T(8,128)(2,1)} %shard_map.59), kind=kLoop, calls=%fused_computation.1 | loop fusion | bytes 393216 | tf_op jit(solution)/shard_map/slice | solution.py:321
  12.8 3.8 %collective-permute-start.4 = (bf16[3,128,128]{2,1,0:T(8,128)(2,1)S(1)}, bf16[3,128,128]{2,1,0:T(8,128)(2,1)S(1)}, u32[]{:S(2)}, u32[]{:S(2)}) collective-permute-start(bf16[3,128,128]{2,1,0:T(8,128)(2,1)S(1)} %get-tuple-element.17), channel_id=1, source_target_pairs={{0,14},{2,12},{4,2},{6,0},{8,6},{10,4},{12,10},{14,8},{1,15},{3,13... | collective-permute-start | bytes 294920 | tf_op jit(solution)/shard_map/ppermute | solution.py:303
  16.6 3.7 %shard_map.58 = (bf16[18,256,128]{2,1,0:T(8,128)(2,1)}, bf16[18,80,112]{2,1,0:T(8,128)(2,1)}) custom-call(), custom_call_target="tpu_custom_call" | custom-call | flops 10000000 | bytes 2000000 | tf_op jit(solution)/shard_map/pallas_call | solution.py:71
  20.4 13.8 %collective-permute-done.4.refs_2_ = bf16[3,128,128]{2,1,0:T(8,128)(2,1)S(1)} collective-permute-done((bf16[3,128,128]{2,1,0:T(8,128)(2,1)S(1)}, bf16[3,128,128]{2,1,0:T(8,128)(2,1)S(1)}, u32[]{:S(2)}, u32[]{:S(2)}) %collective-permute-start.4) | collective-permute-done | bytes 98336 | tf_op jit(solution)/shard_map/ppermute | solution.py:303
  34.1 2.8 %collective-permute-done.3.refs_1_ = bf16[3,128,128]{2,1,0:T(8,128)(2,1)S(1)} collective-permute-done((bf16[3,128,128]{2,1,0:T(8,128)(2,1)S(1)}, bf16[3,128,128]{2,1,0:T(8,128)(2,1)S(1)}, u32[]{:S(2)}, u32[]{:S(2)}) %collective-permute-start.3) | collective-permute-done | bytes 98336 | tf_op jit(solution)/shard_map/ppermute | solution.py:303
  37.0 0.6 copy-done.7
  37.9 0.2 copy-done.4
  38.1 11.8 %shard_map.60.refs_0_ = bf16[78,128,128]{2,1,0:T(8,128)(2,1)} custom-call(s32[128]{0:T(128)} %rad_ref.1, bf16[78,128,128]{2,1,0:T(8,128)(2,1)} %bitcast.5, bf16[17,128,128]{2,1,0:T(8,128)(2,1)} %copy-done.4, bf16[17,128,128]{2,1,0:T(8,128)(2,1)} %copy-done.3, bf16[18,256,128]{2,1,0:T(8,128)(2,1)} %get-tuple-element.9.dec_ref, ...), custom_call_target="tpu_custom_call" | custom-call | flops 4000000000 | bytes 10000000 | tf_op jit(solution)/shard_map/pallas_call | solution.py:186
  50.0 5.0 %collective-permute-done.5.refs_1_ = bf16[78,128,128]{2,1,0:T(8,128)(2,1)S(1)} collective-permute-done((bf16[78,128,128]{2,1,0:T(8,128)(2,1)}, bf16[78,128,128]{2,1,0:T(8,128)(2,1)S(1)}, u32[]{:S(2)}, u32[]{:S(2)}) %collective-permute-start.5) | collective-permute-done | bytes 2555936 | tf_op jit(solution)/shard_map/ppermute | solution.py:295
  55.0 1.5 %copy-done = bf16[78,128,128]{2,1,0:T(8,128)(2,1)} copy-done((bf16[78,128,128]{2,1,0:T(8,128)(2,1)}, bf16[78,128,128]{2,1,0:T(8,128)(2,1)S(1)}, u32[]{:S(2)}) %copy-start) | copy-done | bytes 2555928
  56.5 6.2 %shard_map.61 = (f32[264,128]{1,0:T(8,128)}, bf16[78,128,128]{2,1,0:T(8,128)(2,1)}) custom-call(bf16[78,128,128]{2,1,0:T(8,128)(2,1)} %shard_map.60.refs_0_, bf16[78,128,128]{2,1,0:T(8,128)(2,1)} %copy-done, s32[78,128]{1,0:T(8,128)} %refs_2_.1), custom_call_target="tpu_custom_call" | custom-call | tf_op jit(solution)/shard_map/pallas_call | solution.py:253
  62.7 0.6 collective-permute-start.6
  63.3 5.3 %collective-permute-done.6 = f32[264,128]{1,0:T(8,128)S(1)} collective-permute-done((f32[264,128]{1,0:T(8,128)}, f32[264,128]{1,0:T(8,128)S(1)}, u32[]{:S(2)}, u32[]{:S(2)}) %collective-permute-start.6) | collective-permute-done | bytes 135200 | tf_op jit(solution)/shard_map/ppermute | solution.py:295
  68.6 0.9 %add.6 = f32[264,128]{1,0:T(8,128)S(1)} add(f32[264,128]{1,0:T(8,128)} %get-tuple-element.12, f32[264,128]{1,0:T(8,128)S(1)} %collective-permute-done.6) | non-fusion elementwise | flops 33792 | bytes 405504 | tf_op jit(solution)/shard_map/add | solution.py:332
  69.5 1.6 %collective-permute-start.7 = (f32[264,128]{1,0:T(8,128)S(1)}, f32[264,128]{1,0:T(8,128)S(1)}, u32[]{:S(2)}, u32[]{:S(2)}) collective-permute-start(f32[264,128]{1,0:T(8,128)S(1)} %add.6), channel_id=1, source_target_pairs={{0,4},{4,0},{8,12},{12,8},{1,5},{5,1},{9,13},{13,9},{2,6},{6,2},{1... | collective-permute-start | bytes 405512 | tf_op jit(solution)/shard_map/ppermute | solution.py:295
  71.2 3.4 %collective-permute-done.7 = f32[264,128]{1,0:T(8,128)S(1)} collective-permute-done((f32[264,128]{1,0:T(8,128)S(1)}, f32[264,128]{1,0:T(8,128)S(1)}, u32[]{:S(2)}, u32[]{:S(2)}) %collective-permute-start.7) | collective-permute-done | bytes 135200 | tf_op jit(solution)/shard_map/ppermute | solution.py:295
  74.6 1.0 %collective-permute-start.8 = (f32[264,128]{1,0:T(8,128)S(1)}, f32[264,128]{1,0:T(8,128)S(1)}, u32[]{:S(2)}, u32[]{:S(2)}) collective-permute-start(f32[264,128]{1,0:T(8,128)S(1)} %add.7.mine_ref), channel_id=1, source_target_pairs={{0,8},{4,12},{8,0},{12,4},{1,9},{5,13},{9,1},{13,5},{2,10},{6,14},... | collective-permute-start | bytes 405512 | tf_op jit(solution)/shard_map/ppermute | solution.py:295
  75.7 6.5 %collective-permute-done.8.theirs_ref = f32[264,128]{1,0:T(8,128)S(1)} collective-permute-done((f32[264,128]{1,0:T(8,128)S(1)}, f32[264,128]{1,0:T(8,128)S(1)}, u32[]{:S(2)}, u32[]{:S(2)}) %collective-permute-start.8) | collective-permute-done | bytes 135200 | tf_op jit(solution)/shard_map/ppermute | solution.py:295
  82.1 0.6 copy-done.2
  82.8 1.8 %shard_map.62 = (f32[1,128]{1,0:T(1,128)}, f32[256,128]{1,0:T(8,128)}) custom-call(f32[264,128]{1,0:T(8,128)} %copy-done.1, f32[264,128]{1,0:T(8,128)} %copy-done.2), custom_call_target="tpu_custom_call" | custom-call | tf_op jit(solution)/shard_map/pallas_call | solution.py:283
  (19 shorter events, 0.4 us)
Async XLA Ops:
  2.0 35.0 %collective-permute-start.1 = (bf16[17,128,128]{2,1,0:T(8,128)(2,1)S(1)}, bf16[17,128,128]{2,1,0:T(8,128)(2,1)S(1)}, u32[]{:S(2)}, u32[]{:S(2)}) collective-permute-start(bf16[17,128,128]{2,1,0:T(8,128)(2,1)S(1)} %get-tuple-element.15), channel_id=1, source_target_pairs={{4,0},{8,4},{12,8},{0,12},{5,1},{9,5},{13,9},{1,13},{6,2},{10,6},{... | collective-permute-start | bytes 1671176 | tf_op jit(solution)/shard_map/ppermute | solution.py:315
  7.1 29.9 %collective-permute-start = (bf16[17,128,128]{2,1,0:T(8,128)(2,1)S(1)}, bf16[17,128,128]{2,1,0:T(8,128)(2,1)S(1)}, u32[]{:S(2)}, u32[]{:S(2)}) collective-permute-start(bf16[17,128,128]{2,1,0:T(8,128)(2,1)S(1)} %get-tuple-element.16), channel_id=1, source_target_pairs={{0,4},{4,8},{8,12},{12,0},{1,5},{5,9},{9,13},{13,1},{2,6},{6,10},{... | collective-permute-start | bytes 1671176 | tf_op jit(solution)/shard_map/ppermute | solution.py:315
  10.3 26.7 %collective-permute-start.2 = (bf16[12,128,128]{2,1,0:T(8,128)(2,1)}, bf16[12,128,128]{2,1,0:T(8,128)(2,1)S(1)}, u32[]{:S(2)}, u32[]{:S(2)}) collective-permute-start(bf16[12,128,128]{2,1,0:T(8,128)(2,1)} %shard_map.59), channel_id=1, source_target_pairs={{0,2},{2,0},{1,3},{3,1},{4,6},{6,4},{5,7},{7,5},{8,10},{10,8},{9,1... | collective-permute-start | bytes 1179656 | tf_op jit(solution)/shard_map/ppermute | solution.py:321
  12.8 21.4 %collective-permute-start.4 = (bf16[3,128,128]{2,1,0:T(8,128)(2,1)S(1)}, bf16[3,128,128]{2,1,0:T(8,128)(2,1)S(1)}, u32[]{:S(2)}, u32[]{:S(2)}) collective-permute-start(bf16[3,128,128]{2,1,0:T(8,128)(2,1)S(1)} %get-tuple-element.17), channel_id=1, source_target_pairs={{0,14},{2,12},{4,2},{6,0},{8,6},{10,4},{12,10},{14,8},{1,15},{3,13... | collective-permute-start | bytes 294920 | tf_op jit(solution)/shard_map/ppermute | solution.py:303
  16.6 20.4 %collective-permute-start.3 = (bf16[3,128,128]{2,1,0:T(8,128)(2,1)S(1)}, bf16[3,128,128]{2,1,0:T(8,128)(2,1)S(1)}, u32[]{:S(2)}, u32[]{:S(2)}) collective-permute-start(bf16[3,128,128]{2,1,0:T(8,128)(2,1)S(1)} %get-tuple-element.18), channel_id=1, source_target_pairs={{0,6},{2,4},{4,10},{6,8},{8,14},{10,12},{12,2},{14,0},{1,7},{3,5},... | collective-permute-start | bytes 294920 | tf_op jit(solution)/shard_map/ppermute | solution.py:303
  34.1 2.9 %copy-start.6 = (bf16[3,128,128]{2,1,0:T(8,128)(2,1)}, bf16[3,128,128]{2,1,0:T(8,128)(2,1)S(1)}, u32[]{:S(2)}) copy-start(bf16[3,128,128]{2,1,0:T(8,128)(2,1)S(1)} %collective-permute-done.4.refs_2_) | copy-start | bytes 294916
  37.0 0.6 copy-start.7
  37.0 0.8 copy-start.5
  37.0 0.9 %copy-start.3 = (bf16[17,128,128]{2,1,0:T(8,128)(2,1)}, bf16[17,128,128]{2,1,0:T(8,128)(2,1)S(1)}, u32[]{:S(2)}) copy-start(bf16[17,128,128]{2,1,0:T(8,128)(2,1)S(1)} %collective-permute-done.1.after_ref) | copy-start | bytes 1671172
  37.0 1.1 %copy-start.4 = (bf16[17,128,128]{2,1,0:T(8,128)(2,1)}, bf16[17,128,128]{2,1,0:T(8,128)(2,1)S(1)}, u32[]{:S(2)}) copy-start(bf16[17,128,128]{2,1,0:T(8,128)(2,1)S(1)} %collective-permute-done.before_ref) | copy-start | bytes 1671172
  50.0 5.0 %collective-permute-start.5 = (bf16[78,128,128]{2,1,0:T(8,128)(2,1)}, bf16[78,128,128]{2,1,0:T(8,128)(2,1)S(1)}, u32[]{:S(2)}, u32[]{:S(2)}) collective-permute-start(bf16[78,128,128]{2,1,0:T(8,128)(2,1)} %shard_map.60.refs_0_), channel_id=1, source_target_pairs={{0,1},{1,0},{2,3},{3,2},{4,5},{5,4},{6,7},{7,6},{8,9},{9,8},{10,11... | collective-permute-start | bytes 7667720 | tf_op jit(solution)/shard_map/ppermute | solution.py:295
  55.0 1.5 %copy-start = (bf16[78,128,128]{2,1,0:T(8,128)(2,1)}, bf16[78,128,128]{2,1,0:T(8,128)(2,1)S(1)}, u32[]{:S(2)}) copy-start(bf16[78,128,128]{2,1,0:T(8,128)(2,1)S(1)} %collective-permute-done.5.refs_1_) | copy-start | bytes 7667716
  62.7 5.9 %collective-permute-start.6 = (f32[264,128]{1,0:T(8,128)}, f32[264,128]{1,0:T(8,128)S(1)}, u32[]{:S(2)}, u32[]{:S(2)}) collective-permute-start(f32[264,128]{1,0:T(8,128)} %get-tuple-element.12), channel_id=1, source_target_pairs={{0,2},{2,0},{1,3},{3,1},{4,6},{6,4},{5,7},{7,5},{8,10},{10,8},{9,1... | collective-permute-start | bytes 405512 | tf_op jit(solution)/shard_map/ppermute | solution.py:295
  69.5 5.1 %collective-permute-start.7 = (f32[264,128]{1,0:T(8,128)S(1)}, f32[264,128]{1,0:T(8,128)S(1)}, u32[]{:S(2)}, u32[]{:S(2)}) collective-permute-start(f32[264,128]{1,0:T(8,128)S(1)} %add.6), channel_id=1, source_target_pairs={{0,4},{4,0},{8,12},{12,8},{1,5},{5,1},{9,13},{13,9},{2,6},{6,2},{1... | collective-permute-start | bytes 405512 | tf_op jit(solution)/shard_map/ppermute | solution.py:295
  74.6 7.5 %copy-start.1 = (f32[264,128]{1,0:T(8,128)}, f32[264,128]{1,0:T(8,128)S(1)}, u32[]{:S(2)}) copy-start(f32[264,128]{1,0:T(8,128)S(1)} %add.7.mine_ref) | copy-start | bytes 405508
  74.6 7.5 %collective-permute-start.8 = (f32[264,128]{1,0:T(8,128)S(1)}, f32[264,128]{1,0:T(8,128)S(1)}, u32[]{:S(2)}, u32[]{:S(2)}) collective-permute-start(f32[264,128]{1,0:T(8,128)S(1)} %add.7.mine_ref), channel_id=1, source_target_pairs={{0,8},{4,12},{8,0},{12,4},{1,9},{5,13},{9,1},{13,5},{2,10},{6,14},... | collective-permute-start | bytes 405512 | tf_op jit(solution)/shard_map/ppermute | solution.py:295
  82.1 0.7 copy-start.2

commit v3 on v2

v3 whole, which is shorter than its diff:
```python
import functools

import jax
import jax.numpy as jnp
from jax import lax
from jax.experimental import pallas as pl
from jax.experimental.pallas import tpu as pltpu
from jax.sharding import PartitionSpec as P

RMAX = 17
LANES = 128
SLOTS = LANES // RMAX
EDGE = -(-RMAX // SLOTS)
PAD = 8
HALO = 24
BATCH = 16
VMEM_LIMIT = 32 * 1024 * 1024
BF16, F32 = jnp.bfloat16, jnp.float32
VMEM = pl.BlockSpec(memory_space=pltpu.VMEM)
SMEM = pl.BlockSpec(memory_space=pltpu.SMEM)
PARAMS = pltpu.CompilerParams(vmem_limit_bytes=VMEM_LIMIT)


def row_groups(rows):
    head = [(g * SLOTS, SLOTS) for g in range(EDGE)]
    tail = [(rows - (EDGE - g) * SLOTS, SLOTS) for g in range(EDGE)]
    middle, start, stop = [], EDGE * SLOTS, rows - EDGE * SLOTS
    while start < stop:
        count = min(SLOTS, stop - start)
        middle.append((start, count))
        start += count
    return head + middle + tail


def tables_kernel(sides, rows, dec_ref, inner_ref, outer_ref, *offset_refs):
    cols = dec_ref.shape[2]
    dec = lax.axis_index("dec")

    def offsets(offset_ref, used, offset):
        offset_ref[...] = jnp.where(used, offset, 2 * LANES).astype(F32)

    def grid(ref):
        return [lax.broadcasted_iota(jnp.int32, ref.shape, d) for d in (0, 1)]

    z, y = grid(offset_refs[0])
    before, after = z - cols - RMAX, z
    if sides == 1:
        column = jnp.where(z < cols, z, jnp.where(dec == 0, after, before))
    else:
        column = jnp.where(z < cols, z, jnp.where(z < cols + RMAX, before, after - RMAX))
    offsets(offset_refs[0], z < cols + sides * RMAX, column - y)
    out, source = grid(offset_refs[1])
    offsets(offset_refs[1], source < rows, source - out - RMAX)
    out, source = grid(offset_refs[2])
    own = outer_ref.shape[2] - 2 * HALO
    head, tail = source - own, source - own - HALO
    row = jnp.where(source < own, source, jnp.where(head < HALO, head - RMAX, tail + rows))
    used = (source < rows) | ((head >= 0) & (head < RMAX)) | ((tail >= 0) & (tail < RMAX))
    offsets(offset_refs[2], used, row - jnp.where(out < HALO, out, out - HALO + rows - RMAX))
    line = (lax.broadcasted_iota(jnp.int32, (8, LANES), 1) - RMAX).astype(F32)

    def one_radius(index, carry):
        radius = jnp.full((8, LANES), index, jnp.int32).astype(F32)
        spread = 0.5 * radius
        scale = -1.0 / (2.0 * spread * spread)
        raw = jnp.where(jnp.abs(line) <= radius, jnp.exp(line * line * scale), 0.0)
        inverse = 1.0 / jnp.sum(raw, axis=1, keepdims=True)
        limit, scale, inverse = radius[:1, :1], scale[:1, :1], inverse[:1]
        for ref, offset_ref in zip((dec_ref, inner_ref, outer_ref), offset_refs):
            offset = offset_ref[...]
            taps = jnp.where(jnp.abs(offset) <= limit, jnp.exp(offset * offset * scale) * inverse, 0.0)
            ref[index] = taps.astype(BF16)
        return carry

    lax.fori_loop(1, RMAX + 1, one_radius, 0)


def tables(rows, cols, sides):
    own = -(-rows // 16) * 16
    shapes = [(cols + LANES, cols), (-(-(rows - 2 * RMAX) // 16) * 16, own), (2 * HALO, own + 2 * HALO)]
    return pl.pallas_call(
        functools.partial(tables_kernel, sides, rows),
        out_shape=[pltpu.VMEM((RMAX + 1, *shape), BF16) for shape in shapes],
        out_specs=[VMEM] * 3,
        scratch_shapes=[pltpu.VMEM(shape, F32) for shape in shapes],
        compiler_params=PARAMS,
        cost_estimate=pl.CostEstimate(flops=10**5, bytes_accessed=10**5, transcendentals=0),
    )()


def edges_kernel(sides, rad_ref, source_ref, x_ref, *refs):
    (up_ref, up_rest_ref, down_ref, down_rest_ref), refs = refs[:4], refs[4:]
    edge_refs, (low_wide, high_wide, low_packed, high_packed, sems) = refs[:sides], refs[sides:]
    rows, chans, cols = x_ref.shape
    pitch = chans + PAD
    cap, full = up_ref.shape[0], RMAX * chans
    spans = ((0, RMAX), (rows - RMAX, RMAX), (RMAX, rows - 2 * RMAX))
    copies = [
        pltpu.make_async_copy(source_ref.at[pl.ds(start, n)], x_ref.at[pl.ds(start, n)], sems.at[i])
        for i, (start, n) in enumerate(spans)
    ]
    for copy in copies:
        copy.start()
    low_packed[...] = jnp.zeros_like(low_packed)
    high_packed[...] = jnp.zeros_like(high_packed)
    for copy in copies[:2]:
        copy.wait()
    for i in range(RMAX):
        low_wide[pl.ds(i * pitch, chans), :] = x_ref[i].astype(F32)
        high_wide[pl.ds(i * pitch, chans), :] = x_ref[rows - RMAX + i].astype(F32)

    def upward(c, offset):
        low_packed[pl.ds(HALO + offset, RMAX), :] = low_wide[pl.ds(c, RMAX, stride=pitch), :]
        return offset + rad_ref[c]

    total = lax.fori_loop(0, chans, upward, 0, unroll=8)

    def downward(i, stop):
        c = chans - 1 - i
        high_packed[pl.ds(HALO + stop - RMAX, RMAX), :] = high_wide[pl.ds(c, RMAX, stride=pitch), :]
        return stop - rad_ref[c]

    lax.fori_loop(0, chans, downward, total, unroll=8)
    for packed, ref, rest_ref in ((low_packed, down_ref, down_rest_ref), (high_packed, up_ref, up_rest_ref)):
        ref[...] = packed[HALO:HALO + cap, :].astype(BF16)
        rest_ref[...] = packed[HALO + cap:HALO + full, :].astype(BF16)

    copies[2].wait()
    dec = lax.axis_index("dec")
    lane = lax.broadcasted_iota(jnp.int32, (chans, LANES), 1)
    for side, edge_ref in enumerate(edge_refs):
        if sides == 1:
            first = jnp.where(dec == 0, cols - RMAX, 0)
        else:
            first = cols - RMAX if side == 0 else 0
        for g, (start, count) in enumerate(row_groups(rows)):
            for j in range(count):
                shift = lax.rem(RMAX * j - first + 2 * LANES, LANES)
                piece = pltpu.roll(x_ref[start + j].astype(F32), shift, 1)
                packed = piece if j == 0 else jnp.where(lane < RMAX * j, packed, piece)
            edge_ref[g] = packed.astype(BF16)


def cap_of(chans):
    return RMAX * chans * 5 // 8 // 16 * 16


def edges_of(radii, x, sides):
    rows, chans, cols = x.shape
    full, cap = RMAX * chans, cap_of(chans)
    head, rest = (pltpu.VMEM((n, cols), BF16) for n in (cap, full - cap))
    packed = pltpu.VMEM((len(row_groups(rows)), chans, LANES), BF16)
    return pl.pallas_call(
        functools.partial(edges_kernel, sides),
        out_shape=[pltpu.VMEM(x.shape, BF16), head, rest, head, rest] + [packed] * sides,
        in_specs=[SMEM, pl.BlockSpec(memory_space=pl.ANY)],
        out_specs=[VMEM] * (5 + sides),
        scratch_shapes=[pltpu.VMEM((RMAX * (chans + PAD), cols), F32)] * 2
        + [pltpu.VMEM((full + 2 * HALO, cols), F32)] * 2
        + [pltpu.SemaphoreType.DMA((3,))],
        compiler_params=PARAMS,
        cost_estimate=pl.CostEstimate(flops=10**6, bytes_accessed=5 * 10**6, transcendentals=0),
    )(radii, x)


def widen(tile, j, side_tiles):
    lane = lax.broadcasted_iota(jnp.int32, tile.shape, 1)
    value = None
    for side, part in enumerate(side_tiles):
        shift = (RMAX * side - RMAX * j) % LANES
        part = part if shift == 0 else pltpu.roll(part, shift, 1)
        value = part if side == 0 else jnp.where(lane < RMAX, value, part)
    return value


def inner_kernel(sides, rad_ref, x_ref, dec_ref, ra_ref, *refs):
    edge_refs, (partial_ref, out_ref, own, halo, result) = refs[:sides], refs[sides:]
    rows, chans, cols = x_ref.shape
    pitch = chans + PAD
    own_rows, inner = partial_ref.shape[1], rows - 2 * RMAX

    def copy_row(i, carry):
        own[pl.ds(i * pitch, chans), :] = x_ref[i].astype(F32)
        return carry

    lax.fori_loop(0, rows, copy_row, 0)
    for i in range(rows, own_rows):
        own[pl.ds(i * pitch, chans), :] = jnp.zeros((chans, cols), F32)
        halo[pl.ds(i * pitch, chans), :] = jnp.zeros((chans, cols), F32)
    for g, (start, count) in enumerate(row_groups(rows)):
        tiles = [ref[g].astype(F32) for ref in edge_refs]
        for j in range(count):
            halo[pl.ds((start + j) * pitch, chans), :] = widen(tiles[0], j, tiles)

    def some_channels(i, carry):
        chosen = [i * BATCH + j for j in range(BATCH)]
        radii = [rad_ref[c] for c in chosen]
        partials = []
        for c, radius in zip(chosen, radii):
            picked = pl.ds(c, own_rows, stride=pitch)
            lhs = jnp.concatenate([own[picked, :].astype(BF16), halo[picked, :].astype(BF16)], 1)
            partials.append(jnp.dot(lhs, dec_ref[radius], preferred_element_type=F32).astype(BF16))
        for c, radius, partial in zip(chosen, radii, partials):
            partial_ref[c] = partial
            smoothed = jnp.dot(ra_ref[radius], partial, preferred_element_type=F32)
            result[pl.ds(c, inner, stride=pitch), :] = smoothed[:inner]
        return carry

    lax.fori_loop(0, chans // BATCH, some_channels, 0)

    def store(i, carry):
        out_ref[i] = result[pl.ds(i * pitch, chans), :].astype(BF16)
        return carry

    lax.fori_loop(0, inner, store, 0)


def smooth_inner(radii, x, halos, dec_table, ra_table):
    rows, chans, cols = x.shape
    pitch, own_rows, inner = chans + PAD, ra_table.shape[2], rows - 2 * RMAX
    operands = [x, dec_table, ra_table, *halos]
    return pl.pallas_call(
        functools.partial(inner_kernel, len(halos)),
        out_shape=[
            pltpu.VMEM((chans, own_rows, cols), BF16),
            pltpu.VMEM((inner, chans, cols), BF16),
        ],
        in_specs=[SMEM] + [VMEM] * len(operands),
        out_specs=[VMEM] * 2,
        scratch_shapes=[
            pltpu.VMEM((own_rows * pitch, cols), F32),
            pltpu.VMEM((own_rows * pitch, LANES), F32),
            pltpu.VMEM((inner * pitch, cols), F32),
        ],
        compiler_params=PARAMS,
        cost_estimate=pl.CostEstimate(flops=4 * 10**9, bytes_accessed=10**7, transcendentals=0),
    )(radii, *operands)


def outer_kernel(sides, rows, rad_ref, partial_ref, *refs):
    before_refs, after_refs, (dec_ref, ra_ref), refs = refs[:2], refs[2:4], refs[4:6], refs[6:]
    corner_refs, (out_ref, halo, before, after, result) = refs[:2 * sides], refs[2 * sides:]
    chans, _, cols = partial_ref.shape
    pitch = chans + PAD

    for packed, parts in ((before, before_refs), (after, after_refs)):
        packed[:HALO, :] = jnp.zeros((HALO, cols), F32)
        packed[packed.shape[0] - HALO:, :] = jnp.zeros((HALO, cols), F32)
        start = HALO
        for part in parts:
            packed[start:start + part.shape[0], :] = part[...].astype(F32)
            start += part.shape[0]

    groups = row_groups(rows)
    for part, base in ((0, 0), (1, HALO)):
        for g, (start, count) in enumerate(groups[:EDGE] if part else groups[-EDGE:]):
            tiles = [corner_refs[2 * side + part][g].astype(F32) for side in range(sides)]
            for j in range(count):
                row = start + j if part else start + j - (rows - RMAX)
                if 0 <= row < RMAX:
                    halo[pl.ds((base + row) * pitch, chans), :] = widen(tiles[0], j, tiles)
        for row in range(RMAX, HALO):
            halo[pl.ds((base + row) * pitch, chans), :] = jnp.zeros((chans, LANES), F32)

    def some_channels(i, offset):
        chosen = [i * BATCH + j for j in range(BATCH)]
        radii = [rad_ref[c] for c in chosen]
        partials = []
        for c, radius in zip(chosen, radii):
            planes = [
                before[pl.ds(HALO - RMAX + offset + radius, HALO), :],
                after[pl.ds(HALO + offset, HALO), :],
            ]
            picked = pl.ds(c, 2 * HALO, stride=pitch)
            lhs = jnp.concatenate([jnp.concatenate(planes, 0).astype(BF16), halo[picked, :].astype(BF16)], 1)
            partials.append(jnp.dot(lhs, dec_ref[radius], preferred_element_type=F32).astype(BF16))
            offset = offset + radius
        for c, radius, partial in zip(chosen, radii, partials):
            smoothed = jnp.dot(
                ra_ref[radius], jnp.concatenate([partial_ref[c], partial], 0), preferred_element_type=F32
            )
            result[pl.ds(c, RMAX, stride=pitch), :] = smoothed[:RMAX]
            result[pl.ds(RMAX * pitch + c, RMAX, stride=pitch), :] = smoothed[HALO:HALO + RMAX]
        return offset

    lax.fori_loop(0, chans // BATCH, some_channels, 0)

    def store(i, carry):
        out_ref[i] = result[pl.ds(i * pitch, chans), :].astype(BF16)
        return carry

    lax.fori_loop(0, 2 * RMAX, store, 0)


def smooth_outer(radii, rows, partial, before, after, dec_table, ra_table, corners):
    chans, _, cols = partial.shape
    pitch = chans + PAD
    operands = [partial, *before, *after, dec_table, ra_table] + [part for side in corners for part in side]
    return pl.pallas_call(
        functools.partial(outer_kernel, len(corners), rows),
        out_shape=pltpu.VMEM((2 * RMAX, chans, cols), BF16),
        in_specs=[SMEM] + [VMEM] * len(operands),
        out_specs=VMEM,
        scratch_shapes=[
            pltpu.VMEM((2 * HALO * pitch, LANES), F32),
            pltpu.VMEM((RMAX * chans + 2 * HALO, cols), F32),
            pltpu.VMEM((RMAX * chans + 2 * HALO, cols), F32),
            pltpu.VMEM((2 * RMAX * pitch, cols), F32),
        ],
        compiler_params=PARAMS,
        cost_estimate=pl.CostEstimate(flops=2 * 10**9, bytes_accessed=5 * 10**6, transcendentals=0),
    )(radii, *operands)


SUM_ROWS = 8


def add_products(total, own_ref, other_ref, valid_ref, first_row, rows):
    chans = own_ref.shape[1]
    depth = max(d for d in range(1, 27) if rows % d == 0)

    def nt(a, b):
        return lax.dot_general(a, b, (((1,), (1,)), ((), ())), preferred_element_type=F32)

    def body(i, carry):
        picked = [i * depth + j for j in range(depth)]
        line = jnp.concatenate([valid_ref[pl.ds(first_row(r), 1), :].astype(BF16) for r in picked], 1)
        own, other = (jnp.concatenate([ref[r] for r in picked], 1) for ref in (own_ref, other_ref))
        both = jnp.concatenate([own, other], 0)
        total[:2 * chans, :] += nt(both, own * line)
        sums = nt(jnp.broadcast_to(line, (16, line.shape[1])), both)[:SUM_ROWS]
        total[2 * chans:2 * chans + SUM_ROWS, :] += sums[:, :chans]
        total[2 * chans + SUM_ROWS:, :] += sums[:, chans:]
        return carry

    lax.fori_loop(0, rows // depth, body, 0)


def inner_gram_kernel(own_ref, other_ref, valid_ref, total_ref):
    total_ref[...] = jnp.zeros_like(total_ref)
    add_products(total_ref, own_ref, other_ref, valid_ref, lambda r: r + RMAX, own_ref.shape[0])


def inner_gram(own, other, valid):
    chans = own.shape[1]
    return pl.pallas_call(
        inner_gram_kernel,
        out_shape=pltpu.VMEM((2 * chans + 2 * SUM_ROWS, chans), F32),
        in_specs=[VMEM] * 3,
        out_specs=VMEM,
        compiler_params=PARAMS,
        cost_estimate=pl.CostEstimate(flops=10**9, bytes_accessed=3 * 10**6, transcendentals=0),
    )(own, other, valid)


def gram_kernel(inner_ref, own_ref, other_ref, valid_ref, inner_own_ref, out_ref, smoothed_ref, total, sems):
    rows, chans = valid_ref.shape[0], own_ref.shape[1]
    band = lax.axis_index("band")
    copies = [
        pltpu.make_async_copy(source, smoothed_ref.at[pl.ds(start, source.shape[0])], sems.at[i])
        for i, (source, start) in enumerate((
            (inner_own_ref, RMAX),
            (own_ref.at[pl.ds(0, RMAX)], 0),
            (own_ref.at[pl.ds(RMAX, RMAX)], rows - RMAX),
        ))
    ]
    for copy in copies:
        copy.start()
    total[...] = inner_ref[...]
    add_products(
        total, own_ref, other_ref, valid_ref, lambda r: jnp.where(r < RMAX, r, r + rows - 2 * RMAX), 2 * RMAX
    )
    out_ref[pl.ds(pl.multiple_of(band * chans, chans), chans), :] = total[:chans, :]
    out_ref[pl.ds(pl.multiple_of((1 - band) * chans, chans), chans), :] = total[chans:2 * chans, :]
    row = lax.broadcasted_iota(jnp.int32, (SUM_ROWS, chans), 0)
    own_sum, other_sum = total[2 * chans:2 * chans + SUM_ROWS, :], total[2 * chans + SUM_ROWS:, :]
    sums = jnp.where(row == band, own_sum, other_sum)
    out_ref[2 * chans:, :] = jnp.where(row == 2, jnp.sum(valid_ref[...].astype(F32)), sums)
    for copy in copies:
        copy.wait()


def gram(inner, own, other, valid, inner_own):
    _, chans, cols = own.shape
    return pl.pallas_call(
        gram_kernel,
        out_shape=[
            pltpu.VMEM((2 * chans + SUM_ROWS, chans), F32),
            jax.ShapeDtypeStruct((valid.shape[0], chans, cols), BF16),
        ],
        in_specs=[VMEM] * 5,
        out_specs=[VMEM, pl.BlockSpec(memory_space=pl.ANY)],
        scratch_shapes=[pltpu.VMEM(inner.shape, F32), pltpu.SemaphoreType.DMA((3,))],
        compiler_params=PARAMS,
    )(inner, own, other, valid, inner_own)


def finish_kernel(mine_ref, theirs_ref, mean_ref, cov_ref):
    chans = mine_ref.shape[1]
    band = lax.axis_index("band")
    block = mine_ref[:2 * chans, :] + theirs_ref[:2 * chans, :]
    tail = mine_ref[2 * chans:, :] + theirs_ref[2 * chans:, :]
    count = tail[2:3, 0:1]
    means = tail / count
    own = jnp.where(band == 0, means[0:1, :], means[1:2, :])
    mean_ref[...] = own
    for b in range(2):
        column = jnp.transpose(jnp.broadcast_to(means[b:b + 1, :], (chans, chans)))
        part = block[b * chans:(b + 1) * chans]
        cov_ref[b * chans:(b + 1) * chans, :] = (part - count * column * own) / (count - 1.0)


def finish(mine, theirs):
    chans = mine.shape[1]
    mean, covariance = pl.pallas_call(
        finish_kernel,
        out_shape=[jax.ShapeDtypeStruct((1, chans), F32), jax.ShapeDtypeStruct((2 * chans, chans), F32)],
        in_specs=[VMEM] * 2,
        out_specs=[VMEM] * 2,
        compiler_params=PARAMS,
    )(mine, theirs)
    return mean.reshape(chans), covariance


def swap(array, axis, step):
    size = lax.axis_size(axis)
    return lax.ppermute(array, axis, [(i, i ^ step) for i in range(size)])


def diagonal(array, ra_step, dec_pairs):
    ra_size, dec_size = lax.axis_size("ra"), lax.axis_size("dec")
    pairs = [
        (i * dec_size + a, (i + ra_step) % ra_size * dec_size + b) for i in range(ra_size) for a, b in dec_pairs
    ]
    return lax.ppermute(array, ("ra", "dec"), pairs)


def per_device(sky_maps, radii, valid):
    x = jnp.transpose(sky_maps, (1, 0, 2))
    rows, chans, cols = x.shape
    ra_size, dec_size = lax.axis_size("ra"), lax.axis_size("dec")
    up = [(i, (i + 1) % ra_size) for i in range(ra_size)]
    down = [(j, i) for i, j in up]
    right = [(i, i + 1) for i in range(dec_size - 1)]
    left = [(j, i) for i, j in right]
    sides = [right + left] if dec_size == 2 else [right, left]
    x, up_head, up_rest, down_head, down_rest, *packed = edges_of(radii, x, len(sides))
    over = jnp.sum(radii) > cap_of(chans)
    before_rest, after_rest = lax.cond(
        over,
        lambda a, b: (lax.ppermute(a, "ra", up), lax.ppermute(b, "ra", down)),
        lambda a, b: (a, b),
        up_rest, down_rest,
    )
    before_rest, after_rest, up_head, down_head = lax.optimization_barrier((before_rest, after_rest, up_head, down_head))
    before, after = lax.ppermute(up_head, "ra", up), lax.ppermute(down_head, "ra", down)
    halos = [lax.ppermute(p, "dec", pairs) for p, pairs in zip(packed, sides)]
    corners = [
        (diagonal(p[-EDGE:], 1, pairs), diagonal(p[:EDGE], -1, pairs)) for p, pairs in zip(packed, sides)
    ]
    dec_table, inner_table, outer_table = tables(rows, cols, len(sides))
    halos, corners = lax.optimization_barrier((halos, corners))
    partial, inner = smooth_inner(radii, x, halos, dec_table, inner_table)
    outer = smooth_outer(
        radii, rows, partial, (before, before_rest), (after, after_rest), dec_table, outer_table, corners
    )
    inner_total = inner_gram(inner, swap(inner, "band", 1), valid)
    total, smoothed = gram(inner_total, outer, swap(outer, "band", 1), valid, inner)
    steps = [("dec", 1 << b) for b in range(dec_size.bit_length() - 1)]
    steps += [("ra", 1 << b) for b in range(ra_size.bit_length() - 1)]
    for axis, step in steps[:-1]:
        total = total + swap(total, axis, step)
    mean, covariance = finish(total, swap(total, *steps[-1]))
    return (jnp.transpose(smoothed, (1, 0, 2)), mean, covariance)


def solution(mesh):
    return jax.shard_map(
        per_device,
        mesh=mesh,
        in_specs=(
            P(("groups", "band"), "ra", "dec"),
            P(("groups", "band")),
            P(("groups", "ra"), "dec"),
        ),
        out_specs=(P(("groups", "band"), "ra", "dec"), P(("groups", "band")), P("groups", "band")),
        check_vma=False,
    )
```

time: 84.8 us -> 64 us (0.75)
  waiting for transfers between devices: 36.8 us -> 20.3 us
  Pallas kernels: 26.8 us -> 20.9 us
  starting transfers between devices: 13.7 us -> 16.7 us
  local copies, waits for them, and re-layouts: 5.57 us -> 3.79 us
    ppermute x2, waiting for transfers between devices: 16.6 us -> 0.54 us  [diagonal(): return lax.ppermute(array, ('ra', 'dec'), pairs)]
    ppermute x4 -> x5, waiting for transfers between devices: 20.2 us -> 14.2 us  [swap(): return lax.ppermute(array, axis, [(i, i ^ step) for i in range(size)])]
    ppermute x3, waiting for transfers between devices: 0.01 us -> 5.52 us  [the longest x1 4.72 us: per_device(): lax.ppermute(down_head, 'ra', down)]
    pallas_call x4 -> x6, Pallas kernels: 25 us -> 20.1 us  [the longest x1 6.38 us: smooth_inner(): pl.pallas_call(functools.partial(inner_kernel, len(halos)), out_shape=[pl...]
    ppermute x4 -> x5, starting transfers between devices: 3.29 us -> 5.31 us  [swap(): return lax.ppermute(array, axis, [(i, i ^ step) for i in range(size)])]
    slice x1 -> x0, local copies, waits for them, and re-layouts: 1.34 us -> none  [per_device(): x[:RMAX, r]]
    ppermute x3, starting transfers between devices: 6.6 us -> 7.79 us  [the longest x1 3.89 us: per_device(): lax.ppermute(down_head, 'ra', down)]
    pallas_call x1, Pallas kernels: 1.77 us -> 0.81 us  [finish(): pl.pallas_call(finish_kernel, out_shape=[jax.ShapeDtypeStruct((1, chans),...]
  transfers between devices with their start and end apart: 9 -> 10, of which waited for: 6 -> 8; matrix products, arithmetic and copies ran while one was open for 1% -> 2% of each run, Pallas kernels for 8% -> 25%
where the time goes in v3:
time: 64 us; the launch traced here: 63.8 us
  Pallas kernels  20.9 us (33%)
  waiting for transfers between devices  20.3 us (32%)
  starting transfers between devices  16.7 us (26%)
  local copies, waits for them, and re-layouts  3.79 us (6%)
  between operations  1.4 us (2%)
  other arithmetic  0.67 us (1%)
    ppermute x5, waiting for transfers between devices, swap(): return lax.ppermute(array, axis, [(i, i ^ step) for i in range(size)])  14.2 us
    pallas_call x1, Pallas kernels, smooth_inner(): pl.pallas_call(functools.partial(inner_kernel, len(halos)), out_shape=[pl...  6.38 us
    pallas_call x1, Pallas kernels, smooth_outer(): pl.pallas_call(functools.partial(outer_kernel, len(corners), rows), out_s...  5.44 us
    ppermute x5, starting transfers between devices, swap(): return lax.ppermute(array, axis, [(i, i ^ step) for i in range(size)])  5.31 us
    ppermute x1, waiting for transfers between devices, per_device(): lax.ppermute(down_head, 'ra', down)  4.72 us
    ppermute x1, starting transfers between devices, per_device(): lax.ppermute(down_head, 'ra', down)  3.89 us
    ppermute x2, starting transfers between devices, diagonal(): return lax.ppermute(array, ('ra', 'dec'), pairs)  3.59 us
    unnamed x16, local copies, waits for them, and re-layouts  3.11 us
  transfers between devices with their start and end apart: 10, of which 8 were waited for; matrix products, arithmetic and copies ran while one was open for 2% of the time, Pallas kernels for 25%

profile of v3, /device:TPU:0, one launch (start us, length us, event | category | flops | bytes accessed | tf_op | source)
XLA Modules:
  0.0 63.8 jit_solution(12188120115709912719)
XLA Ops:
  0.6 1.7 %copy-done = bf16[128,78,128]{2,0,1:T(8,128)(2,1)S(1)} copy-done((bf16[128,78,128]{2,0,1:T(8,128)(2,1)S(1)}, bf16[128,78,128]{2,0,1:T(8,128)(2,1)}, u32[]{:S(2)}) %copy-start) | copy-done | bytes 2555928
  2.4 0.7 %copy-done.2 = s32[128]{0:T(128)S(1)} copy-done((s32[128]{0:T(128)S(1)}, s32[128]{0:T(128)}, u32[]{:S(2)}) %copy-start.2) | copy-done | bytes 536
  3.0 2.8 %shard_map.58 = (bf16[78,128,128]{2,1,0:T(8,128)(2,1)S(1)}, bf16[1360,128]{1,0:T(8,128)(2,1)S(1)}, bf16[816,128]{1,0:T(8,128)(2,1)S(1)}, bf16[1360,128]{1,0:T(8,...) custom-call(s32[128]{0:T(128)S(1)} %copy-done.2, bf16[78,128,128]{2,1,0:T(8,128)(2,1)S(1)} %bitcast.3), custom_call_target="tpu_custom_call" | custom-call | flops 1000000 | bytes 5000000 | tf_op jit(solution)/shard_map/pallas_call | solution.py:153
  5.9 0.7 %copy-done.5 = bf16[1360,128]{1,0:T(8,128)(2,1)} copy-done((bf16[1360,128]{1,0:T(8,128)(2,1)}, bf16[1360,128]{1,0:T(8,128)(2,1)S(1)}, u32[]{:S(2)}) %copy-start.5) | copy-done | bytes 348184
  6.6 2.9 %collective-permute-start.2 = (bf16[12,128,128]{2,1,0:T(8,128)(2,1)S(1)}, bf16[12,128,128]{2,1,0:T(8,128)(2,1)S(1)}, u32[]{:S(2)}, u32[]{:S(2)}) collective-permute-start(bf16[12,128,128]{2,1,0:T(8,128)(2,1)S(1)} %get-tuple-element.40), channel_id=1, source_target_pairs={{0,2},{2,0},{1,3},{3,1},{4,6},{6,4},{5,7},{7,5},{8,10},{10,8},{9,1... | collective-permute-start | bytes 1179656 | tf_op jit(solution)/shard_map/ppermute | solution.py:457
  9.5 0.7 %fusion = (bf16[3,128,128]{2,1,0:T(8,128)(2,1)}, bf16[3,128,128]{2,1,0:T(8,128)(2,1)}) fusion(bf16[12,128,128]{2,1,0:T(8,128)(2,1)S(1)} %get-tuple-element.40), kind=kLoop, calls=%fused_computation | loop fusion | bytes 393216 | tf_op jit(solution)/shard_map/slice | solution.py:459
  10.2 3.6 %collective-permute-start.4 = (bf16[3,128,128]{2,1,0:T(8,128)(2,1)}, bf16[3,128,128]{2,1,0:T(8,128)(2,1)}, u32[]{:S(2)}, u32[]{:S(2)}) collective-permute-start(bf16[3,128,128]{2,1,0:T(8,128)(2,1)} %get-tuple-element.61), channel_id=1, source_target_pairs={{0,14},{2,12},{4,2},{6,0},{8,6},{10,4},{12,10},{14,8},{1,15},{3,13... | collective-permute-start | bytes 294920 | tf_op jit(solution)/shard_map/ppermute | solution.py:435
  13.8 0.6 reduce_sum.9
  15.1 1.0 %collective-permute-start.6 = (bf16[1360,128]{1,0:T(8,128)(2,1)}, bf16[1360,128]{1,0:T(8,128)(2,1)S(1)}, u32[]{:S(2)}, u32[]{:S(2)}) collective-permute-start(bf16[1360,128]{1,0:T(8,128)(2,1)} %copy-done.5), channel_id=1, source_target_pairs={{0,4},{4,8},{8,12},{12,0},{1,5},{5,9},{9,13},{13,1},{2,6},{6,10},{... | collective-permute-start | bytes 1044488 | tf_op jit(solution)/shard_map/ppermute | solution.py:456
  16.1 3.9 %collective-permute-start.7 = (bf16[1360,128]{1,0:T(8,128)(2,1)}, bf16[1360,128]{1,0:T(8,128)(2,1)S(1)}, u32[]{:S(2)}, u32[]{:S(2)}) collective-permute-start(bf16[1360,128]{1,0:T(8,128)(2,1)} %copy-done.4), channel_id=1, source_target_pairs={{4,0},{8,4},{12,8},{0,12},{5,1},{9,5},{13,9},{1,13},{6,2},{10,6},{... | collective-permute-start | bytes 1044488 | tf_op jit(solution)/shard_map/ppermute | solution.py:456
  20.0 2.1 %shard_map.59 = (bf16[18,256,128]{2,1,0:T(8,128)(2,1)S(1)}, bf16[18,48,80]{2,1,0:T(8,128)(2,1)S(1)}, bf16[18,48,128]{2,1,0:T(8,128)(2,1)S(1)}) custom-call(), custom_call_target="tpu_custom_call" | custom-call | flops 100000 | bytes 100000 | tf_op jit(solution)/shard_map/pallas_call | solution.py:81
  22.8 6.4 %shard_map.60 = (bf16[128,80,128]{2,1,0:T(8,128)(2,1)S(1)}, bf16[44,128,128]{2,1,0:T(8,128)(2,1)S(1)}) custom-call(s32[128]{0:T(128)S(1)} %copy-done.3, bf16[78,128,128]{2,1,0:T(8,128)(2,1)S(1)} %get-tuple-element.37.x_ref, bf16[18,256,128]{2,1,0:T(8,128)(2,1)S(1)} %get-tuple-element.38.dec_ref.refs_4_, bf16[18,48,80]{2,1,0:T(8,128)(2,1)S(1)} %get-tuple-element.39.ra_ref, ...), custom_call_target="tpu_custom_call" | custom-call | flops 4000000000 | bytes 10000000 | tf_op jit(solution)/shard_map/pallas_call | solution.py:222
  29.9 4.7 %collective-permute-done.7.refs_2_ = bf16[1360,128]{1,0:T(8,128)(2,1)S(1)} collective-permute-done((bf16[1360,128]{1,0:T(8,128)(2,1)}, bf16[1360,128]{1,0:T(8,128)(2,1)S(1)}, u32[]{:S(2)}, u32[]{:S(2)}) %collective-permute-start.7) | collective-permute-done | bytes 348192 | tf_op jit(solution)/shard_map/ppermute | solution.py:456
  34.6 5.4 %shard_map.62.own_ref = bf16[34,128,128]{2,1,0:T(8,128)(2,1)S(1)} custom-call(s32[128]{0:T(128)S(1)} %copy-done.3, bf16[128,80,128]{2,1,0:T(8,128)(2,1)S(1)} %get-tuple-element.43.partial_ref, bf16[1360,128]{1,0:T(8,128)(2,1)S(1)} %collective-permute-done.6.refs_0_, bf16[816,128]{1,0:T(8,128)(2,1)S(1)} %copy-done.7, ...), custom_call_target="tpu_custom_call" | custom-call | flops 2000000000 | bytes 5000000 | tf_op jit(solution)/shard_map/pallas_call | solution.py:299
  40.2 1.7 %shard_map.61.inner_ref = f32[272,128]{1,0:T(8,128)S(1)} custom-call(bf16[44,128,128]{2,1,0:T(8,128)(2,1)S(1)} %get-tuple-element.42.own_ref.inner_own_ref, bf16[44,128,128]{2,1,0:T(8,128)(2,1)S(1)} %collective-permute-done.5.other_ref, s32[78,128]{1,0:T(8,128)S(1)} %copy-done.1), custom_call_target="tpu_custom_call" | custom-call | flops 1000000000 | bytes 3000000 | tf_op jit(solution)/shard_map/pallas_call | solution.py:346
  41.9 1.0 %collective-permute-done.8.other_ref = bf16[34,128,128]{2,1,0:T(8,128)(2,1)S(1)} collective-permute-done((bf16[34,128,128]{2,1,0:T(8,128)(2,1)S(1)}, bf16[34,128,128]{2,1,0:T(8,128)(2,1)S(1)}, u32[]{:S(2)}, u32[]{:S(2)}) %collective-permute-start.8) | collective-permute-done | bytes 1114144 | tf_op jit(solution)/shard_map/ppermute | solution.py:427
  42.9 1.6 %shard_map.63 = (f32[264,128]{1,0:T(8,128)S(1)}, bf16[78,128,128]{2,1,0:T(8,128)(2,1)}) custom-call(f32[272,128]{1,0:T(8,128)S(1)} %shard_map.61.inner_ref, bf16[34,128,128]{2,1,0:T(8,128)(2,1)S(1)} %shard_map.62.own_ref, bf16[34,128,128]{2,1,0:T(8,128)(2,1)S(1)} %collective-permute-done.8.other_ref, s32[78,128]{1,0:T(8,128)S(1)} %copy-done.1, ...), custom_call_target="tpu_custom_call" | custom-call | tf_op jit(solution)/shard_map/pallas_call | solution.py:385
  44.5 1.3 %collective-permute-start.9 = (f32[264,128]{1,0:T(8,128)S(1)}, f32[264,128]{1,0:T(8,128)S(1)}, u32[]{:S(2)}, u32[]{:S(2)}) collective-permute-start(f32[264,128]{1,0:T(8,128)S(1)} %get-tuple-element.58), channel_id=1, source_target_pairs={{0,2},{2,0},{1,3},{3,1},{4,6},{6,4},{5,7},{7,5},{8,10},{10,8},{9,1... | collective-permute-start | bytes 405512 | tf_op jit(solution)/shard_map/ppermute | solution.py:427
  45.8 4.4 %collective-permute-done.9 = f32[264,128]{1,0:T(8,128)S(1)} collective-permute-done((f32[264,128]{1,0:T(8,128)S(1)}, f32[264,128]{1,0:T(8,128)S(1)}, u32[]{:S(2)}, u32[]{:S(2)}) %collective-permute-start.9) | collective-permute-done | bytes 135200 | tf_op jit(solution)/shard_map/ppermute | solution.py:427
  50.2 1.9 %collective-permute-start.10 = (f32[264,128]{1,0:T(8,128)S(1)}, f32[264,128]{1,0:T(8,128)S(1)}, u32[]{:S(2)}, u32[]{:S(2)}) collective-permute-start(f32[264,128]{1,0:T(8,128)S(1)} %add.6), channel_id=1, source_target_pairs={{0,4},{4,0},{8,12},{12,8},{1,5},{5,1},{9,13},{13,9},{2,6},{6,2},{1... | collective-permute-start | bytes 405512 | tf_op jit(solution)/shard_map/ppermute | solution.py:427
  52.1 3.1 %collective-permute-done.10 = f32[264,128]{1,0:T(8,128)S(1)} collective-permute-done((f32[264,128]{1,0:T(8,128)S(1)}, f32[264,128]{1,0:T(8,128)S(1)}, u32[]{:S(2)}, u32[]{:S(2)}) %collective-permute-start.10) | collective-permute-done | bytes 135200 | tf_op jit(solution)/shard_map/ppermute | solution.py:427
  55.3 2.0 %collective-permute-start.11 = (f32[264,128]{1,0:T(8,128)S(1)}, f32[264,128]{1,0:T(8,128)S(1)}, u32[]{:S(2)}, u32[]{:S(2)}) collective-permute-start(f32[264,128]{1,0:T(8,128)S(1)} %add.7.mine_ref), channel_id=1, source_target_pairs={{0,8},{4,12},{8,0},{12,4},{1,9},{5,13},{9,1},{13,5},{2,10},{6,14},... | collective-permute-start | bytes 405512 | tf_op jit(solution)/shard_map/ppermute | solution.py:427
  57.3 5.7 %collective-permute-done.11.theirs_ref = f32[264,128]{1,0:T(8,128)S(1)} collective-permute-done((f32[264,128]{1,0:T(8,128)S(1)}, f32[264,128]{1,0:T(8,128)S(1)}, u32[]{:S(2)}, u32[]{:S(2)}) %collective-permute-start.11) | collective-permute-done | bytes 135200 | tf_op jit(solution)/shard_map/ppermute | solution.py:427
  62.9 0.8 %shard_map.64 = (f32[1,128]{1,0:T(1,128)}, f32[256,128]{1,0:T(8,128)}) custom-call(f32[264,128]{1,0:T(8,128)S(1)} %add.7.mine_ref, f32[264,128]{1,0:T(8,128)S(1)} %collective-permute-done.11.theirs_ref), custom_call_target="tpu_custom_call" | custom-call | tf_op jit(solution)/shard_map/pallas_call | solution.py:415
  (24 shorter events, 1.6 us)
Async XLA Ops:
  0.6 1.7 %copy-start = (bf16[128,78,128]{2,0,1:T(8,128)(2,1)S(1)}, bf16[128,78,128]{2,0,1:T(8,128)(2,1)}, u32[]{:S(2)}) copy-start(bf16[128,78,128]{2,0,1:T(8,128)(2,1)} %param.5) | copy-start | bytes 7667716
  2.4 0.7 %copy-start.2 = (s32[128]{0:T(128)S(1)}, s32[128]{0:T(128)}, u32[]{:S(2)}) copy-start(s32[128]{0:T(128)} %rad_ref.5) | copy-start | bytes 1540
  3.0 10.8 %copy-start.3 = (s32[128]{0:T(128)S(1)}, s32[128]{0:T(128)}, u32[]{:S(2)}) copy-start(s32[128]{0:T(128)} %rad_ref.5) | copy-start | bytes 1540
  5.8 0.7 %copy-start.5 = (bf16[1360,128]{1,0:T(8,128)(2,1)}, bf16[1360,128]{1,0:T(8,128)(2,1)S(1)}, u32[]{:S(2)}) copy-start(bf16[1360,128]{1,0:T(8,128)(2,1)S(1)} %get-tuple-element.50) | copy-start | bytes 1044484
  6.6 3.6 %copy-start.4 = (bf16[1360,128]{1,0:T(8,128)(2,1)}, bf16[1360,128]{1,0:T(8,128)(2,1)S(1)}, u32[]{:S(2)}) copy-start(bf16[1360,128]{1,0:T(8,128)(2,1)S(1)} %get-tuple-element.52) | copy-start | bytes 1044484
  6.6 3.6 %copy-start.6 = (bf16[816,128]{1,0:T(8,128)(2,1)}, bf16[816,128]{1,0:T(8,128)(2,1)S(1)}, u32[]{:S(2)}) copy-start(bf16[816,128]{1,0:T(8,128)(2,1)S(1)} %get-tuple-element.44) | copy-start | bytes 626692
  6.6 16.3 %collective-permute-start.2 = (bf16[12,128,128]{2,1,0:T(8,128)(2,1)S(1)}, bf16[12,128,128]{2,1,0:T(8,128)(2,1)S(1)}, u32[]{:S(2)}, u32[]{:S(2)}) collective-permute-start(bf16[12,128,128]{2,1,0:T(8,128)(2,1)S(1)} %get-tuple-element.40), channel_id=1, source_target_pairs={{0,2},{2,0},{1,3},{3,1},{4,6},{6,4},{5,7},{7,5},{8,10},{10,8},{9,1... | collective-permute-start | bytes 1179656 | tf_op jit(solution)/shard_map/ppermute | solution.py:457
  10.2 11.9 %collective-permute-start.4 = (bf16[3,128,128]{2,1,0:T(8,128)(2,1)}, bf16[3,128,128]{2,1,0:T(8,128)(2,1)}, u32[]{:S(2)}, u32[]{:S(2)}) collective-permute-start(bf16[3,128,128]{2,1,0:T(8,128)(2,1)} %get-tuple-element.61), channel_id=1, source_target_pairs={{0,14},{2,12},{4,2},{6,0},{8,6},{10,4},{12,10},{14,8},{1,15},{3,13... | collective-permute-start | bytes 294920 | tf_op jit(solution)/shard_map/ppermute | solution.py:435
  13.8 8.8 %collective-permute-start.3 = (bf16[3,128,128]{2,1,0:T(8,128)(2,1)}, bf16[3,128,128]{2,1,0:T(8,128)(2,1)}, u32[]{:S(2)}, u32[]{:S(2)}) collective-permute-start(bf16[3,128,128]{2,1,0:T(8,128)(2,1)} %get-tuple-element.62), channel_id=1, source_target_pairs={{0,6},{2,4},{4,10},{6,8},{8,14},{10,12},{12,2},{14,0},{1,7},{3,5},... | collective-permute-start | bytes 294920 | tf_op jit(solution)/shard_map/ppermute | solution.py:435
  15.1 14.8 %collective-permute-start.6 = (bf16[1360,128]{1,0:T(8,128)(2,1)}, bf16[1360,128]{1,0:T(8,128)(2,1)S(1)}, u32[]{:S(2)}, u32[]{:S(2)}) collective-permute-start(bf16[1360,128]{1,0:T(8,128)(2,1)} %copy-done.5), channel_id=1, source_target_pairs={{0,4},{4,8},{8,12},{12,0},{1,5},{5,9},{9,13},{13,1},{2,6},{6,10},{... | collective-permute-start | bytes 1044488 | tf_op jit(solution)/shard_map/ppermute | solution.py:456
  16.1 18.5 %collective-permute-start.7 = (bf16[1360,128]{1,0:T(8,128)(2,1)}, bf16[1360,128]{1,0:T(8,128)(2,1)S(1)}, u32[]{:S(2)}, u32[]{:S(2)}) collective-permute-start(bf16[1360,128]{1,0:T(8,128)(2,1)} %copy-done.4), channel_id=1, source_target_pairs={{4,0},{8,4},{12,8},{0,12},{5,1},{9,5},{13,9},{1,13},{6,2},{10,6},{... | collective-permute-start | bytes 1044488 | tf_op jit(solution)/shard_map/ppermute | solution.py:456
  22.8 11.8 %copy-start.7 = (bf16[816,128]{1,0:T(8,128)(2,1)S(1)}, bf16[816,128]{1,0:T(8,128)(2,1)}, u32[]{:S(2)}) copy-start(bf16[816,128]{1,0:T(8,128)(2,1)} %get-tuple-element.51.refs_1_) | copy-start | bytes 626692
  29.2 10.9 %collective-permute-start.5 = (bf16[44,128,128]{2,1,0:T(8,128)(2,1)S(1)}, bf16[44,128,128]{2,1,0:T(8,128)(2,1)S(1)}, u32[]{:S(2)}, u32[]{:S(2)}) collective-permute-start(bf16[44,128,128]{2,1,0:T(8,128)(2,1)S(1)} %get-tuple-element.42.own_ref.inner_own_ref), channel_id=1, source_target_pairs={{0,1},{1,0},{2,3},{3,2},{4,5},{5,4},{6,7},{7,6},{8,9},{9,8},{10,11... | collective-permute-start | bytes 4325384 | tf_op jit(solution)/shard_map/ppermute | solution.py:427
  34.6 5.5 %copy-start.1 = (s32[78,128]{1,0:T(8,128)S(1)}, s32[78,128]{1,0:T(8,128)}, u32[]{:S(2)}) copy-start(s32[78,128]{1,0:T(8,128)} %valid_ref.3) | copy-start | bytes 119812
  40.1 2.8 %collective-permute-start.8 = (bf16[34,128,128]{2,1,0:T(8,128)(2,1)S(1)}, bf16[34,128,128]{2,1,0:T(8,128)(2,1)S(1)}, u32[]{:S(2)}, u32[]{:S(2)}) collective-permute-start(bf16[34,128,128]{2,1,0:T(8,128)(2,1)S(1)} %shard_map.62.own_ref), channel_id=1, source_target_pairs={{0,1},{1,0},{2,3},{3,2},{4,5},{5,4},{6,7},{7,6},{8,9},{9,8},{10,11... | collective-permute-start | bytes 3342344 | tf_op jit(solution)/shard_map/ppermute | solution.py:427
  44.5 5.7 %collective-permute-start.9 = (f32[264,128]{1,0:T(8,128)S(1)}, f32[264,128]{1,0:T(8,128)S(1)}, u32[]{:S(2)}, u32[]{:S(2)}) collective-permute-start(f32[264,128]{1,0:T(8,128)S(1)} %get-tuple-element.58), channel_id=1, source_target_pairs={{0,2},{2,0},{1,3},{3,1},{4,6},{6,4},{5,7},{7,5},{8,10},{10,8},{9,1... | collective-permute-start | bytes 405512 | tf_op jit(solution)/shard_map/ppermute | solution.py:427
  50.2 5.1 %collective-permute-start.10 = (f32[264,128]{1,0:T(8,128)S(1)}, f32[264,128]{1,0:T(8,128)S(1)}, u32[]{:S(2)}, u32[]{:S(2)}) collective-permute-start(f32[264,128]{1,0:T(8,128)S(1)} %add.6), channel_id=1, source_target_pairs={{0,4},{4,0},{8,12},{12,8},{1,5},{5,1},{9,13},{13,9},{2,6},{6,2},{1... | collective-permute-start | bytes 405512 | tf_op jit(solution)/shard_map/ppermute | solution.py:427
  55.3 7.6 %collective-permute-start.11 = (f32[264,128]{1,0:T(8,128)S(1)}, f32[264,128]{1,0:T(8,128)S(1)}, u32[]{:S(2)}, u32[]{:S(2)}) collective-permute-start(f32[264,128]{1,0:T(8,128)S(1)} %add.7.mine_ref), channel_id=1, source_target_pairs={{0,8},{4,12},{8,0},{12,4},{1,9},{5,13},{9,1},{13,5},{2,10},{6,14},... | collective-permute-start | bytes 405512 | tf_op jit(solution)/shard_map/ppermute | solution.py:427

commit v4 on v3

v4 whole, which is shorter than its diff:
```python
import functools

import jax
import jax.numpy as jnp
from jax import lax
from jax.experimental import pallas as pl
from jax.experimental.pallas import tpu as pltpu
from jax.sharding import PartitionSpec as P

RMAX = 17
LANES = 128
SLOTS = LANES // RMAX
EDGE = -(-RMAX // SLOTS)
PAD = 8
HALO = 24
VMEM_LIMIT = 32 * 1024 * 1024
BF16, F32 = jnp.bfloat16, jnp.float32
VMEM = pl.BlockSpec(memory_space=pltpu.VMEM)
SMEM = pl.BlockSpec(memory_space=pltpu.SMEM)
HBM = pl.BlockSpec(memory_space=pltpu.HBM)
PARAMS = pltpu.CompilerParams(vmem_limit_bytes=VMEM_LIMIT)


SPARE = LANES - SLOTS * RMAX


def row_groups(rows):
    middle = rows - 2 * EDGE * SLOTS
    count = min(n for n in range(middle + 1) if middle - n * SLOTS <= n // 2)
    first = EDGE * SLOTS
    starts = [g * SLOTS for g in range(EDGE + count)] + [rows - (EDGE - g) * SLOTS for g in range(EDGE)]
    left_over = [(first + count * SLOTS + i, EDGE + 2 * i) for i in range(max(0, middle - count * SLOTS))]
    return starts, left_over


def tables_kernel(sides, rows, order_ref, dec_ref, inner_ref, outer_ref, *offset_refs):
    cols = dec_ref.shape[2]
    dec = lax.axis_index("dec")

    def offsets(offset_ref, used, offset):
        offset_ref[...] = jnp.where(used, offset, 2 * LANES).astype(F32)

    def grid(ref):
        return [lax.broadcasted_iota(jnp.int32, ref.shape, d) for d in (0, 1)]

    z, y = grid(offset_refs[0])
    before, after = z - cols - RMAX, z
    if sides == 1:
        column = jnp.where(z < cols, z, jnp.where(dec == 0, after, before))
    else:
        column = jnp.where(z < cols, z, jnp.where(z < cols + RMAX, before, after - RMAX))
    offsets(offset_refs[0], z < cols + sides * RMAX, column - y)
    out, source = grid(offset_refs[1])
    edge = out - (offset_refs[1].shape[0] - 2 * HALO)
    row = jnp.where(edge < 0, out + RMAX, jnp.where(edge < HALO, edge, edge - HALO + rows - RMAX))
    offsets(offset_refs[1], source < rows, source - row)
    out, source = grid(offset_refs[2])
    row = jnp.where(out < HALO, out, out - HALO + rows - RMAX)
    tail = source - HALO
    offsets(
        offset_refs[2], (source < RMAX) | ((tail >= 0) & (tail < RMAX)), jnp.where(tail < 0, source - RMAX, tail + rows) - row
    )
    line = (lax.broadcasted_iota(jnp.int32, (8, LANES), 1) - RMAX).astype(F32)

    def one_radius(index, carry):
        radius = jnp.full((8, LANES), index, jnp.int32).astype(F32)
        spread = 0.5 * radius
        scale = -1.0 / (2.0 * spread * spread)
        raw = jnp.where(jnp.abs(line) <= radius, jnp.exp(line * line * scale), 0.0)
        inverse = 1.0 / jnp.sum(raw, axis=1, keepdims=True)
        limit, scale, inverse = radius[:1, :1], scale[:1, :1], inverse[:1]
        for ref, offset_ref in zip((dec_ref, inner_ref, outer_ref), offset_refs):
            offset = offset_ref[...]
            taps = jnp.where(jnp.abs(offset) <= limit, jnp.exp(offset * offset * scale) * inverse, 0.0)
            ref[index] = taps.astype(BF16)
        return carry

    lax.fori_loop(1, RMAX + 1, one_radius, 0)


def tables(rows, cols, sides, order):
    own = -(-rows // 16) * 16
    inner = -(-(rows - 2 * RMAX) // 16) * 16
    shapes = [(cols + LANES, cols), (inner + 2 * HALO, own), (2 * HALO, 2 * HALO)]
    return pl.pallas_call(
        functools.partial(tables_kernel, sides, rows),
        out_shape=[pltpu.VMEM((RMAX + 1, *shape), BF16) for shape in shapes],
        in_specs=[pl.BlockSpec(memory_space=pl.ANY)],
        out_specs=[VMEM] * 3,
        scratch_shapes=[pltpu.VMEM(shape, F32) for shape in shapes],
        compiler_params=PARAMS,
        cost_estimate=pl.CostEstimate(flops=10**5, bytes_accessed=10**5, transcendentals=0),
    )(order)


def edges_kernel(sides, rad_ref, source_ref, *refs):
    (over_ref, up_ref, up_rest_ref, down_ref, down_rest_ref), refs = refs[:5], refs[5:]
    edge_refs, refs = refs[:3 * sides], refs[3 * sides:]
    x_ref, low_wide, high_wide, low_packed, high_packed, low_rest, high_rest, sems = refs
    rows, chans, cols = x_ref.shape
    pitch = chans + PAD
    cap, full = up_ref.shape[0], RMAX * chans
    spans = ((0, RMAX), (rows - RMAX, RMAX), (RMAX, rows - 2 * RMAX))
    copies = [
        pltpu.make_async_copy(source_ref.at[pl.ds(start, n)], x_ref.at[pl.ds(start, n)], sems.at[i])
        for i, (start, n) in enumerate(spans)
    ]
    for copy in copies:
        copy.start()
    low_packed[...] = jnp.zeros_like(low_packed)
    high_packed[...] = jnp.zeros_like(high_packed)
    for copy in copies[:2]:
        copy.wait()
    for i in range(RMAX):
        low_wide[pl.ds(i * pitch, chans), :] = x_ref[i].astype(F32)
        high_wide[pl.ds(i * pitch, chans), :] = x_ref[rows - RMAX + i].astype(F32)

    total = 0
    for c in range(chans):
        total = total + rad_ref[c]

    def both_ways(i, carry):
        start, stop = carry
        c = chans - 1 - i
        low_packed[pl.ds(HALO + start, RMAX), :] = low_wide[pl.ds(i, RMAX, stride=pitch), :]
        high_packed[pl.ds(HALO + stop - RMAX, RMAX), :] = high_wide[pl.ds(c, RMAX, stride=pitch), :]
        return start + rad_ref[i], stop - rad_ref[c]

    lax.fori_loop(0, chans, both_ways, (0, total), unroll=16)
    rests = []
    for i, (packed, ref, rest, rest_ref) in enumerate((
        (low_packed, down_ref, low_rest, down_rest_ref), (high_packed, up_ref, high_rest, up_rest_ref)
    )):
        ref[...] = packed[HALO:HALO + cap, :].astype(BF16)
        rest[...] = packed[HALO + cap:HALO + full, :].astype(BF16)
        rests.append(pltpu.make_async_copy(rest, rest_ref, sems.at[3 + i]))
        rests[-1].start()
    over_ref[0] = jnp.where(total > cap, 1, 0)

    copies[2].wait()
    dec = lax.axis_index("dec")
    lane = lax.broadcasted_iota(jnp.int32, (chans, LANES), 1)
    for side in range(sides):
        edge_ref, low_ref, high_ref = edge_refs[3 * side:3 * side + 3]
        if sides == 1:
            first = jnp.where(dec == 0, cols - RMAX, 0)
        else:
            first = cols - RMAX if side == 0 else 0
        starts, left_over = row_groups(rows)

        def moved(row, lane_of_first):
            return pltpu.roll(x_ref[row].astype(F32), lax.rem(lane_of_first - first + 2 * LANES, LANES), 1)

        tiles = []
        for g, start in enumerate(starts):
            packed = moved(start, 0)
            for j in range(1, SLOTS):
                packed = jnp.where(lane < RMAX * j, packed, moved(start + j, RMAX * j))
            for row, tile in left_over:
                if g in (tile, tile + 1):
                    packed = jnp.where(lane < LANES - SPARE, packed, moved(row, LANES - SPARE - SPARE * (g - tile)))
            edge_ref[g] = packed.astype(BF16)
            tiles.append(packed)
        half = chans // 2
        shared = [jnp.where(
            (lane[:half] < LANES // 2) == (part is tiles[EDGE - 1]), part[:half], pltpu.roll(part[half:], LANES // 2, 1)
        ) for part in (tiles[EDGE - 1], tiles[-EDGE])]
        for ref, whole, part in ((low_ref, tiles[:EDGE - 1], shared[0]), (high_ref, tiles[1 - EDGE:], shared[1])):
            for i, tile in enumerate(whole):
                ref[i * chans:(i + 1) * chans, :] = tile.astype(BF16)
            ref[(EDGE - 1) * chans:, :] = part.astype(BF16)
    for copy in rests:
        copy.wait()


def cap_of(chans):
    return RMAX * chans * 5 // 8 // 16 * 16


def edges_of(radii, x, sides):
    rows, chans, cols = x.shape
    full, cap = RMAX * chans, cap_of(chans)
    head, rest = pltpu.VMEM((cap, cols), BF16), jax.ShapeDtypeStruct((full - cap, cols), BF16)
    packed = [pltpu.VMEM((len(row_groups(rows)[0]), chans, LANES), BF16)]
    packed += [pltpu.VMEM(((EDGE - 1) * chans + chans // 2, LANES), BF16)] * 2
    return pl.pallas_call(
        functools.partial(edges_kernel, sides),
        out_shape=[pltpu.SMEM((1,), jnp.int32), head, rest, head, rest] + packed * sides,
        in_specs=[SMEM, HBM],
        out_specs=[SMEM] + [VMEM, HBM] * 2 + [VMEM] * (3 * sides),
        scratch_shapes=[pltpu.VMEM(x.shape, BF16)] + [pltpu.VMEM((RMAX * (chans + PAD), cols), F32)] * 2
        + [pltpu.VMEM((full + 2 * HALO, cols), F32)] * 2
        + [pltpu.VMEM(rest.shape, BF16)] * 2
        + [pltpu.SemaphoreType.DMA((5,))],
        compiler_params=PARAMS,
        cost_estimate=pl.CostEstimate(flops=10**6, bytes_accessed=5 * 10**6, transcendentals=0),
    )(radii, x)


def widen(tiles, j):
    lane = lax.broadcasted_iota(jnp.int32, tiles[0].shape, 1)
    value = None
    for side, part in enumerate(tiles):
        shift = (RMAX * side - RMAX * j) % LANES
        part = part if shift == 0 else pltpu.roll(part, shift, 1)
        value = part if side == 0 else jnp.where(lane < RMAX, value, part)
    return value


def inner_kernel(sides, rad_ref, x_ref, dec_ref, ra_ref, *refs):
    edge_refs, (out_ref, begun, x, own, halo, result, sem) = refs[:sides], refs[sides:]
    rows, chans, cols = x_ref.shape
    load = pltpu.make_async_copy(x_ref, x, sem)
    load.start()
    pitch = chans + PAD
    own_rows, inner = ra_ref.shape[2], rows - 2 * RMAX
    base = ra_ref.shape[1] - 2 * HALO

    starts, left_over = row_groups(rows)
    for g, start in enumerate(starts):
        tiles = [ref[g].astype(F32) for ref in edge_refs]
        for j in range(SLOTS):
            halo[pl.ds((start + j) * pitch, chans), :] = widen(tiles, j)
    lane = lax.broadcasted_iota(jnp.int32, (chans, LANES), 1)
    for row, g in left_over:
        tiles = []
        for ref in edge_refs:
            begin, end = (pltpu.roll(ref[g + i].astype(F32), SPARE * (1 + i), 1) for i in range(2))
            tiles.append(jnp.where(lane < SPARE, begin, end))
        halo[pl.ds(row * pitch, chans), :] = widen(tiles, 0)

    def copy_row(i, carry):
        own[pl.ds(i * pitch, chans), :] = x[i].astype(F32)
        return carry

    load.wait()
    lax.fori_loop(0, rows, copy_row, 0)
    for i in range(rows, own_rows):
        own[pl.ds(i * pitch, chans), :] = jnp.zeros((chans, cols), F32)
        halo[pl.ds(i * pitch, chans), :] = jnp.zeros((chans, cols), F32)

    radii = [rad_ref[c] for c in range(chans)]
    partials = []
    for c, radius in enumerate(radii):
        picked = pl.ds(c, own_rows, stride=pitch)
        lhs = jnp.concatenate([own[picked, :].astype(BF16), halo[picked, :].astype(BF16)], 1)
        partials.append(jnp.dot(lhs, dec_ref[radius], preferred_element_type=F32).astype(BF16))
    for c, (radius, partial) in enumerate(zip(radii, partials)):
        smoothed = jnp.dot(ra_ref[radius], partial, preferred_element_type=F32)
        result[pl.ds(c, inner, stride=pitch), :] = smoothed[:inner]
        begun[pl.ds(c, RMAX, stride=pitch), :] = smoothed[base:base + RMAX]
        begun[pl.ds(RMAX * pitch + c, RMAX, stride=pitch), :] = smoothed[base + HALO:base + HALO + RMAX]

    def store(i, carry):
        out_ref[i] = result[pl.ds(i * pitch, chans), :].astype(BF16)
        return carry

    lax.fori_loop(0, inner, store, 0)


def smooth_inner(radii, x, halos, dec_table, ra_table):
    rows, chans, cols = x.shape
    pitch, own_rows, inner = chans + PAD, ra_table.shape[2], rows - 2 * RMAX
    operands = [x, dec_table, ra_table, *halos]
    return pl.pallas_call(
        functools.partial(inner_kernel, len(halos)),
        out_shape=[
            pltpu.VMEM((inner, chans, cols), BF16),
            pltpu.VMEM((2 * RMAX * pitch, cols), F32),
        ],
        in_specs=[SMEM, HBM] + [VMEM] * (len(operands) - 1),
        out_specs=[VMEM] * 2,
        scratch_shapes=[
            pltpu.VMEM(x.shape, BF16),
            pltpu.VMEM((own_rows * pitch, cols), F32),
            pltpu.VMEM((own_rows * pitch, LANES), F32),
            pltpu.VMEM((inner * pitch, cols), F32),
            pltpu.SemaphoreType.DMA,
        ],
        compiler_params=PARAMS,
        cost_estimate=pl.CostEstimate(flops=1, bytes_accessed=1, transcendentals=0),
    )(radii, *operands)


def outer_kernel(sides, rad_ref, begun, before_ref, before_rest, after_ref, after_rest, dec_ref, ra_ref, *refs):
    corner_refs, (out_ref, corner, before, after, result) = refs[:2 * sides], refs[2 * sides:]
    rows, chans, cols = out_ref.shape
    pitch = chans + PAD

    for part, base in ((0, 0), (1, HALO)):
        starts = [g * SLOTS if part else g * SLOTS + RMAX - EDGE * SLOTS for g in range(EDGE)]
        shared = EDGE - 1 if part else 0
        order = [*range(EDGE - 1), EDGE - 1] if part else [EDGE - 1, *range(EDGE - 1)]
        for g, (start, place) in enumerate(zip(starts, order)):
            tiles = []
            for ref in corner_refs[part::2]:
                tile = ref[place * chans:min(place * chans + chans, ref.shape[0]), :].astype(F32)
                if g == shared:
                    tile = jnp.concatenate([tile, pltpu.roll(tile, LANES // 2, 1)], 0)
                tiles.append(tile)
            for j in range(SLOTS):
                if 0 <= start + j < RMAX:
                    corner[pl.ds((base + start + j) * pitch, chans), :] = widen(tiles, j)
        for row in range(RMAX, HALO):
            corner[pl.ds((base + row) * pitch, chans), :] = jnp.zeros((chans, LANES), F32)

    for packed, parts in ((before, (before_ref, before_rest)), (after, (after_ref, after_rest))):
        packed[:HALO, :] = jnp.zeros((HALO, cols), F32)
        packed[packed.shape[0] - HALO:, :] = jnp.zeros((HALO, cols), F32)
        start = HALO
        for part in parts:
            packed[start:start + part.shape[0], :] = part[...].astype(F32)
            start += part.shape[0]

    radii = [rad_ref[c] for c in range(chans)]
    partials = []
    offset = 0
    for c, radius in enumerate(radii):
        planes = [
            before[pl.ds(HALO - RMAX + offset + radius, HALO), :],
            after[pl.ds(HALO + offset, HALO), :],
        ]
        picked = pl.ds(c, 2 * HALO, stride=pitch)
        lhs = jnp.concatenate([jnp.concatenate(planes, 0).astype(BF16), corner[picked, :].astype(BF16)], 1)
        partials.append(jnp.dot(lhs, dec_ref[radius], preferred_element_type=F32).astype(BF16))
        offset = offset + radius
    for c, (radius, partial) in enumerate(zip(radii, partials)):
        smoothed = jnp.dot(ra_ref[radius], partial, preferred_element_type=F32)
        result[pl.ds(c, RMAX, stride=pitch), :] = smoothed[:RMAX]
        result[pl.ds(RMAX * pitch + c, RMAX, stride=pitch), :] = smoothed[HALO:HALO + RMAX]

    def store(i, carry):
        picked = pl.ds(i * pitch, chans)
        out_ref[i] = (begun[picked, :] + result[picked, :]).astype(BF16)
        return carry

    lax.fori_loop(0, rows, store, 0)


def smooth_outer(radii, begun, before, after, dec_table, ra_table, corners):
    chans, cols = radii.shape[0], begun.shape[1]
    pitch = chans + PAD
    operands = [begun, *before, *after, dec_table, ra_table] + [part for side in corners for part in side]
    return pl.pallas_call(
        functools.partial(outer_kernel, len(corners)),
        out_shape=pltpu.VMEM((2 * RMAX, chans, cols), BF16),
        in_specs=[SMEM] + [VMEM] * len(operands),
        out_specs=VMEM,
        scratch_shapes=[
            pltpu.VMEM((2 * HALO * pitch, LANES), F32),
            pltpu.VMEM((RMAX * chans + 2 * HALO, cols), F32),
            pltpu.VMEM((RMAX * chans + 2 * HALO, cols), F32),
            pltpu.VMEM((2 * RMAX * pitch, cols), F32),
        ],
        compiler_params=PARAMS,
        cost_estimate=pl.CostEstimate(flops=10000000000, bytes_accessed=5 * 10**6, transcendentals=0),
    )(radii, *operands)


SUM_ROWS = 8


def add_products(total, own_ref, other_ref, valid_ref, first_row, rows):
    chans = own_ref.shape[1]
    depth = max(d for d in range(1, 27) if rows % d == 0)

    def nt(a, b):
        return lax.dot_general(a, b, (((1,), (1,)), ((), ())), preferred_element_type=F32)

    def body(i, carry):
        picked = [i * depth + j for j in range(depth)]
        line = jnp.concatenate([valid_ref[pl.ds(first_row(r), 1), :].astype(BF16) for r in picked], 1)
        own, other = (jnp.concatenate([ref[r] for r in picked], 1) for ref in (own_ref, other_ref))
        both = jnp.concatenate([own, other], 0)
        total[:2 * chans, :] += nt(both, own * line)
        total[2 * chans:, :] += nt(jnp.broadcast_to(line, (16, line.shape[1])), own)[:SUM_ROWS]
        return carry

    lax.fori_loop(0, rows // depth, body, 0)


def inner_gram_kernel(own_ref, other_ref, valid_ref, total_ref):
    total_ref[...] = jnp.zeros_like(total_ref)
    add_products(total_ref, own_ref, other_ref, valid_ref, lambda r: r + RMAX, own_ref.shape[0])


def inner_gram(own, other, valid):
    chans = own.shape[1]
    return pl.pallas_call(
        inner_gram_kernel,
        out_shape=pltpu.VMEM((2 * chans + SUM_ROWS, chans), F32),
        in_specs=[VMEM] * 3,
        out_specs=VMEM,
        compiler_params=PARAMS,
        cost_estimate=pl.CostEstimate(flops=10**9, bytes_accessed=3 * 10**6, transcendentals=0),
    )(own, other, valid)


def gram_kernel(inner_ref, own_ref, other_ref, valid_ref, inner_own_ref, out_ref, smoothed_ref, total, sems):
    rows, chans = valid_ref.shape[0], own_ref.shape[1]
    half = chans // 2
    band = lax.axis_index("band")
    copies = [
        pltpu.make_async_copy(source, smoothed_ref.at[pl.ds(start, source.shape[0])], sems.at[i])
        for i, (source, start) in enumerate((
            (inner_own_ref, RMAX),
            (own_ref.at[pl.ds(0, RMAX)], 0),
            (own_ref.at[pl.ds(RMAX, RMAX)], rows - RMAX),
        ))
    ]
    for copy in copies:
        copy.start()
    total[...] = inner_ref[...]
    add_products(
        total, own_ref, other_ref, valid_ref, lambda r: jnp.where(r < RMAX, r, r + rows - 2 * RMAX), 2 * RMAX
    )
    low = pltpu.roll(total[half:chans, :], half, 1)
    row = lax.broadcasted_iota(jnp.int32, (half, chans), 0)
    lane = lax.broadcasted_iota(jnp.int32, (half, chans), 1)
    out_ref[:half, :] = jnp.where(lane < row, low, total[:half, :])
    cross = total[chans:2 * chans, :]
    out_ref[half:chans, :] = jnp.where(band == 0, cross[:half], jnp.transpose(cross)[half:])
    diagonal = jnp.sum(jnp.where(lane == row, low, 0.0), axis=0, keepdims=True)
    row = lax.broadcasted_iota(jnp.int32, (SUM_ROWS, chans), 0)
    tail = jnp.where(row == 1, diagonal, total[2 * chans:, :])
    out_ref[chans:, :] = jnp.where(row == 2, jnp.sum(valid_ref[...].astype(F32)), tail)
    for copy in copies:
        copy.wait()


def gram(inner, own, other, valid, inner_own):
    _, chans, cols = own.shape
    return pl.pallas_call(
        gram_kernel,
        out_shape=[
            pltpu.VMEM((chans + SUM_ROWS, chans), F32),
            jax.ShapeDtypeStruct((valid.shape[0], chans, cols), BF16),
        ],
        in_specs=[VMEM] * 5,
        out_specs=[VMEM, pl.BlockSpec(memory_space=pl.ANY)],
        scratch_shapes=[pltpu.VMEM(inner.shape, F32), pltpu.SemaphoreType.DMA((3,))],
        compiler_params=PARAMS,
    )(inner, own, other, valid, inner_own)


def finish_kernel(mine_ref, theirs_ref, mean_ref, cov_ref):
    chans = mine_ref.shape[1]
    half = chans // 2
    band = lax.axis_index("band")
    count = mine_ref[chans + 2:chans + 3, :1]
    folded = mine_ref[:half, :]
    mirror = jnp.transpose(jnp.concatenate([folded, jnp.zeros((half, chans), F32)], 0))
    row = lax.broadcasted_iota(jnp.int32, (half, chans), 0)
    lane = lax.broadcasted_iota(jnp.int32, (half, chans), 1)
    upper = jnp.where(lane < row, mirror[:half], folded)
    column = lane - half
    corner = jnp.where(column < row, pltpu.roll(folded, half, 1), pltpu.roll(mirror[:half], half, 1))
    corner = jnp.where(column == row, pltpu.roll(mine_ref[chans:chans + SUM_ROWS, :], half, 1)[1:2, :], corner)
    own = jnp.concatenate([upper, jnp.where(column < 0, mirror[half:], corner)], 0)
    mine, theirs = mine_ref[half:chans, :], theirs_ref[half:chans, :]
    cross = jnp.concatenate([jnp.where(band == 0, mine, theirs), jnp.where(band == 0, theirs, mine)], 0)
    cross = jnp.where(band == 0, cross, jnp.transpose(cross))
    mean = mine_ref[chans:chans + 1, :] / count
    other_mean = theirs_ref[chans:chans + 1, :] / count
    mean_ref[...] = mean
    for block, left, b in ((own, mean, band), (cross, other_mean, 1 - band)):
        left = jnp.transpose(jnp.broadcast_to(left, (chans, chans)))
        cov_ref[pl.ds(pl.multiple_of(b * chans, chans), chans), :] = (block - count * left * mean) / (count - 1.0)


def finish(mine, theirs):
    chans = mine.shape[1]
    mean, covariance = pl.pallas_call(
        finish_kernel,
        out_shape=[jax.ShapeDtypeStruct((1, chans), F32), jax.ShapeDtypeStruct((2 * chans, chans), F32)],
        in_specs=[VMEM] * 2,
        out_specs=[VMEM] * 2,
        compiler_params=PARAMS,
    )(mine, theirs)
    return mean.reshape(chans), covariance


def swap(array, axis, step):
    size = lax.axis_size(axis)
    return lax.ppermute(array, axis, [(i, i ^ step) for i in range(size)])


def diagonal(array, ra_step, dec_pairs):
    ra_size, dec_size = lax.axis_size("ra"), lax.axis_size("dec")
    pairs = [
        (i * dec_size + a, (i + ra_step) % ra_size * dec_size + b) for i in range(ra_size) for a, b in dec_pairs
    ]
    return lax.ppermute(array, ("ra", "dec"), pairs)


def per_device(sky_maps, radii, valid):
    x = jnp.transpose(sky_maps, (1, 0, 2))
    radii = pltpu.with_memory_space_constraint(radii, pltpu.HBM)
    x = pltpu.with_memory_space_constraint(x, pltpu.HBM)
    rows, chans, cols = x.shape
    ra_size, dec_size = lax.axis_size("ra"), lax.axis_size("dec")
    up = [(i, (i + 1) % ra_size) for i in range(ra_size)]
    down = [(j, i) for i, j in up]
    right = [(i, i + 1) for i in range(dec_size - 1)]
    left = [(j, i) for i, j in right]
    sides = [right + left] if dec_size == 2 else [right, left]
    over, up_head, up_rest, down_head, down_rest, *packed = edges_of(radii, x, len(sides))
    before_rest, after_rest = lax.switch(
        over[0],
        [lambda a, b: (a, b), lambda a, b: (lax.ppermute(a, "ra", up), lax.ppermute(b, "ra", down))],
        up_rest, down_rest,
    )
    before, after = lax.ppermute(up_head, "ra", up), lax.ppermute(down_head, "ra", down)
    packed = [packed[3 * i:3 * i + 3] for i in range(len(sides))]
    halos = [lax.ppermute(p, "dec", pairs) for (p, _, _), pairs in zip(packed, sides)]
    corners = [
        (diagonal(high, 1, pairs), diagonal(low, -1, pairs)) for (_, low, high), pairs in zip(packed, sides)
    ]
    dec_table, inner_table, outer_table = tables(rows, cols, len(sides), before_rest)
    inner, begun = smooth_inner(radii, x, halos, dec_table, inner_table)
    outer = smooth_outer(
        radii, begun, (before, before_rest), (after, after_rest), dec_table, outer_table, corners
    )
    inner_total = inner_gram(inner, swap(inner, "band", 1), valid)
    total, smoothed = gram(inner_total, outer, swap(outer, "band", 1), valid, inner)
    steps = [("dec", 1 << b) for b in range(dec_size.bit_length() - 1)]
    steps += [("ra", 1 << b) for b in range(ra_size.bit_length() - 1)]
    for axis, step in steps:
        total = total + swap(total, axis, step)
    mean, covariance = finish(total, swap(total, "band", 1))
    return (jnp.transpose(smoothed, (1, 0, 2)), mean, covariance)


def solution(mesh):
    return jax.shard_map(
        per_device,
        mesh=mesh,
        in_specs=(
            P(("groups", "band"), "ra", "dec"),
            P(("groups", "band")),
            P(("groups", "ra"), "dec"),
        ),
        out_specs=(P(("groups", "band"), "ra", "dec"), P(("groups", "band")), P("groups", "band")),
        check_vma=False,
    )
```

time: 64 us -> 55.5 us (0.87)
  local copies, waits for them, and re-layouts: 3.79 us -> 0.01 us
  waiting for transfers between devices: 20.3 us -> 16.7 us
  Pallas kernels: 20.9 us -> 21.9 us
  starting transfers between devices: 16.7 us -> 16 us
  between operations: 1.4 us -> 0.74 us
  other arithmetic: 0.67 us -> 0.03 us
    ppermute x1, waiting for transfers between devices: 4.72 us -> 0.01 us  [per_device(): lax.ppermute(down_head, 'ra', down)]
    unnamed x16 -> x2, local copies, waits for them, and re-layouts: 3.11 us -> 0.01 us
    ppermute x2, waiting for transfers between devices: 0.54 us -> 3.57 us  [diagonal(): return lax.ppermute(array, ('ra', 'dec'), pairs)]
    ppermute x1, starting transfers between devices: 3.89 us -> 2.25 us  [per_device(): lax.ppermute(down_head, 'ra', down)]
    ppermute x5 -> x6, waiting for transfers between devices: 14.2 us -> 13.1 us  [swap(): return lax.ppermute(array, axis, [(i, i ^ step) for i in range(size)])]
    ppermute x2, starting transfers between devices: 3.59 us -> 4.72 us  [diagonal(): return lax.ppermute(array, ('ra', 'dec'), pairs)]
    pallas_call x1, Pallas kernels: 6.38 us -> 7.45 us  [smooth_inner(): pl.pallas_call(functools.partial(inner_kernel, len(halos)), out_shape=[pl...]
    ppermute x5 -> x6, starting transfers between devices: 5.31 us -> 4.44 us  [swap(): return lax.ppermute(array, axis, [(i, i ^ step) for i in range(size)])]
  transfers between devices with their start and end apart: 10 -> 11, of which waited for: 8 -> 7; matrix products, arithmetic and copies ran while one was open for 2% -> 0% of each run, Pallas kernels for 25% -> 28%
where the time goes in v4:
time: 55.5 us; the launch traced here: 55.3 us
  Pallas kernels  21.9 us (39%)
  waiting for transfers between devices  16.7 us (30%)
  starting transfers between devices  16 us (29%)
  between operations  0.74 us (1%)
    ppermute x6, waiting for transfers between devices, swap(): return lax.ppermute(array, axis, [(i, i ^ step) for i in range(size)])  13.1 us
    pallas_call x1, Pallas kernels, smooth_inner(): pl.pallas_call(functools.partial(inner_kernel, len(halos)), out_shape=[pl...  7.45 us
    ppermute x2, starting transfers between devices, diagonal(): return lax.ppermute(array, ('ra', 'dec'), pairs)  4.72 us
    ppermute x6, starting transfers between devices, swap(): return lax.ppermute(array, axis, [(i, i ^ step) for i in range(size)])  4.44 us
    pallas_call x1, Pallas kernels, smooth_outer(): pl.pallas_call(functools.partial(outer_kernel, len(corners)), out_shape=p...  4.23 us
    pallas_call x1, Pallas kernels, edges_of(): pl.pallas_call(functools.partial(edges_kernel, sides), out_shape=[pltpu.S...  4.16 us
    ppermute x2, waiting for transfers between devices, diagonal(): return lax.ppermute(array, ('ra', 'dec'), pairs)  3.57 us
    ppermute x1, starting transfers between devices, per_device(): lax.ppermute(p, 'dec', pairs)  3 us
  transfers between devices with their start and end apart: 11, of which 7 were waited for; matrix products, arithmetic and copies ran while one was open for 0% of the time, Pallas kernels for 28%

profile of v4, /device:TPU:0, one launch (start us, length us, event | category | flops | bytes accessed | tf_op | source)
XLA Modules:
  0.0 55.3 jit_solution(8434498235453353960)
XLA Ops:
  0.6 4.2 %shard_map.58 = (s32[1]{0:T(128)S(4)}, bf16[1360,128]{1,0:T(8,128)(2,1)S(1)}, bf16[816,128]{1,0:T(8,128)(2,1)S(1)}, bf16[1360,128]{1,0:T(8,128)(2,1)S(1)}, bf16[...) custom-call(s32[128]{0:T(128)} %rad_ref.5, ...), custom_call_target="tpu_custom_call" | custom-call | flops 1000000 | bytes 5000000 | tf_op jit(solution)/shard_map/pallas_call | solution.py:186
  4.8 3.0 %collective-permute-start.2 = (bf16[11,128,128]{2,1,0:T(8,128)(2,1)S(1)}, bf16[11,128,128]{2,1,0:T(8,128)(2,1)S(1)}, u32[]{:S(2)}, u32[]{:S(2)}) collective-permute-start(bf16[11,128,128]{2,1,0:T(8,128)(2,1)S(1)} %get-tuple-element.38), channel_id=1, source_target_pairs={{0,2},{2,0},{1,3},{3,1},{4,6},{6,4},{5,7},{7,5},{8,10},{10,8},{9,1... | collective-permute-start | bytes 1081352 | tf_op jit(solution)/shard_map/ppermute | solution.py:515
  7.8 1.6 %collective-permute-start.4 = (bf16[1360,128]{1,0:T(8,128)(2,1)S(1)}, bf16[1360,128]{1,0:T(8,128)(2,1)S(1)}, u32[]{:S(2)}, u32[]{:S(2)}) collective-permute-start(bf16[1360,128]{1,0:T(8,128)(2,1)S(1)} %get-tuple-element.41), channel_id=1, source_target_pairs={{0,4},{4,8},{8,12},{12,0},{1,5},{5,9},{9,13},{13,1},{2,6},{6,10},{... | collective-permute-start | bytes 1044488 | tf_op jit(solution)/shard_map/ppermute | solution.py:513
  9.4 2.2 %collective-permute-start.5 = (bf16[1360,128]{1,0:T(8,128)(2,1)S(1)}, bf16[1360,128]{1,0:T(8,128)(2,1)S(1)}, u32[]{:S(2)}, u32[]{:S(2)}) collective-permute-start(bf16[1360,128]{1,0:T(8,128)(2,1)S(1)} %get-tuple-element.42), channel_id=1, source_target_pairs={{4,0},{8,4},{12,8},{0,12},{5,1},{9,5},{13,9},{1,13},{6,2},{10,6},{... | collective-permute-start | bytes 1044488 | tf_op jit(solution)/shard_map/ppermute | solution.py:513
  11.6 4.7 %collective-permute-start.7 = (bf16[320,128]{1,0:T(8,128)(2,1)S(1)}, bf16[320,128]{1,0:T(8,128)(2,1)S(1)}, u32[]{:S(2)}, u32[]{:S(2)}) collective-permute-start(bf16[320,128]{1,0:T(8,128)(2,1)S(1)} %get-tuple-element.46), channel_id=1, source_target_pairs={{0,14},{2,12},{4,2},{6,0},{8,6},{10,4},{12,10},{14,8},{1,15},{3,13... | collective-permute-start | bytes 245768 | tf_op jit(solution)/shard_map/ppermute | solution.py:493
  16.4 2.2 %shard_map.59 = (bf16[18,256,128]{2,1,0:T(8,128)(2,1)S(1)}, bf16[18,96,80]{2,1,0:T(8,128)(2,1)S(1)}, bf16[18,48,48]{2,1,0:T(8,128)(2,1)S(1)}) custom-call(bf16[816,128]{1,0:T(8,128)(2,1)S(1)} %get-tuple-element.35.order_ref.before_rest), custom_call_target="tpu_custom_call" | custom-call | flops 100000 | bytes 100000 | tf_op jit(solution)/shard_map/pallas_call | solution.py:85
  18.5 7.4 %shard_map.60 = (bf16[44,128,128]{2,1,0:T(8,128)(2,1)S(1)}, f32[4624,128]{1,0:T(8,128)S(1)}) custom-call(s32[128]{0:T(128)} %rad_ref.5, bf16[78,128,128]{2,1,0:T(8,128)(2,1)} %bitcast.5, bf16[18,256,128]{2,1,0:T(8,128)(2,1)S(1)} %get-tuple-element.36.dec_ref, bf16[18,96,80]{2,1,0:T(8,128)(2,1)S(1)} %get-tuple-element.37.ra_ref, ...), custom_call_target="tpu_custom_call" | custom-call | flops 1 | bytes 1 | tf_op jit(solution)/shard_map/pallas_call | solution.py:265
  26.0 0.1 collective-permute-start.3
  26.1 3.4 %collective-permute-done.6.refs_0_ = bf16[320,128]{1,0:T(8,128)(2,1)S(1)} collective-permute-done((bf16[320,128]{1,0:T(8,128)(2,1)S(1)}, bf16[320,128]{1,0:T(8,128)(2,1)S(1)}, u32[]{:S(2)}, u32[]{:S(2)}) %collective-permute-start.6) | collective-permute-done | bytes 81952 | tf_op jit(solution)/shard_map/ppermute | solution.py:493
  29.5 0.2 collective-permute-done.7.refs_1_
  29.7 4.2 %shard_map.62.own_ref = bf16[34,128,128]{2,1,0:T(8,128)(2,1)S(1)} custom-call(s32[128]{0:T(128)} %rad_ref.5, f32[4624,128]{1,0:T(8,128)S(1)} %get-tuple-element.40.begun, bf16[1360,128]{1,0:T(8,128)(2,1)S(1)} %collective-permute-done.4.before_ref, bf16[816,128]{1,0:T(8,128)(2,1)S(1)} %get-tuple-element.35.order_ref.before_rest, ...), custom_call_target="tpu_custom_call" | custom-call | flops 10000000000 | bytes 5000000 | tf_op jit(solution)/shard_map/pallas_call | solution.py:344
  33.9 0.1 collective-permute-start.8
  34.0 1.4 %shard_map.61.inner_ref = f32[264,128]{1,0:T(8,128)S(1)} custom-call(bf16[44,128,128]{2,1,0:T(8,128)(2,1)S(1)} %get-tuple-element.39.own_ref.inner_own_ref, bf16[44,128,128]{2,1,0:T(8,128)(2,1)S(1)} %collective-permute-done.3.other_ref, s32[78,128]{1,0:T(8,128)S(1)} %copy-done), custom_call_target="tpu_custom_call" | custom-call | flops 1000000000 | bytes 3000000 | tf_op jit(solution)/shard_map/pallas_call | solution.py:389
  35.4 1.3 %collective-permute-done.8.other_ref = bf16[34,128,128]{2,1,0:T(8,128)(2,1)S(1)} collective-permute-done((bf16[34,128,128]{2,1,0:T(8,128)(2,1)S(1)}, bf16[34,128,128]{2,1,0:T(8,128)(2,1)S(1)}, u32[]{:S(2)}, u32[]{:S(2)}) %collective-permute-start.8) | collective-permute-done | bytes 1114144 | tf_op jit(solution)/shard_map/ppermute | solution.py:485
  36.7 1.5 %shard_map.63 = (f32[136,128]{1,0:T(8,128)S(1)}, bf16[78,128,128]{2,1,0:T(8,128)(2,1)}) custom-call(f32[264,128]{1,0:T(8,128)S(1)} %shard_map.61.inner_ref, bf16[34,128,128]{2,1,0:T(8,128)(2,1)S(1)} %shard_map.62.own_ref, bf16[34,128,128]{2,1,0:T(8,128)(2,1)S(1)} %collective-permute-done.8.other_ref, s32[78,128]{1,0:T(8,128)S(1)} %copy-done, ...), custom_call_target="tpu_custom_call" | custom-call | tf_op jit(solution)/shard_map/pallas_call | solution.py:433
  38.2 1.6 %collective-permute-start.9 = (f32[136,128]{1,0:T(8,128)S(1)}, f32[136,128]{1,0:T(8,128)S(1)}, u32[]{:S(2)}, u32[]{:S(2)}) collective-permute-start(f32[136,128]{1,0:T(8,128)S(1)} %get-tuple-element.48), channel_id=1, source_target_pairs={{0,2},{2,0},{1,3},{3,1},{4,6},{6,4},{5,7},{7,5},{8,10},{10,8},{9,1... | collective-permute-start | bytes 208904 | tf_op jit(solution)/shard_map/ppermute | solution.py:485
  39.8 2.8 %collective-permute-done.9 = f32[136,128]{1,0:T(8,128)S(1)} collective-permute-done((f32[136,128]{1,0:T(8,128)S(1)}, f32[136,128]{1,0:T(8,128)S(1)}, u32[]{:S(2)}, u32[]{:S(2)}) %collective-permute-start.9) | collective-permute-done | bytes 69664 | tf_op jit(solution)/shard_map/ppermute | solution.py:485
  42.6 1.2 %collective-permute-start.10 = (f32[136,128]{1,0:T(8,128)S(1)}, f32[136,128]{1,0:T(8,128)S(1)}, u32[]{:S(2)}, u32[]{:S(2)}) collective-permute-start(f32[136,128]{1,0:T(8,128)S(1)} %add.9), channel_id=1, source_target_pairs={{0,4},{4,0},{8,12},{12,8},{1,5},{5,1},{9,13},{13,9},{2,6},{6,2},{1... | collective-permute-start | bytes 208904 | tf_op jit(solution)/shard_map/ppermute | solution.py:485
  43.8 3.2 %collective-permute-done.10 = f32[136,128]{1,0:T(8,128)S(1)} collective-permute-done((f32[136,128]{1,0:T(8,128)S(1)}, f32[136,128]{1,0:T(8,128)S(1)}, u32[]{:S(2)}, u32[]{:S(2)}) %collective-permute-start.10) | collective-permute-done | bytes 69664 | tf_op jit(solution)/shard_map/ppermute | solution.py:485
  47.0 1.5 %collective-permute-start.11 = (f32[136,128]{1,0:T(8,128)S(1)}, f32[136,128]{1,0:T(8,128)S(1)}, u32[]{:S(2)}, u32[]{:S(2)}) collective-permute-start(f32[136,128]{1,0:T(8,128)S(1)} %add.10), channel_id=1, source_target_pairs={{0,8},{4,12},{8,0},{12,4},{1,9},{5,13},{9,1},{13,5},{2,10},{6,14},... | collective-permute-start | bytes 208904 | tf_op jit(solution)/shard_map/ppermute | solution.py:485
  48.5 4.5 %collective-permute-done.11 = f32[136,128]{1,0:T(8,128)S(1)} collective-permute-done((f32[136,128]{1,0:T(8,128)S(1)}, f32[136,128]{1,0:T(8,128)S(1)}, u32[]{:S(2)}, u32[]{:S(2)}) %collective-permute-start.11) | collective-permute-done | bytes 69664 | tf_op jit(solution)/shard_map/ppermute | solution.py:485
  53.0 0.1 collective-permute-start.12
  53.1 1.2 %collective-permute-done.12.theirs_ref = f32[136,128]{1,0:T(8,128)S(1)} collective-permute-done((f32[136,128]{1,0:T(8,128)S(1)}, f32[136,128]{1,0:T(8,128)S(1)}, u32[]{:S(2)}, u32[]{:S(2)}) %collective-permute-start.12) | collective-permute-done | bytes 69664 | tf_op jit(solution)/shard_map/ppermute | solution.py:485
  54.3 0.9 %shard_map.64 = (f32[1,128]{1,0:T(1,128)}, f32[256,128]{1,0:T(8,128)}) custom-call(f32[136,128]{1,0:T(8,128)S(1)} %add.11.mine_ref, f32[136,128]{1,0:T(8,128)S(1)} %collective-permute-done.12.theirs_ref), custom_call_target="tpu_custom_call" | custom-call | tf_op jit(solution)/shard_map/pallas_call | solution.py:473
  (11 shorter events, 0.0 us)
Async XLA Ops:
  4.8 13.7 %collective-permute-start.2 = (bf16[11,128,128]{2,1,0:T(8,128)(2,1)S(1)}, bf16[11,128,128]{2,1,0:T(8,128)(2,1)S(1)}, u32[]{:S(2)}, u32[]{:S(2)}) collective-permute-start(bf16[11,128,128]{2,1,0:T(8,128)(2,1)S(1)} %get-tuple-element.38), channel_id=1, source_target_pairs={{0,2},{2,0},{1,3},{3,1},{4,6},{6,4},{5,7},{7,5},{8,10},{10,8},{9,1... | collective-permute-start | bytes 1081352 | tf_op jit(solution)/shard_map/ppermute | solution.py:515
  7.8 21.9 %collective-permute-start.4 = (bf16[1360,128]{1,0:T(8,128)(2,1)S(1)}, bf16[1360,128]{1,0:T(8,128)(2,1)S(1)}, u32[]{:S(2)}, u32[]{:S(2)}) collective-permute-start(bf16[1360,128]{1,0:T(8,128)(2,1)S(1)} %get-tuple-element.41), channel_id=1, source_target_pairs={{0,4},{4,8},{8,12},{12,0},{1,5},{5,9},{9,13},{13,1},{2,6},{6,10},{... | collective-permute-start | bytes 1044488 | tf_op jit(solution)/shard_map/ppermute | solution.py:513
  9.4 20.3 %collective-permute-start.5 = (bf16[1360,128]{1,0:T(8,128)(2,1)S(1)}, bf16[1360,128]{1,0:T(8,128)(2,1)S(1)}, u32[]{:S(2)}, u32[]{:S(2)}) collective-permute-start(bf16[1360,128]{1,0:T(8,128)(2,1)S(1)} %get-tuple-element.42), channel_id=1, source_target_pairs={{4,0},{8,4},{12,8},{0,12},{5,1},{9,5},{13,9},{1,13},{6,2},{10,6},{... | collective-permute-start | bytes 1044488 | tf_op jit(solution)/shard_map/ppermute | solution.py:513
  11.6 17.9 %collective-permute-start.6 = (bf16[320,128]{1,0:T(8,128)(2,1)S(1)}, bf16[320,128]{1,0:T(8,128)(2,1)S(1)}, u32[]{:S(2)}, u32[]{:S(2)}) collective-permute-start(bf16[320,128]{1,0:T(8,128)(2,1)S(1)} %get-tuple-element.45), channel_id=1, source_target_pairs={{0,6},{2,4},{4,10},{6,8},{8,14},{10,12},{12,2},{14,0},{1,7},{3,5},... | collective-permute-start | bytes 245768 | tf_op jit(solution)/shard_map/ppermute | solution.py:493
  11.6 18.0 %collective-permute-start.7 = (bf16[320,128]{1,0:T(8,128)(2,1)S(1)}, bf16[320,128]{1,0:T(8,128)(2,1)S(1)}, u32[]{:S(2)}, u32[]{:S(2)}) collective-permute-start(bf16[320,128]{1,0:T(8,128)(2,1)S(1)} %get-tuple-element.46), channel_id=1, source_target_pairs={{0,14},{2,12},{4,2},{6,0},{8,6},{10,4},{12,10},{14,8},{1,15},{3,13... | collective-permute-start | bytes 245768 | tf_op jit(solution)/shard_map/ppermute | solution.py:493
  26.0 8.0 %collective-permute-start.3 = (bf16[44,128,128]{2,1,0:T(8,128)(2,1)S(1)}, bf16[44,128,128]{2,1,0:T(8,128)(2,1)S(1)}, u32[]{:S(2)}, u32[]{:S(2)}) collective-permute-start(bf16[44,128,128]{2,1,0:T(8,128)(2,1)S(1)} %get-tuple-element.39.own_ref.inner_own_ref), channel_id=1, source_target_pairs={{0,1},{1,0},{2,3},{3,2},{4,5},{5,4},{6,7},{7,6},{8,9},{9,8},{10,11... | collective-permute-start | bytes 4325384 | tf_op jit(solution)/shard_map/ppermute | solution.py:485
  29.7 4.3 %copy-start = (s32[78,128]{1,0:T(8,128)S(1)}, s32[78,128]{1,0:T(8,128)}, u32[]{:S(2)}) copy-start(s32[78,128]{1,0:T(8,128)} %valid_ref.3) | copy-start | bytes 119812
  33.9 2.8 %collective-permute-start.8 = (bf16[34,128,128]{2,1,0:T(8,128)(2,1)S(1)}, bf16[34,128,128]{2,1,0:T(8,128)(2,1)S(1)}, u32[]{:S(2)}, u32[]{:S(2)}) collective-permute-start(bf16[34,128,128]{2,1,0:T(8,128)(2,1)S(1)} %shard_map.62.own_ref), channel_id=1, source_target_pairs={{0,1},{1,0},{2,3},{3,2},{4,5},{5,4},{6,7},{7,6},{8,9},{9,8},{10,11... | collective-permute-start | bytes 3342344 | tf_op jit(solution)/shard_map/ppermute | solution.py:485
  38.2 4.4 %collective-permute-start.9 = (f32[136,128]{1,0:T(8,128)S(1)}, f32[136,128]{1,0:T(8,128)S(1)}, u32[]{:S(2)}, u32[]{:S(2)}) collective-permute-start(f32[136,128]{1,0:T(8,128)S(1)} %get-tuple-element.48), channel_id=1, source_target_pairs={{0,2},{2,0},{1,3},{3,1},{4,6},{6,4},{5,7},{7,5},{8,10},{10,8},{9,1... | collective-permute-start | bytes 208904 | tf_op jit(solution)/shard_map/ppermute | solution.py:485
  42.6 4.4 %collective-permute-start.10 = (f32[136,128]{1,0:T(8,128)S(1)}, f32[136,128]{1,0:T(8,128)S(1)}, u32[]{:S(2)}, u32[]{:S(2)}) collective-permute-start(f32[136,128]{1,0:T(8,128)S(1)} %add.9), channel_id=1, source_target_pairs={{0,4},{4,0},{8,12},{12,8},{1,5},{5,1},{9,13},{13,9},{2,6},{6,2},{1... | collective-permute-start | bytes 208904 | tf_op jit(solution)/shard_map/ppermute | solution.py:485
  47.0 6.0 %collective-permute-start.11 = (f32[136,128]{1,0:T(8,128)S(1)}, f32[136,128]{1,0:T(8,128)S(1)}, u32[]{:S(2)}, u32[]{:S(2)}) collective-permute-start(f32[136,128]{1,0:T(8,128)S(1)} %add.10), channel_id=1, source_target_pairs={{0,8},{4,12},{8,0},{12,4},{1,9},{5,13},{9,1},{13,5},{2,10},{6,14},... | collective-permute-start | bytes 208904 | tf_op jit(solution)/shard_map/ppermute | solution.py:485
  53.0 1.3 %collective-permute-start.12 = (f32[136,128]{1,0:T(8,128)S(1)}, f32[136,128]{1,0:T(8,128)S(1)}, u32[]{:S(2)}, u32[]{:S(2)}) collective-permute-start(f32[136,128]{1,0:T(8,128)S(1)} %add.11.mine_ref), channel_id=1, source_target_pairs={{0,1},{1,0},{2,3},{3,2},{4,5},{5,4},{6,7},{7,6},{8,9},{9,8},{10,11... | collective-permute-start | bytes 208904 | tf_op jit(solution)/shard_map/ppermute | solution.py:485

commit v5 on v4

--- a/solution.py
+++ b/solution.py
@@ -26,11 +26,12 @@
 
 def row_groups(rows):
     middle = rows - 2 * EDGE * SLOTS
-    count = min(n for n in range(middle + 1) if middle - n * SLOTS <= n // 2)
-    first = EDGE * SLOTS
+    small = LANES // 2 // RMAX
+    count = min(n for n in range(middle + 1) if middle - n * SLOTS <= (2 * EDGE + n) // 2 + small)
     starts = [g * SLOTS for g in range(EDGE + count)] + [rows - (EDGE - g) * SLOTS for g in range(EDGE)]
-    left_over = [(first + count * SLOTS + i, EDGE + 2 * i) for i in range(max(0, middle - count * SLOTS))]
-    return starts, left_over
+    rest = list(range((EDGE + count) * SLOTS, rows - EDGE * SLOTS))
+    left_over = [(row, 2 * i) for i, row in enumerate(rest[small:])]
+    return starts, left_over, rest[:small]
 
 
 def tables_kernel(sides, rows, order_ref, dec_ref, inner_ref, outer_ref, *offset_refs):
@@ -107,8 +108,6 @@
     ]
     for copy in copies:
         copy.start()
-    low_packed[...] = jnp.zeros_like(low_packed)
-    high_packed[...] = jnp.zeros_like(high_packed)
     for copy in copies[:2]:
         copy.wait()
     for i in range(RMAX):
@@ -131,10 +130,17 @@
     for i, (packed, ref, rest, rest_ref) in enumerate((
         (low_packed, down_ref, low_rest, down_rest_ref), (high_packed, up_ref, high_rest, up_rest_ref)
     )):
+        packed[pl.ds(HALO + total, HALO), :] = jnp.zeros((HALO, cols), F32)
         ref[...] = packed[HALO:HALO + cap, :].astype(BF16)
-        rest[...] = packed[HALO + cap:HALO + full, :].astype(BF16)
         rests.append(pltpu.make_async_copy(rest, rest_ref, sems.at[3 + i]))
-        rests[-1].start()
+
+    @pl.when(total > cap)
+    def _():
+        for packed, rest, copy in ((low_packed, low_rest, rests[0]), (high_packed, high_rest, rests[1])):
+            rest[...] = packed[HALO + cap:HALO + full, :].astype(BF16)
+            copy.start()
+            copy.wait()
+
     over_ref[0] = jnp.where(total > cap, 1, 0)
 
     copies[2].wait()
@@ -146,7 +152,7 @@
             first = jnp.where(dec == 0, cols - RMAX, 0)
         else:
             first = cols - RMAX if side == 0 else 0
-        starts, left_over = row_groups(rows)
+        starts, left_over, shared = row_groups(rows)
 
         def moved(row, lane_of_first):
             return pltpu.roll(x_ref[row].astype(F32), lax.rem(lane_of_first - first + 2 * LANES, LANES), 1)
@@ -159,18 +165,24 @@
             for row, tile in left_over:
                 if g in (tile, tile + 1):
                     packed = jnp.where(lane < LANES - SPARE, packed, moved(row, LANES - SPARE - SPARE * (g - tile)))
-            edge_ref[g] = packed.astype(BF16)
+            edge_ref[g * chans:(g + 1) * chans, :] = packed.astype(BF16)
             tiles.append(packed)
         half = chans // 2
-        shared = [jnp.where(
-            (lane[:half] < LANES // 2) == (part is tiles[EDGE - 1]), part[:half], pltpu.roll(part[half:], LANES // 2, 1)
-        ) for part in (tiles[EDGE - 1], tiles[-EDGE])]
-        for ref, whole, part in ((low_ref, tiles[:EDGE - 1], shared[0]), (high_ref, tiles[1 - EDGE:], shared[1])):
+
+        def beside(part, low):
+            return jnp.where((lane[:half] < LANES // 2) == low, part[:half], pltpu.roll(part[half:], LANES // 2, 1))
+
+        packed = jnp.zeros((chans, LANES), F32)
+        for j, row in enumerate(shared):
+            packed = jnp.where(lane < RMAX * j, packed, moved(row, RMAX * j))
+        edge_ref[len(starts) * chans:, :] = beside(packed, True).astype(BF16)
+        for ref, whole, part in (
+            (low_ref, tiles[:EDGE - 1], beside(tiles[EDGE - 1], True)),
+            (high_ref, tiles[1 - EDGE:], beside(tiles[-EDGE], False)),
+        ):
             for i, tile in enumerate(whole):
                 ref[i * chans:(i + 1) * chans, :] = tile.astype(BF16)
             ref[(EDGE - 1) * chans:, :] = part.astype(BF16)
-    for copy in rests:
-        copy.wait()
 
 
 def cap_of(chans):
@@ -181,14 +193,14 @@
     rows, chans, cols = x.shape
     full, cap = RMAX * chans, cap_of(chans)
     head, rest = pltpu.VMEM((cap, cols), BF16), jax.ShapeDtypeStruct((full - cap, cols), BF16)
-    packed = [pltpu.VMEM((len(row_groups(rows)[0]), chans, LANES), BF16)]
+    packed = [pltpu.VMEM((len(row_groups(rows)[0]) * chans + chans // 2, LANES), BF16)]
     packed += [pltpu.VMEM(((EDGE - 1) * chans + chans // 2, LANES), BF16)] * 2
     return pl.pallas_call(
         functools.partial(edges_kernel, sides),
         out_shape=[pltpu.SMEM((1,), jnp.int32), head, rest, head, rest] + packed * sides,
         in_specs=[SMEM, HBM],
         out_specs=[SMEM] + [VMEM, HBM] * 2 + [VMEM] * (3 * sides),
-        scratch_shapes=[pltpu.VMEM(x.shape, BF16)] + [pltpu.VMEM((RMAX * (chans + PAD), cols), F32)] * 2
+        scratch_shapes=[pltpu.VMEM(x.shape, BF16)] + [pltpu.VMEM(((RMAX + 1) * (chans + PAD), cols), F32)] * 2
         + [pltpu.VMEM((full + 2 * HALO, cols), F32)] * 2
         + [pltpu.VMEM(rest.shape, BF16)] * 2
         + [pltpu.SemaphoreType.DMA((5,))],
@@ -216,18 +228,24 @@
     own_rows, inner = ra_ref.shape[2], rows - 2 * RMAX
     base = ra_ref.shape[1] - 2 * HALO
 
-    starts, left_over = row_groups(rows)
+    starts, left_over, shared = row_groups(rows)
     for g, start in enumerate(starts):
-        tiles = [ref[g].astype(F32) for ref in edge_refs]
+        tiles = [ref[g * chans:(g + 1) * chans, :].astype(F32) for ref in edge_refs]
         for j in range(SLOTS):
             halo[pl.ds((start + j) * pitch, chans), :] = widen(tiles, j)
     lane = lax.broadcasted_iota(jnp.int32, (chans, LANES), 1)
     for row, g in left_over:
         tiles = []
         for ref in edge_refs:
-            begin, end = (pltpu.roll(ref[g + i].astype(F32), SPARE * (1 + i), 1) for i in range(2))
+            begin, end = (
+                pltpu.roll(ref[(g + i) * chans:(g + i + 1) * chans, :].astype(F32), SPARE * (1 + i), 1) for i in range(2)
+            )
             tiles.append(jnp.where(lane < SPARE, begin, end))
         halo[pl.ds(row * pitch, chans), :] = widen(tiles, 0)
+    tiles = [ref[len(starts) * chans:, :].astype(F32) for ref in edge_refs]
+    tiles = [jnp.concatenate([tile, pltpu.roll(tile, LANES // 2, 1)], 0) for tile in tiles]
+    for j, row in enumerate(shared):
+        halo[pl.ds(row * pitch, chans), :] = widen(tiles, j)
 
     def copy_row(i, carry):
         own[pl.ds(i * pitch, chans), :] = x[i].astype(F32)
@@ -266,15 +284,15 @@
         functools.partial(inner_kernel, len(halos)),
         out_shape=[
             pltpu.VMEM((inner, chans, cols), BF16),
-            pltpu.VMEM((2 * RMAX * pitch, cols), F32),
+            pltpu.VMEM(((2 * RMAX + 1) * pitch, cols), F32),
         ],
         in_specs=[SMEM, HBM] + [VMEM] * (len(operands) - 1),
         out_specs=[VMEM] * 2,
         scratch_shapes=[
             pltpu.VMEM(x.shape, BF16),
-            pltpu.VMEM((own_rows * pitch, cols), F32),
-            pltpu.VMEM((own_rows * pitch, LANES), F32),
-            pltpu.VMEM((inner * pitch, cols), F32),
+            pltpu.VMEM(((own_rows + 1) * pitch, cols), F32),
+            pltpu.VMEM(((own_rows + 1) * pitch, LANES), F32),
+            pltpu.VMEM(((inner + 1) * pitch, cols), F32),
             pltpu.SemaphoreType.DMA,
         ],
         compiler_params=PARAMS,
@@ -282,10 +300,55 @@
     )(radii, *operands)
 
 
-def outer_kernel(sides, rad_ref, begun, before_ref, before_rest, after_ref, after_rest, dec_ref, ra_ref, *refs):
-    corner_refs, (out_ref, corner, before, after, result) = refs[:2 * sides], refs[2 * sides:]
+def reach_lanes(sides):
+    return -(-sides * RMAX // 16) * 16
+
+
+def outer_begin_kernel(rad_ref, order_ref, before_ref, before_rest, after_ref, after_rest, dec_ref, begun, before, after):
+    chans, _, cols = begun.shape
+    radii = [rad_ref[c] for c in range(chans)]
+    total = functools.reduce(lambda a, b: a + b, radii)
+    cap = before_ref.shape[0]
+    for packed, head, rest in ((before, before_ref, before_rest), (after, after_ref, after_rest)):
+        packed[:HALO, :] = jnp.zeros((HALO, cols), F32)
+        packed[HALO:HALO + cap, :] = head[...].astype(F32)
+        packed[HALO + cap:2 * HALO + cap, :] = jnp.zeros((HALO, cols), F32)
+        packed[packed.shape[0] - HALO:, :] = jnp.zeros((HALO, cols), F32)
+
+        @pl.when(total > cap)
+        def _():
+            packed[HALO + cap:HALO + cap + rest.shape[0], :] = rest[...].astype(F32)
+
+    offset = 0
+    for c, radius in enumerate(radii):
+        planes = [
+            before[pl.ds(HALO - RMAX + offset + radius, HALO), :],
+            after[pl.ds(HALO + offset, HALO), :],
+        ]
+        lhs = jnp.concatenate(planes, 0).astype(BF16)
+        begun[c] = jnp.dot(lhs, dec_ref[radius, :cols, :], preferred_element_type=F32)
+        offset = offset + radius
+
+
+def outer_begin(radii, order, before, after, dec_table):
+    chans, cols = radii.shape[0], dec_table.shape[2]
+    operands = [*before, *after, dec_table]
+    return pl.pallas_call(
+        outer_begin_kernel,
+        out_shape=pltpu.VMEM((chans, 2 * HALO, cols), F32),
+        in_specs=[SMEM, pl.BlockSpec(memory_space=pl.ANY)] + [VMEM] * len(operands),
+        out_specs=VMEM,
+        scratch_shapes=[pltpu.VMEM((RMAX * chans + 2 * HALO, cols), F32)] * 2,
+        compiler_params=PARAMS,
+        cost_estimate=pl.CostEstimate(flops=2 * 10**9, bytes_accessed=5 * 10**6, transcendentals=0),
+    )(radii, order, *operands)
+
+
+def outer_kernel(sides, rad_ref, dec_begun, ra_begun, dec_ref, ra_ref, *refs):
+    corner_refs, (out_ref, corner, result) = refs[:2 * sides], refs[2 * sides:]
     rows, chans, cols = out_ref.shape
     pitch = chans + PAD
+    width = reach_lanes(sides)
 
     for part, base in ((0, 0), (1, HALO)):
         starts = [g * SLOTS if part else g * SLOTS + RMAX - EDGE * SLOTS for g in range(EDGE)]
@@ -304,26 +367,12 @@
         for row in range(RMAX, HALO):
             corner[pl.ds((base + row) * pitch, chans), :] = jnp.zeros((chans, LANES), F32)
 
-    for packed, parts in ((before, (before_ref, before_rest)), (after, (after_ref, after_rest))):
-        packed[:HALO, :] = jnp.zeros((HALO, cols), F32)
-        packed[packed.shape[0] - HALO:, :] = jnp.zeros((HALO, cols), F32)
-        start = HALO
-        for part in parts:
-            packed[start:start + part.shape[0], :] = part[...].astype(F32)
-            start += part.shape[0]
-
     radii = [rad_ref[c] for c in range(chans)]
     partials = []
-    offset = 0
     for c, radius in enumerate(radii):
-        planes = [
-            before[pl.ds(HALO - RMAX + offset + radius, HALO), :],
-            after[pl.ds(HALO + offset, HALO), :],
-        ]
-        picked = pl.ds(c, 2 * HALO, stride=pitch)
-        lhs = jnp.concatenate([jnp.concatenate(planes, 0).astype(BF16), corner[picked, :].astype(BF16)], 1)
-        partials.append(jnp.dot(lhs, dec_ref[radius], preferred_element_type=F32).astype(BF16))
-        offset = offset + radius
+        lhs = corner[pl.ds(c, 2 * HALO, stride=pitch), :].astype(BF16)[:, :width]
+        partial = jnp.dot(lhs, dec_ref[radius, cols:cols + width, :], preferred_element_type=F32) + dec_begun[c]
+        partials.append(partial.astype(BF16))
     for c, (radius, partial) in enumerate(zip(radii, partials)):
         smoothed = jnp.dot(ra_ref[radius], partial, preferred_element_type=F32)
         result[pl.ds(c, RMAX, stride=pitch), :] = smoothed[:RMAX]
@@ -331,37 +380,34 @@
 
     def store(i, carry):
         picked = pl.ds(i * pitch, chans)
-        out_ref[i] = (begun[picked, :] + result[picked, :]).astype(BF16)
+        out_ref[i] = (ra_begun[picked, :] + result[picked, :]).astype(BF16)
         return carry
 
     lax.fori_loop(0, rows, store, 0)
 
 
-def smooth_outer(radii, begun, before, after, dec_table, ra_table, corners):
-    chans, cols = radii.shape[0], begun.shape[1]
+def smooth_outer(radii, dec_begun, ra_begun, dec_table, ra_table, corners):
+    chans, _, cols = dec_begun.shape
     pitch = chans + PAD
-    operands = [begun, *before, *after, dec_table, ra_table] + [part for side in corners for part in side]
+    operands = [dec_begun, ra_begun, dec_table, ra_table] + [part for side in corners for part in side]
     return pl.pallas_call(
         functools.partial(outer_kernel, len(corners)),
         out_shape=pltpu.VMEM((2 * RMAX, chans, cols), BF16),
         in_specs=[SMEM] + [VMEM] * len(operands),
         out_specs=VMEM,
         scratch_shapes=[
-            pltpu.VMEM((2 * HALO * pitch, LANES), F32),
-            pltpu.VMEM((RMAX * chans + 2 * HALO, cols), F32),
-            pltpu.VMEM((RMAX * chans + 2 * HALO, cols), F32),
-            pltpu.VMEM((2 * RMAX * pitch, cols), F32),
+            pltpu.VMEM(((2 * HALO + 1) * pitch, LANES), F32),
+            pltpu.VMEM(((2 * RMAX + 1) * pitch, cols), F32),
         ],
         compiler_params=PARAMS,
-        cost_estimate=pl.CostEstimate(flops=10000000000, bytes_accessed=5 * 10**6, transcendentals=0),
+        cost_estimate=pl.CostEstimate(flops=10**10, bytes_accessed=5 * 10**6, transcendentals=0),
     )(radii, *operands)
 
 
 SUM_ROWS = 8
 
 
-def add_products(total, own_ref, other_ref, valid_ref, first_row, rows):
-    chans = own_ref.shape[1]
+def add_products(total, row_refs, own_ref, valid_ref, first_row, rows, sums=None):
     depth = max(d for d in range(1, 27) if rows % d == 0)
 
     def nt(a, b):
@@ -370,77 +416,87 @@
     def body(i, carry):
         picked = [i * depth + j for j in range(depth)]
         line = jnp.concatenate([valid_ref[pl.ds(first_row(r), 1), :].astype(BF16) for r in picked], 1)
-        own, other = (jnp.concatenate([ref[r] for r in picked], 1) for ref in (own_ref, other_ref))
-        both = jnp.concatenate([own, other], 0)
-        total[:2 * chans, :] += nt(both, own * line)
-        total[2 * chans:, :] += nt(jnp.broadcast_to(line, (16, line.shape[1])), own)[:SUM_ROWS]
+        own, *others = (jnp.concatenate([ref[r] for r in picked], 1) for ref in (own_ref, *row_refs))
+        total[...] += nt(jnp.concatenate(others, 0), own * line)
+        if sums is not None:
+            sums[...] += nt(jnp.broadcast_to(line, (16, line.shape[1])), own)[:SUM_ROWS]
         return carry
 
     lax.fori_loop(0, rows // depth, body, 0)
 
 
-def inner_gram_kernel(own_ref, other_ref, valid_ref, total_ref):
-    total_ref[...] = jnp.zeros_like(total_ref)
-    add_products(total_ref, own_ref, other_ref, valid_ref, lambda r: r + RMAX, own_ref.shape[0])
-
-
-def inner_gram(own, other, valid):
-    chans = own.shape[1]
-    return pl.pallas_call(
-        inner_gram_kernel,
-        out_shape=pltpu.VMEM((2 * chans + SUM_ROWS, chans), F32),
-        in_specs=[VMEM] * 3,
-        out_specs=VMEM,
-        compiler_params=PARAMS,
-        cost_estimate=pl.CostEstimate(flops=10**9, bytes_accessed=3 * 10**6, transcendentals=0),
-    )(own, other, valid)
-
-
-def gram_kernel(inner_ref, own_ref, other_ref, valid_ref, inner_own_ref, out_ref, smoothed_ref, total, sems):
+def outer_row(image_rows):
+    return lambda r: jnp.where(r < RMAX, r, r + image_rows - 2 * RMAX)
+
+
+def own_gram_kernel(own_ref, other_ref, outer_ref, valid_ref, out_ref, cross_ref, smoothed_ref, both, sems):
     rows, chans = valid_ref.shape[0], own_ref.shape[1]
     half = chans // 2
-    band = lax.axis_index("band")
     copies = [
         pltpu.make_async_copy(source, smoothed_ref.at[pl.ds(start, source.shape[0])], sems.at[i])
         for i, (source, start) in enumerate((
-            (inner_own_ref, RMAX),
-            (own_ref.at[pl.ds(0, RMAX)], 0),
-            (own_ref.at[pl.ds(RMAX, RMAX)], rows - RMAX),
+            (own_ref, RMAX),
+            (outer_ref.at[pl.ds(0, RMAX)], 0),
+            (outer_ref.at[pl.ds(RMAX, RMAX)], rows - RMAX),
         ))
     ]
     for copy in copies:
         copy.start()
-    total[...] = inner_ref[...]
-    add_products(
-        total, own_ref, other_ref, valid_ref, lambda r: jnp.where(r < RMAX, r, r + rows - 2 * RMAX), 2 * RMAX
-    )
-    low = pltpu.roll(total[half:chans, :], half, 1)
+    both[...] = jnp.zeros_like(both)
+    products, own, sums = both.at[:2 * chans], both.at[:chans], both.at[2 * chans:]
+    add_products(products, (own_ref, other_ref), own_ref, valid_ref, lambda r: r + RMAX, own_ref.shape[0], sums)
+    add_products(own, (outer_ref,), outer_ref, valid_ref, outer_row(rows), 2 * RMAX, sums)
+    cross_ref[...] = both[chans:2 * chans, :]
+    low = pltpu.roll(both[half:chans, :], half, 1)
     row = lax.broadcasted_iota(jnp.int32, (half, chans), 0)
     lane = lax.broadcasted_iota(jnp.int32, (half, chans), 1)
-    out_ref[:half, :] = jnp.where(lane < row, low, total[:half, :])
-    cross = total[chans:2 * chans, :]
-    out_ref[half:chans, :] = jnp.where(band == 0, cross[:half], jnp.transpose(cross)[half:])
+    out_ref[:half, :] = jnp.where(lane < row, low, both[:half, :])
     diagonal = jnp.sum(jnp.where(lane == row, low, 0.0), axis=0, keepdims=True)
     row = lax.broadcasted_iota(jnp.int32, (SUM_ROWS, chans), 0)
-    tail = jnp.where(row == 1, diagonal, total[2 * chans:, :])
-    out_ref[chans:, :] = jnp.where(row == 2, jnp.sum(valid_ref[...].astype(F32)), tail)
+    tail = jnp.where(row == 1, diagonal, both[2 * chans:, :])
+    out_ref[half:, :] = jnp.where(row == 2, jnp.sum(valid_ref[...].astype(F32)), tail)
     for copy in copies:
         copy.wait()
 
 
-def gram(inner, own, other, valid, inner_own):
+def own_gram(own, other, outer, valid):
     _, chans, cols = own.shape
     return pl.pallas_call(
-        gram_kernel,
+        own_gram_kernel,
         out_shape=[
-            pltpu.VMEM((chans + SUM_ROWS, chans), F32),
+            pltpu.VMEM((chans // 2 + SUM_ROWS, chans), F32),
+            pltpu.VMEM((chans, chans), F32),
             jax.ShapeDtypeStruct((valid.shape[0], chans, cols), BF16),
         ],
+        in_specs=[VMEM] * 4,
+        out_specs=[VMEM, VMEM, HBM],
+        scratch_shapes=[pltpu.VMEM((2 * chans + SUM_ROWS, chans), F32), pltpu.SemaphoreType.DMA((3,))],
+        compiler_params=PARAMS,
+        cost_estimate=pl.CostEstimate(flops=10**9, bytes_accessed=3 * 10**6, transcendentals=0),
+    )(own, other, outer, valid)
+
+
+def cross_gram_kernel(folded_ref, cross_ref, own_ref, other_ref, valid_ref, out_ref, total):
+    chans = own_ref.shape[1]
+    half = chans // 2
+    total[...] = cross_ref[...]
+    add_products(total, (other_ref,), own_ref, valid_ref, outer_row(valid_ref.shape[0]), 2 * RMAX)
+    cross = total[...]
+    out_ref[:half, :] = folded_ref[:half, :]
+    out_ref[half:chans, :] = jnp.where(lax.axis_index("band") == 0, cross[:half], jnp.transpose(cross)[half:])
+    out_ref[chans:, :] = folded_ref[half:, :]
+
+
+def cross_gram(folded, cross, own, other, valid):
+    chans = own.shape[1]
+    return pl.pallas_call(
+        cross_gram_kernel,
+        out_shape=pltpu.VMEM((chans + SUM_ROWS, chans), F32),
         in_specs=[VMEM] * 5,
-        out_specs=[VMEM, pl.BlockSpec(memory_space=pl.ANY)],
-        scratch_shapes=[pltpu.VMEM(inner.shape, F32), pltpu.SemaphoreType.DMA((3,))],
-        compiler_params=PARAMS,
-    )(inner, own, other, valid, inner_own)
+        out_specs=VMEM,
+        scratch_shapes=[pltpu.VMEM((chans, chans), F32)],
+        compiler_params=PARAMS,
+    )(folded, cross, own, other, valid)
 
 
 def finish_kernel(mine_ref, theirs_ref, mean_ref, cov_ref):
@@ -518,11 +574,10 @@
     ]
     dec_table, inner_table, outer_table = tables(rows, cols, len(sides), before_rest)
     inner, begun = smooth_inner(radii, x, halos, dec_table, inner_table)
-    outer = smooth_outer(
-        radii, begun, (before, before_rest), (after, after_rest), dec_table, outer_table, corners
-    )
-    inner_total = inner_gram(inner, swap(inner, "band", 1), valid)
-    total, smoothed = gram(inner_total, outer, swap(outer, "band", 1), valid, inner)
+    dec_begun = outer_begin(radii, begun, (before, before_rest), (after, after_rest), dec_table)
+    outer = smooth_outer(radii, dec_begun, begun, dec_table, outer_table, corners)
+    folded, cross, smoothed = own_gram(inner, swap(inner, "band", 1), outer, valid)
+    total = cross_gram(folded, cross, outer, swap(outer, "band", 1), valid)
     steps = [("dec", 1 << b) for b in range(dec_size.bit_length() - 1)]
     steps += [("ra", 1 << b) for b in range(ra_size.bit_length() - 1)]
     for axis, step in steps:

time: 55.5 us -> 53.2 us (0.959)
  waiting for transfers between devices: 16.7 us -> 13.3 us
  Pallas kernels: 21.9 us -> 22.9 us
    ppermute x2, waiting for transfers between devices: 3.57 us -> 0.06 us  [diagonal(): return lax.ppermute(array, ('ra', 'dec'), pairs)]
    pallas_call x2 -> x3, Pallas kernels: 2.92 us -> 5.39 us  [the longest x1 2.51 us: own_gram(): pl.pallas_call(own_gram_kernel, out_shape=[pltpu.VMEM((chans // 2 + SUM_R...]
    ppermute x1, starting transfers between devices: 1.58 us -> 3.08 us  [per_device(): lax.ppermute(up_head, 'ra', up)]
    ppermute x1, starting transfers between devices: 3 us -> 1.65 us  [per_device(): lax.ppermute(p, 'dec', pairs)]
    pallas_call x1, Pallas kernels: 4.23 us -> 3.19 us  [smooth_outer(): pl.pallas_call(functools.partial(outer_kernel, len(corners)), out_shape=p...]
    ppermute x1, waiting for transfers between devices: 0.01 us -> 0.97 us  [per_device(): lax.ppermute(p, 'dec', pairs)]
    ppermute x6, waiting for transfers between devices: 13.1 us -> 12.2 us  [swap(): return lax.ppermute(array, axis, [(i, i ^ step) for i in range(size)])]
  transfers between devices with their start and end apart: 11 -> 11, of which waited for: 7 -> 6; matrix products, arithmetic and copies ran while one was open for 0% -> 0% of each run, Pallas kernels for 28% -> 33%
where the time goes in v5:
time: 53.2 us; the launch traced here: 52.9 us
  Pallas kernels  22.9 us (43%)
  starting transfers between devices  16 us (30%)
  waiting for transfers between devices  13.3 us (25%)
  between operations  0.75 us (1%)
    ppermute x6, waiting for transfers between devices, swap(): return lax.ppermute(array, axis, [(i, i ^ step) for i in range(size)])  12.2 us
    pallas_call x1, Pallas kernels, smooth_inner(): pl.pallas_call(functools.partial(inner_kernel, len(halos)), out_shape=[pl...  7.59 us
    ppermute x2, starting transfers between devices, diagonal(): return lax.ppermute(array, ('ra', 'dec'), pairs)  4.72 us
    ppermute x6, starting transfers between devices, swap(): return lax.ppermute(array, axis, [(i, i ^ step) for i in range(size)])  4.46 us
    pallas_call x1, Pallas kernels, edges_of(): pl.pallas_call(functools.partial(edges_kernel, sides), out_shape=[pltpu.S...  3.62 us
    pallas_call x1, Pallas kernels, smooth_outer(): pl.pallas_call(functools.partial(outer_kernel, len(corners)), out_shape=p...  3.19 us
    ppermute x1, starting transfers between devices, per_device(): lax.ppermute(up_head, 'ra', up)  3.08 us
    pallas_call x1, Pallas kernels, own_gram(): pl.pallas_call(own_gram_kernel, out_shape=[pltpu.VMEM((chans // 2 + SUM_R...  2.51 us
  transfers between devices with their start and end apart: 11, of which 6 were waited for; matrix products, arithmetic and copies ran while one was open for 0% of the time, Pallas kernels for 33%

profile of v5, /device:TPU:0, one launch (start us, length us, event | category | flops | bytes accessed | tf_op | source)
XLA Modules:
  0.0 52.9 jit_solution(11600598578997088078)
XLA Ops:
  0.6 3.6 %shard_map.58 = (s32[1]{0:T(128)S(4)}, bf16[1360,128]{1,0:T(8,128)(2,1)S(1)}, bf16[816,128]{1,0:T(8,128)(2,1)S(1)}, bf16[1360,128]{1,0:T(8,128)(2,1)S(1)}, bf16[...) custom-call(s32[128]{0:T(128)} %rad_ref.7, ...), custom_call_target="tpu_custom_call" | custom-call | flops 1000000 | bytes 5000000 | tf_op jit(solution)/shard_map/pallas_call | solution.py:198
  4.3 3.1 %collective-permute-start.4 = (bf16[1360,128]{1,0:T(8,128)(2,1)S(1)}, bf16[1360,128]{1,0:T(8,128)(2,1)S(1)}, u32[]{:S(2)}, u32[]{:S(2)}) collective-permute-start(bf16[1360,128]{1,0:T(8,128)(2,1)S(1)} %get-tuple-element.42), channel_id=1, source_target_pairs={{0,4},{4,8},{8,12},{12,0},{1,5},{5,9},{9,13},{13,1},{2,6},{6,10},{... | collective-permute-start | bytes 1044488 | tf_op jit(solution)/shard_map/ppermute | solution.py:569
  7.3 2.1 %collective-permute-start.5 = (bf16[1360,128]{1,0:T(8,128)(2,1)S(1)}, bf16[1360,128]{1,0:T(8,128)(2,1)S(1)}, u32[]{:S(2)}, u32[]{:S(2)}) collective-permute-start(bf16[1360,128]{1,0:T(8,128)(2,1)S(1)} %get-tuple-element.43), channel_id=1, source_target_pairs={{4,0},{8,4},{12,8},{0,12},{5,1},{9,5},{13,9},{1,13},{6,2},{10,6},{... | collective-permute-start | bytes 1044488 | tf_op jit(solution)/shard_map/ppermute | solution.py:569
  9.4 1.6 %collective-permute-start.2 = (bf16[1344,128]{1,0:T(8,128)(2,1)S(1)}, bf16[1344,128]{1,0:T(8,128)(2,1)S(1)}, u32[]{:S(2)}, u32[]{:S(2)}) collective-permute-start(bf16[1344,128]{1,0:T(8,128)(2,1)S(1)} %get-tuple-element.39), channel_id=1, source_target_pairs={{0,2},{2,0},{1,3},{3,1},{4,6},{6,4},{5,7},{7,5},{8,10},{10,8},{9,1... | collective-permute-start | bytes 1032200 | tf_op jit(solution)/shard_map/ppermute | solution.py:571
  11.1 4.7 %collective-permute-start.7 = (bf16[320,128]{1,0:T(8,128)(2,1)S(1)}, bf16[320,128]{1,0:T(8,128)(2,1)S(1)}, u32[]{:S(2)}, u32[]{:S(2)}) collective-permute-start(bf16[320,128]{1,0:T(8,128)(2,1)S(1)} %get-tuple-element.47), channel_id=1, source_target_pairs={{0,14},{2,12},{4,2},{6,0},{8,6},{10,4},{12,10},{14,8},{1,15},{3,13... | collective-permute-start | bytes 245768 | tf_op jit(solution)/shard_map/ppermute | solution.py:549
  15.8 2.2 %shard_map.59 = (bf16[18,256,128]{2,1,0:T(8,128)(2,1)S(1)}, bf16[18,96,80]{2,1,0:T(8,128)(2,1)S(1)}, bf16[18,48,48]{2,1,0:T(8,128)(2,1)S(1)}) custom-call(bf16[816,128]{1,0:T(8,128)(2,1)S(1)} %get-tuple-element.36.order_ref.before_rest), custom_call_target="tpu_custom_call" | custom-call | flops 100000 | bytes 100000 | tf_op jit(solution)/shard_map/pallas_call | solution.py:86
  18.0 1.0 %collective-permute-done.2.refs_0_ = bf16[1344,128]{1,0:T(8,128)(2,1)S(1)} collective-permute-done((bf16[1344,128]{1,0:T(8,128)(2,1)S(1)}, bf16[1344,128]{1,0:T(8,128)(2,1)S(1)}, u32[]{:S(2)}, u32[]{:S(2)}) %collective-permute-start.2) | collective-permute-done | bytes 344096 | tf_op jit(solution)/shard_map/ppermute | solution.py:571
  18.9 7.6 %shard_map.60 = (bf16[44,128,128]{2,1,0:T(8,128)(2,1)S(1)}, f32[4760,128]{1,0:T(8,128)S(1)}) custom-call(s32[128]{0:T(128)} %rad_ref.7, bf16[78,128,128]{2,1,0:T(8,128)(2,1)} %bitcast.5, bf16[18,256,128]{2,1,0:T(8,128)(2,1)S(1)} %get-tuple-element.37.dec_ref, bf16[18,96,80]{2,1,0:T(8,128)(2,1)S(1)} %get-tuple-element.38.ra_ref, ...), custom_call_target="tpu_custom_call" | custom-call | flops 1 | bytes 1 | tf_op jit(solution)/shard_map/pallas_call | solution.py:283
  26.5 0.1 collective-permute-start.3
  26.6 2.1 %shard_map.61.dec_begun = f32[128,48,128]{2,1,0:T(8,128)S(1)} custom-call(s32[128]{0:T(128)} %rad_ref.7, f32[4760,128]{1,0:T(8,128)S(1)} %get-tuple-element.41.order_ref.ra_begun, bf16[1360,128]{1,0:T(8,128)(2,1)S(1)} %collective-permute-done.4.before_ref, bf16[816,128]{1,0:T(8,128)(2,1)S(1)} %get-tuple-element.36.order_ref.before_rest, ...), custom_call_target="tpu_custom_call" | custom-call | flops 2000000000 | bytes 5000000 | tf_op jit(solution)/shard_map/pallas_call | solution.py:336
  28.8 0.1 collective-permute-done.7.refs_1_
  28.8 3.2 %shard_map.62.outer_ref.own_ref = bf16[34,128,128]{2,1,0:T(8,128)(2,1)S(1)} custom-call(s32[128]{0:T(128)} %rad_ref.7, f32[128,48,128]{2,1,0:T(8,128)S(1)} %shard_map.61.dec_begun, f32[4760,128]{1,0:T(8,128)S(1)} %get-tuple-element.41.order_ref.ra_begun, bf16[18,256,128]{2,1,0:T(8,128)(2,1)S(1)} %get-tuple-element.37.dec_ref, ...), custom_call_target="tpu_custom_call" | custom-call | flops 10000000000 | bytes 5000000 | tf_op jit(solution)/shard_map/pallas_call | solution.py:393
  32.0 0.5 collective-permute-start.8
  32.6 2.5 %shard_map.63 = (f32[72,128]{1,0:T(8,128)S(1)}, f32[128,128]{1,0:T(8,128)S(1)}, bf16[78,128,128]{2,1,0:T(8,128)(2,1)}) custom-call(bf16[44,128,128]{2,1,0:T(8,128)(2,1)S(1)} %get-tuple-element.40.own_ref, bf16[44,128,128]{2,1,0:T(8,128)(2,1)S(1)} %collective-permute-done.3.other_ref, bf16[34,128,128]{2,1,0:T(8,128)(2,1)S(1)} %shard_map.62.outer_ref.own_ref, ...), custom_call_target="tpu_custom_call" | custom-call | flops 1000000000 | bytes 3000000 | tf_op jit(solution)/shard_map/pallas_call | solution.py:464
  35.1 0.8 %shard_map.64 = f32[136,128]{1,0:T(8,128)S(1)} custom-call(f32[72,128]{1,0:T(8,128)S(1)} %get-tuple-element.49.folded_ref, f32[128,128]{1,0:T(8,128)S(1)} %get-tuple-element.50.cross_ref, bf16[34,128,128]{2,1,0:T(8,128)(2,1)S(1)} %shard_map.62.outer_ref.own_ref, bf16[34,128,128]{2,1,0:T(8,128)(2,1)S(1)} %collective-permute-done.8.other_ref, ...), custom_call_target="tpu_custom_call" | custom-call | tf_op jit(solution)/shard_map/pallas_call | solution.py:492
  35.9 1.6 %collective-permute-start.9 = (f32[136,128]{1,0:T(8,128)S(1)}, f32[136,128]{1,0:T(8,128)S(1)}, u32[]{:S(2)}, u32[]{:S(2)}) collective-permute-start(f32[136,128]{1,0:T(8,128)S(1)} %shard_map.64), channel_id=1, source_target_pairs={{0,2},{2,0},{1,3},{3,1},{4,6},{6,4},{5,7},{7,5},{8,10},{10,8},{9,1... | collective-permute-start | bytes 208904 | tf_op jit(solution)/shard_map/ppermute | solution.py:541
  37.4 2.8 %collective-permute-done.9 = f32[136,128]{1,0:T(8,128)S(1)} collective-permute-done((f32[136,128]{1,0:T(8,128)S(1)}, f32[136,128]{1,0:T(8,128)S(1)}, u32[]{:S(2)}, u32[]{:S(2)}) %collective-permute-start.9) | collective-permute-done | bytes 69664 | tf_op jit(solution)/shard_map/ppermute | solution.py:541
  40.2 1.0 %collective-permute-start.10 = (f32[136,128]{1,0:T(8,128)S(1)}, f32[136,128]{1,0:T(8,128)S(1)}, u32[]{:S(2)}, u32[]{:S(2)}) collective-permute-start(f32[136,128]{1,0:T(8,128)S(1)} %add.9), channel_id=1, source_target_pairs={{0,4},{4,0},{8,12},{12,8},{1,5},{5,1},{9,13},{13,9},{2,6},{6,2},{1... | collective-permute-start | bytes 208904 | tf_op jit(solution)/shard_map/ppermute | solution.py:541
  41.3 3.4 %collective-permute-done.10 = f32[136,128]{1,0:T(8,128)S(1)} collective-permute-done((f32[136,128]{1,0:T(8,128)S(1)}, f32[136,128]{1,0:T(8,128)S(1)}, u32[]{:S(2)}, u32[]{:S(2)}) %collective-permute-start.10) | collective-permute-done | bytes 69664 | tf_op jit(solution)/shard_map/ppermute | solution.py:541
  44.6 1.2 %collective-permute-start.11 = (f32[136,128]{1,0:T(8,128)S(1)}, f32[136,128]{1,0:T(8,128)S(1)}, u32[]{:S(2)}, u32[]{:S(2)}) collective-permute-start(f32[136,128]{1,0:T(8,128)S(1)} %add.10), channel_id=1, source_target_pairs={{0,8},{4,12},{8,0},{12,4},{1,9},{5,13},{9,1},{13,5},{2,10},{6,14},... | collective-permute-start | bytes 208904 | tf_op jit(solution)/shard_map/ppermute | solution.py:541
  45.9 4.8 %collective-permute-done.11 = f32[136,128]{1,0:T(8,128)S(1)} collective-permute-done((f32[136,128]{1,0:T(8,128)S(1)}, f32[136,128]{1,0:T(8,128)S(1)}, u32[]{:S(2)}, u32[]{:S(2)}) %collective-permute-start.11) | collective-permute-done | bytes 69664 | tf_op jit(solution)/shard_map/ppermute | solution.py:541
  50.7 0.1 collective-permute-start.12
  50.7 1.2 %collective-permute-done.12.theirs_ref = f32[136,128]{1,0:T(8,128)S(1)} collective-permute-done((f32[136,128]{1,0:T(8,128)S(1)}, f32[136,128]{1,0:T(8,128)S(1)}, u32[]{:S(2)}, u32[]{:S(2)}) %collective-permute-start.12) | collective-permute-done | bytes 69664 | tf_op jit(solution)/shard_map/ppermute | solution.py:541
  52.0 0.9 %shard_map.65 = (f32[1,128]{1,0:T(1,128)}, f32[256,128]{1,0:T(8,128)}) custom-call(f32[136,128]{1,0:T(8,128)S(1)} %add.11.mine_ref, f32[136,128]{1,0:T(8,128)S(1)} %collective-permute-done.12.theirs_ref), custom_call_target="tpu_custom_call" | custom-call | tf_op jit(solution)/shard_map/pallas_call | solution.py:529
  (12 shorter events, 0.0 us)
Async XLA Ops:
  4.3 22.4 %collective-permute-start.4 = (bf16[1360,128]{1,0:T(8,128)(2,1)S(1)}, bf16[1360,128]{1,0:T(8,128)(2,1)S(1)}, u32[]{:S(2)}, u32[]{:S(2)}) collective-permute-start(bf16[1360,128]{1,0:T(8,128)(2,1)S(1)} %get-tuple-element.42), channel_id=1, source_target_pairs={{0,4},{4,8},{8,12},{12,0},{1,5},{5,9},{9,13},{13,1},{2,6},{6,10},{... | collective-permute-start | bytes 1044488 | tf_op jit(solution)/shard_map/ppermute | solution.py:569
  7.3 19.3 %collective-permute-start.5 = (bf16[1360,128]{1,0:T(8,128)(2,1)S(1)}, bf16[1360,128]{1,0:T(8,128)(2,1)S(1)}, u32[]{:S(2)}, u32[]{:S(2)}) collective-permute-start(bf16[1360,128]{1,0:T(8,128)(2,1)S(1)} %get-tuple-element.43), channel_id=1, source_target_pairs={{4,0},{8,4},{12,8},{0,12},{5,1},{9,5},{13,9},{1,13},{6,2},{10,6},{... | collective-permute-start | bytes 1044488 | tf_op jit(solution)/shard_map/ppermute | solution.py:569
  9.4 9.5 %collective-permute-start.2 = (bf16[1344,128]{1,0:T(8,128)(2,1)S(1)}, bf16[1344,128]{1,0:T(8,128)(2,1)S(1)}, u32[]{:S(2)}, u32[]{:S(2)}) collective-permute-start(bf16[1344,128]{1,0:T(8,128)(2,1)S(1)} %get-tuple-element.39), channel_id=1, source_target_pairs={{0,2},{2,0},{1,3},{3,1},{4,6},{6,4},{5,7},{7,5},{8,10},{10,8},{9,1... | collective-permute-start | bytes 1032200 | tf_op jit(solution)/shard_map/ppermute | solution.py:571
  11.1 17.7 %collective-permute-start.6 = (bf16[320,128]{1,0:T(8,128)(2,1)S(1)}, bf16[320,128]{1,0:T(8,128)(2,1)S(1)}, u32[]{:S(2)}, u32[]{:S(2)}) collective-permute-start(bf16[320,128]{1,0:T(8,128)(2,1)S(1)} %get-tuple-element.46), channel_id=1, source_target_pairs={{0,6},{2,4},{4,10},{6,8},{8,14},{10,12},{12,2},{14,0},{1,7},{3,5},... | collective-permute-start | bytes 245768 | tf_op jit(solution)/shard_map/ppermute | solution.py:549
  11.1 17.8 %collective-permute-start.7 = (bf16[320,128]{1,0:T(8,128)(2,1)S(1)}, bf16[320,128]{1,0:T(8,128)(2,1)S(1)}, u32[]{:S(2)}, u32[]{:S(2)}) collective-permute-start(bf16[320,128]{1,0:T(8,128)(2,1)S(1)} %get-tuple-element.47), channel_id=1, source_target_pairs={{0,14},{2,12},{4,2},{6,0},{8,6},{10,4},{12,10},{14,8},{1,15},{3,13... | collective-permute-start | bytes 245768 | tf_op jit(solution)/shard_map/ppermute | solution.py:549
  26.5 6.0 %collective-permute-start.3 = (bf16[44,128,128]{2,1,0:T(8,128)(2,1)S(1)}, bf16[44,128,128]{2,1,0:T(8,128)(2,1)S(1)}, u32[]{:S(2)}, u32[]{:S(2)}) collective-permute-start(bf16[44,128,128]{2,1,0:T(8,128)(2,1)S(1)} %get-tuple-element.40.own_ref), channel_id=1, source_target_pairs={{0,1},{1,0},{2,3},{3,2},{4,5},{5,4},{6,7},{7,6},{8,9},{9,8},{10,11... | collective-permute-start | bytes 4325384 | tf_op jit(solution)/shard_map/ppermute | solution.py:541
  28.8 3.7 %copy-start = (s32[78,128]{1,0:T(8,128)S(1)}, s32[78,128]{1,0:T(8,128)}, u32[]{:S(2)}) copy-start(s32[78,128]{1,0:T(8,128)} %valid_ref.3) | copy-start | bytes 119812
  32.0 3.0 %collective-permute-start.8 = (bf16[34,128,128]{2,1,0:T(8,128)(2,1)S(1)}, bf16[34,128,128]{2,1,0:T(8,128)(2,1)S(1)}, u32[]{:S(2)}, u32[]{:S(2)}) collective-permute-start(bf16[34,128,128]{2,1,0:T(8,128)(2,1)S(1)} %shard_map.62.outer_ref.own_ref), channel_id=1, source_target_pairs={{0,1},{1,0},{2,3},{3,2},{4,5},{5,4},{6,7},{7,6},{8,9},{9,8},{10,11... | collective-permute-start | bytes 3342344 | tf_op jit(solution)/shard_map/ppermute | solution.py:541
  35.9 4.4 %collective-permute-start.9 = (f32[136,128]{1,0:T(8,128)S(1)}, f32[136,128]{1,0:T(8,128)S(1)}, u32[]{:S(2)}, u32[]{:S(2)}) collective-permute-start(f32[136,128]{1,0:T(8,128)S(1)} %shard_map.64), channel_id=1, source_target_pairs={{0,2},{2,0},{1,3},{3,1},{4,6},{6,4},{5,7},{7,5},{8,10},{10,8},{9,1... | collective-permute-start | bytes 208904 | tf_op jit(solution)/shard_map/ppermute | solution.py:541
  40.2 4.4 %collective-permute-start.10 = (f32[136,128]{1,0:T(8,128)S(1)}, f32[136,128]{1,0:T(8,128)S(1)}, u32[]{:S(2)}, u32[]{:S(2)}) collective-permute-start(f32[136,128]{1,0:T(8,128)S(1)} %add.9), channel_id=1, source_target_pairs={{0,4},{4,0},{8,12},{12,8},{1,5},{5,1},{9,13},{13,9},{2,6},{6,2},{1... | collective-permute-start | bytes 208904 | tf_op jit(solution)/shard_map/ppermute | solution.py:541
  44.6 6.0 %collective-permute-start.11 = (f32[136,128]{1,0:T(8,128)S(1)}, f32[136,128]{1,0:T(8,128)S(1)}, u32[]{:S(2)}, u32[]{:S(2)}) collective-permute-start(f32[136,128]{1,0:T(8,128)S(1)} %add.10), channel_id=1, source_target_pairs={{0,8},{4,12},{8,0},{12,4},{1,9},{5,13},{9,1},{13,5},{2,10},{6,14},... | collective-permute-start | bytes 208904 | tf_op jit(solution)/shard_map/ppermute | solution.py:541
  50.7 1.3 %collective-permute-start.12 = (f32[136,128]{1,0:T(8,128)S(1)}, f32[136,128]{1,0:T(8,128)S(1)}, u32[]{:S(2)}, u32[]{:S(2)}) collective-permute-start(f32[136,128]{1,0:T(8,128)S(1)} %add.11.mine_ref), channel_id=1, source_target_pairs={{0,1},{1,0},{2,3},{3,2},{4,5},{5,4},{6,7},{7,6},{8,9},{9,8},{10,11... | collective-permute-start | bytes 208904 | tf_op jit(solution)/shard_map/ppermute | solution.py:541

commit v6 on v5

--- a/solution.py
+++ b/solution.py
@@ -34,8 +34,10 @@
     return starts, left_over, rest[:small]
 
 
-def tables_kernel(sides, rows, order_ref, dec_ref, inner_ref, outer_ref, *offset_refs):
-    cols = dec_ref.shape[2]
+def tables_kernel(sides, order_ref, x_ref, dec_ref, inner_ref, outer_ref, own, x, sem, *offset_refs):
+    rows, chans, cols = x_ref.shape
+    load = pltpu.make_async_copy(x_ref, x, sem)
+    load.start()
     dec = lax.axis_index("dec")
 
     def offsets(offset_ref, used, offset):
@@ -77,42 +79,49 @@
         return carry
 
     lax.fori_loop(1, RMAX + 1, one_radius, 0)
-
-
-def tables(rows, cols, sides, order):
+    pitch = chans + PAD
+
+    def copy_row(i, carry):
+        own[pl.ds(i * pitch, chans), :] = x[i].astype(F32)
+        return carry
+
+    load.wait()
+    lax.fori_loop(0, rows, copy_row, 0)
+    for i in range(rows, inner_ref.shape[2]):
+        own[pl.ds(i * pitch, chans), :] = jnp.zeros((chans, cols), F32)
+
+
+def tables(x, sides, order):
+    rows, chans, cols = x.shape
     own = -(-rows // 16) * 16
     inner = -(-(rows - 2 * RMAX) // 16) * 16
     shapes = [(cols + LANES, cols), (inner + 2 * HALO, own), (2 * HALO, 2 * HALO)]
     return pl.pallas_call(
-        functools.partial(tables_kernel, sides, rows),
-        out_shape=[pltpu.VMEM((RMAX + 1, *shape), BF16) for shape in shapes],
-        in_specs=[pl.BlockSpec(memory_space=pl.ANY)],
-        out_specs=[VMEM] * 3,
-        scratch_shapes=[pltpu.VMEM(shape, F32) for shape in shapes],
+        functools.partial(tables_kernel, sides),
+        out_shape=[pltpu.VMEM((RMAX + 1, *shape), BF16) for shape in shapes]
+        + [pltpu.VMEM(((own + 1) * (chans + PAD), cols), F32)],
+        in_specs=[pl.BlockSpec(memory_space=pl.ANY), HBM],
+        out_specs=[VMEM] * 4,
+        scratch_shapes=[pltpu.VMEM(x.shape, BF16), pltpu.SemaphoreType.DMA] + [pltpu.VMEM(shape, F32) for shape in shapes],
         compiler_params=PARAMS,
         cost_estimate=pl.CostEstimate(flops=10**5, bytes_accessed=10**5, transcendentals=0),
-    )(order)
-
-
-def edges_kernel(sides, rad_ref, source_ref, *refs):
-    (over_ref, up_ref, up_rest_ref, down_ref, down_rest_ref), refs = refs[:5], refs[5:]
-    edge_refs, refs = refs[:3 * sides], refs[3 * sides:]
-    x_ref, low_wide, high_wide, low_packed, high_packed, low_rest, high_rest, sems = refs
-    rows, chans, cols = x_ref.shape
+    )(order, x)
+
+
+def gather_kernel(rad_ref, source_ref, over_ref, up_ref, up_rest_ref, down_ref, down_rest_ref, low, high, low_wide, high_wide, low_packed, high_packed, low_rest, high_rest, sems):
+    rows, chans, cols = source_ref.shape
     pitch = chans + PAD
     cap, full = up_ref.shape[0], RMAX * chans
-    spans = ((0, RMAX), (rows - RMAX, RMAX), (RMAX, rows - 2 * RMAX))
     copies = [
-        pltpu.make_async_copy(source_ref.at[pl.ds(start, n)], x_ref.at[pl.ds(start, n)], sems.at[i])
-        for i, (start, n) in enumerate(spans)
+        pltpu.make_async_copy(source_ref.at[pl.ds(start, RMAX)], ref, sems.at[i])
+        for i, (start, ref) in enumerate(((0, low), (rows - RMAX, high)))
     ]
     for copy in copies:
         copy.start()
-    for copy in copies[:2]:
+    for copy, ref, wide in zip(copies, (low, high), (low_wide, high_wide)):
         copy.wait()
-    for i in range(RMAX):
-        low_wide[pl.ds(i * pitch, chans), :] = x_ref[i].astype(F32)
-        high_wide[pl.ds(i * pitch, chans), :] = x_ref[rows - RMAX + i].astype(F32)
+        for i in range(RMAX):
+            wide[pl.ds(i * pitch, chans), :] = ref[i].astype(F32)
 
     total = 0
     for c in range(chans):
@@ -143,7 +152,44 @@
 
     over_ref[0] = jnp.where(total > cap, 1, 0)
 
-    copies[2].wait()
+
+def cap_of(chans):
+    return RMAX * chans * 5 // 8 // 16 * 16
+
+
+def gather(radii, x):
+    rows, chans, cols = x.shape
+    full, cap = RMAX * chans, cap_of(chans)
+    head, rest = pltpu.VMEM((cap, cols), BF16), jax.ShapeDtypeStruct((full - cap, cols), BF16)
+    return pl.pallas_call(
+        gather_kernel,
+        out_shape=[pltpu.SMEM((1,), jnp.int32), head, rest, head, rest],
+        in_specs=[SMEM, HBM],
+        out_specs=[SMEM] + [VMEM, HBM] * 2,
+        scratch_shapes=[pltpu.VMEM((RMAX, chans, cols), BF16)] * 2
+        + [pltpu.VMEM(((RMAX + 1) * (chans + PAD), cols), F32)] * 2
+        + [pltpu.VMEM((full + 2 * HALO, cols), F32)] * 2
+        + [pltpu.VMEM(rest.shape, BF16)] * 2
+        + [pltpu.SemaphoreType.DMA((5,))],
+        compiler_params=PARAMS,
+        cost_estimate=pl.CostEstimate(flops=1, bytes_accessed=1, transcendentals=0),
+    )(radii, x)
+
+
+def pack_kernel(sides, order_ref, source_ref, *refs):
+    edge_refs, (x_ref, sems) = refs[:3 * sides], refs[3 * sides:]
+    rows, chans, cols = x_ref.shape
+    starts, left_over, shared = row_groups(rows)
+    edge, tail = EDGE * SLOTS, rows - EDGE * SLOTS
+    middle = starts[-EDGE - 1] + SLOTS
+    spans = [(middle, tail - middle), (0, edge), (edge, middle - edge), (tail, edge)]
+    loads = [
+        pltpu.make_async_copy(source_ref.at[pl.ds(start, n)], x_ref.at[pl.ds(start, n)], sems.at[i])
+        for i, (start, n) in enumerate(spans)
+    ]
+    for load in loads:
+        load.start()
+    loads[0].wait()
     dec = lax.axis_index("dec")
     lane = lax.broadcasted_iota(jnp.int32, (chans, LANES), 1)
     for side in range(sides):
@@ -152,13 +198,14 @@
             first = jnp.where(dec == 0, cols - RMAX, 0)
         else:
             first = cols - RMAX if side == 0 else 0
-        starts, left_over, shared = row_groups(rows)
 
         def moved(row, lane_of_first):
             return pltpu.roll(x_ref[row].astype(F32), lax.rem(lane_of_first - first + 2 * LANES, LANES), 1)
 
         tiles = []
         for g, start in enumerate(starts):
+            if side == 0 and start in (0, edge, tail):
+                loads[(0, edge, tail).index(start) + 1].wait()
             packed = moved(start, 0)
             for j in range(1, SLOTS):
                 packed = jnp.where(lane < RMAX * j, packed, moved(start + j, RMAX * j))
@@ -185,28 +232,19 @@
             ref[(EDGE - 1) * chans:, :] = part.astype(BF16)
 
 
-def cap_of(chans):
-    return RMAX * chans * 5 // 8 // 16 * 16
-
-
-def edges_of(radii, x, sides):
+def pack(x, sides, order):
     rows, chans, cols = x.shape
-    full, cap = RMAX * chans, cap_of(chans)
-    head, rest = pltpu.VMEM((cap, cols), BF16), jax.ShapeDtypeStruct((full - cap, cols), BF16)
     packed = [pltpu.VMEM((len(row_groups(rows)[0]) * chans + chans // 2, LANES), BF16)]
     packed += [pltpu.VMEM(((EDGE - 1) * chans + chans // 2, LANES), BF16)] * 2
     return pl.pallas_call(
-        functools.partial(edges_kernel, sides),
-        out_shape=[pltpu.SMEM((1,), jnp.int32), head, rest, head, rest] + packed * sides,
+        functools.partial(pack_kernel, sides),
+        out_shape=packed * sides,
         in_specs=[SMEM, HBM],
-        out_specs=[SMEM] + [VMEM, HBM] * 2 + [VMEM] * (3 * sides),
-        scratch_shapes=[pltpu.VMEM(x.shape, BF16)] + [pltpu.VMEM(((RMAX + 1) * (chans + PAD), cols), F32)] * 2
-        + [pltpu.VMEM((full + 2 * HALO, cols), F32)] * 2
-        + [pltpu.VMEM(rest.shape, BF16)] * 2
-        + [pltpu.SemaphoreType.DMA((5,))],
-        compiler_params=PARAMS,
-        cost_estimate=pl.CostEstimate(flops=10**6, bytes_accessed=5 * 10**6, transcendentals=0),
-    )(radii, x)
+        out_specs=[VMEM] * (3 * sides),
+        scratch_shapes=[pltpu.VMEM(x.shape, BF16), pltpu.SemaphoreType.DMA((4,))],
+        compiler_params=PARAMS,
+        cost_estimate=pl.CostEstimate(flops=1, bytes_accessed=1, transcendentals=0),
+    )(order, x)
 
 
 def widen(tiles, j):
@@ -219,13 +257,12 @@
     return value
 
 
-def inner_kernel(sides, rad_ref, x_ref, dec_ref, ra_ref, *refs):
-    edge_refs, (out_ref, begun, x, own, halo, result, sem) = refs[:sides], refs[sides:]
-    rows, chans, cols = x_ref.shape
-    load = pltpu.make_async_copy(x_ref, x, sem)
-    load.start()
+def inner_kernel(sides, rad_ref, own, dec_ref, ra_ref, *refs):
+    edge_refs, (out_ref, begun, halo, result) = refs[:sides], refs[sides:]
+    inner, chans, cols = out_ref.shape
+    rows = inner + 2 * RMAX
     pitch = chans + PAD
-    own_rows, inner = ra_ref.shape[2], rows - 2 * RMAX
+    own_rows = ra_ref.shape[2]
     base = ra_ref.shape[1] - 2 * HALO
 
     starts, left_over, shared = row_groups(rows)
@@ -247,14 +284,7 @@
     for j, row in enumerate(shared):
         halo[pl.ds(row * pitch, chans), :] = widen(tiles, j)
 
-    def copy_row(i, carry):
-        own[pl.ds(i * pitch, chans), :] = x[i].astype(F32)
-        return carry
-
-    load.wait()
-    lax.fori_loop(0, rows, copy_row, 0)
     for i in range(rows, own_rows):
-        own[pl.ds(i * pitch, chans), :] = jnp.zeros((chans, cols), F32)
         halo[pl.ds(i * pitch, chans), :] = jnp.zeros((chans, cols), F32)
 
     radii = [rad_ref[c] for c in range(chans)]
@@ -276,24 +306,21 @@
     lax.fori_loop(0, inner, store, 0)
 
 
-def smooth_inner(radii, x, halos, dec_table, ra_table):
-    rows, chans, cols = x.shape
+def smooth_inner(radii, rows, own, halos, dec_table, ra_table):
+    chans, cols = radii.shape[0], own.shape[1]
     pitch, own_rows, inner = chans + PAD, ra_table.shape[2], rows - 2 * RMAX
-    operands = [x, dec_table, ra_table, *halos]
+    operands = [own, dec_table, ra_table, *halos]
     return pl.pallas_call(
         functools.partial(inner_kernel, len(halos)),
         out_shape=[
             pltpu.VMEM((inner, chans, cols), BF16),
             pltpu.VMEM(((2 * RMAX + 1) * pitch, cols), F32),
         ],
-        in_specs=[SMEM, HBM] + [VMEM] * (len(operands) - 1),
+        in_specs=[SMEM] + [VMEM] * len(operands),
         out_specs=[VMEM] * 2,
         scratch_shapes=[
-            pltpu.VMEM(x.shape, BF16),
-            pltpu.VMEM(((own_rows + 1) * pitch, cols), F32),
             pltpu.VMEM(((own_rows + 1) * pitch, LANES), F32),
             pltpu.VMEM(((inner + 1) * pitch, cols), F32),
-            pltpu.SemaphoreType.DMA,
         ],
         compiler_params=PARAMS,
         cost_estimate=pl.CostEstimate(flops=1, bytes_accessed=1, transcendentals=0),
@@ -560,7 +587,8 @@
     right = [(i, i + 1) for i in range(dec_size - 1)]
     left = [(j, i) for i, j in right]
     sides = [right + left] if dec_size == 2 else [right, left]
-    over, up_head, up_rest, down_head, down_rest, *packed = edges_of(radii, x, len(sides))
+    over, up_head, up_rest, down_head, down_rest = gather(radii, x)
+    packed = pack(x, len(sides), over)
     before_rest, after_rest = lax.switch(
         over[0],
         [lambda a, b: (a, b), lambda a, b: (lax.ppermute(a, "ra", up), lax.ppermute(b, "ra", down))],
@@ -572,8 +600,8 @@
     corners = [
         (diagonal(high, 1, pairs), diagonal(low, -1, pairs)) for (_, low, high), pairs in zip(packed, sides)
     ]
-    dec_table, inner_table, outer_table = tables(rows, cols, len(sides), before_rest)
-    inner, begun = smooth_inner(radii, x, halos, dec_table, inner_table)
+    dec_table, inner_table, outer_table, own = tables(x, len(sides), before_rest)
+    inner, begun = smooth_inner(radii, rows, own, halos, dec_table, inner_table)
     dec_begun = outer_begin(radii, begun, (before, before_rest), (after, after_rest), dec_table)
     outer = smooth_outer(radii, dec_begun, begun, dec_table, outer_table, corners)
     folded, cross, smoothed = own_gram(inner, swap(inner, "band", 1), outer, valid)

time: 53.2 us -> 52.1 us (0.979)
  Pallas kernels: 22.9 us -> 22 us
    pallas_call x1, Pallas kernels: 7.59 us -> 4.89 us  [smooth_inner(): pl.pallas_call(functools.partial(inner_kernel, len(halos)), out_shape=[pl...]
    pallas_call x2 -> x3, Pallas kernels: 5.79 us -> 7.62 us  [the longest x1 2.72 us: tables(): pl.pallas_call(functools.partial(tables_kernel, sides), out_shape=[pltpu....]
    ppermute x1, waiting for transfers between devices: 0.97 us -> 0.42 us  [per_device(): lax.ppermute(p, 'dec', pairs)]
  transfers between devices with their start and end apart: 11 -> 11, of which waited for: 6 -> 8; matrix products, arithmetic and copies ran while one was open for 0% -> 0% of each run, Pallas kernels for 33% -> 34%
where the time goes in v6:
time: 52.1 us; the launch traced here: 51.8 us
  Pallas kernels  22 us (42%)
  starting transfers between devices  15.9 us (31%)
  waiting for transfers between devices  13.2 us (25%)
  between operations  0.74 us (1%)
    ppermute x6, waiting for transfers between devices, swap(): return lax.ppermute(array, axis, [(i, i ^ step) for i in range(size)])  12.3 us
    pallas_call x1, Pallas kernels, smooth_inner(): pl.pallas_call(functools.partial(inner_kernel, len(halos)), out_shape=[pl...  4.89 us
    ppermute x2, starting transfers between devices, diagonal(): return lax.ppermute(array, ('ra', 'dec'), pairs)  4.72 us
    ppermute x6, starting transfers between devices, swap(): return lax.ppermute(array, axis, [(i, i ^ step) for i in range(size)])  4.25 us
    pallas_call x1, Pallas kernels, smooth_outer(): pl.pallas_call(functools.partial(outer_kernel, len(corners)), out_shape=p...  3.19 us
    ppermute x1, starting transfers between devices, per_device(): lax.ppermute(up_head, 'ra', up)  3.08 us
    pallas_call x1, Pallas kernels, tables(): pl.pallas_call(functools.partial(tables_kernel, sides), out_shape=[pltpu....  2.72 us
    pallas_call x1, Pallas kernels, gather(): pl.pallas_call(gather_kernel, out_shape=[pltpu.SMEM((1,), jnp.int32), hea...  2.67 us
  transfers between devices with their start and end apart: 11, of which 8 were waited for; matrix products, arithmetic and copies ran while one was open for 0% of the time, Pallas kernels for 34%

profile of v6, /device:TPU:0, one launch (start us, length us, event | category | flops | bytes accessed | tf_op | source)
XLA Modules:
  0.0 51.8 jit_solution(2989929329853271039)
XLA Ops:
  0.6 2.7 %shard_map.58 = (s32[1]{0:T(128)S(4)}, bf16[1360,128]{1,0:T(8,128)(2,1)S(1)}, bf16[816,128]{1,0:T(8,128)(2,1)S(1)}, bf16[1360,128]{1,0:T(8,128)(2,1)S(1)}, bf16[816,128]{1,0:T(8,128)(2,1)S(1)}) custom-call(s32[128]{0:T(128)} %rad_ref.7, bf16[78,128,128]{2,1,0:T(8,128)(2,1)} %bitcast.4), custom_call_target="tpu_custom_call" | custom-call | flops 1 | bytes 1 | tf_op jit(solution)/shard_map/pallas_call | solution.py:164
  3.3 3.1 %collective-permute-start.4 = (bf16[1360,128]{1,0:T(8,128)(2,1)S(1)}, bf16[1360,128]{1,0:T(8,128)(2,1)S(1)}, u32[]{:S(2)}, u32[]{:S(2)}) collective-permute-start(bf16[1360,128]{1,0:T(8,128)(2,1)S(1)} %get-tuple-element.44), channel_id=1, source_target_pairs={{0,4},{4,8},{8,12},{12,0},{1,5},{5,9},{9,13},{13,1},{2,6},{6,10},{... | collective-permute-start | bytes 1044488 | tf_op jit(solution)/shard_map/ppermute | solution.py:597
  6.4 2.1 %collective-permute-start.5 = (bf16[1360,128]{1,0:T(8,128)(2,1)S(1)}, bf16[1360,128]{1,0:T(8,128)(2,1)S(1)}, u32[]{:S(2)}, u32[]{:S(2)}) collective-permute-start(bf16[1360,128]{1,0:T(8,128)(2,1)S(1)} %get-tuple-element.45), channel_id=1, source_target_pairs={{4,0},{8,4},{12,8},{0,12},{5,1},{9,5},{13,9},{1,13},{6,2},{10,6},{... | collective-permute-start | bytes 1044488 | tf_op jit(solution)/shard_map/ppermute | solution.py:597
  8.5 2.2 %shard_map.60 = (bf16[1344,128]{1,0:T(8,128)(2,1)S(1)}, bf16[320,128]{1,0:T(8,128)(2,1)S(1)}, bf16[320,128]{1,0:T(8,128)(2,1)S(1)}) custom-call(s32[1]{0:T(128)S(4)} %get-tuple-element.34.order_ref, bf16[78,128,128]{2,1,0:T(8,128)(2,1)} %bitcast.5), custom_call_target="tpu_custom_call" | custom-call | flops 1 | bytes 1 | tf_op jit(solution)/shard_map/pallas_call | solution.py:239
  10.7 1.7 %collective-permute-start.2 = (bf16[1344,128]{1,0:T(8,128)(2,1)S(1)}, bf16[1344,128]{1,0:T(8,128)(2,1)S(1)}, u32[]{:S(2)}, u32[]{:S(2)}) collective-permute-start(bf16[1344,128]{1,0:T(8,128)(2,1)S(1)} %get-tuple-element.41), channel_id=1, source_target_pairs={{0,2},{2,0},{1,3},{3,1},{4,6},{6,4},{5,7},{7,5},{8,10},{10,8},{9,1... | collective-permute-start | bytes 1032200 | tf_op jit(solution)/shard_map/ppermute | solution.py:599
  12.4 4.7 %collective-permute-start.7 = (bf16[320,128]{1,0:T(8,128)(2,1)S(1)}, bf16[320,128]{1,0:T(8,128)(2,1)S(1)}, u32[]{:S(2)}, u32[]{:S(2)}) collective-permute-start(bf16[320,128]{1,0:T(8,128)(2,1)S(1)} %get-tuple-element.49), channel_id=1, source_target_pairs={{0,14},{2,12},{4,2},{6,0},{8,6},{10,4},{12,10},{14,8},{1,15},{3,13... | collective-permute-start | bytes 245768 | tf_op jit(solution)/shard_map/ppermute | solution.py:576
  17.2 2.7 %shard_map.59 = (bf16[18,256,128]{2,1,0:T(8,128)(2,1)S(1)}, bf16[18,96,80]{2,1,0:T(8,128)(2,1)S(1)}, bf16[18,48,48]{2,1,0:T(8,128)(2,1)S(1)}, f32[11016,128]{1,0:T(8,128)S(1)}) custom-call(bf16[816,128]{1,0:T(8,128)(2,1)S(1)} %get-tuple-element.37.order_ref.before_rest, bf16[78,128,128]{2,1,0:T(8,128)(2,1)} %bitcast.6), custom_call_target="tpu_custom_call" | custom-call | flops 100000 | bytes 100000 | tf_op jit(solution)/shard_map/pallas_call | solution.py:99
  19.9 0.4 collective-permute-done.2.refs_0_
  20.3 4.9 %shard_map.61 = (bf16[44,128,128]{2,1,0:T(8,128)(2,1)S(1)}, f32[4760,128]{1,0:T(8,128)S(1)}) custom-call(s32[128]{0:T(128)} %rad_ref.7, f32[11016,128]{1,0:T(8,128)S(1)} %get-tuple-element.38.own, bf16[18,256,128]{2,1,0:T(8,128)(2,1)S(1)} %get-tuple-element.39.dec_ref, bf16[18,96,80]{2,1,0:T(8,128)(2,1)S(1)} %get-tuple-element.40.ra_ref, ...), custom_call_target="tpu_custom_call" | custom-call | flops 1 | bytes 1 | tf_op jit(solution)/shard_map/pallas_call | solution.py:313
  25.3 2.1 %shard_map.62.dec_begun = f32[128,48,128]{2,1,0:T(8,128)S(1)} custom-call(s32[128]{0:T(128)} %rad_ref.7, f32[4760,128]{1,0:T(8,128)S(1)} %get-tuple-element.43.order_ref.ra_begun, bf16[1360,128]{1,0:T(8,128)(2,1)S(1)} %collective-permute-done.4.before_ref, bf16[816,128]{1,0:T(8,128)(2,1)S(1)} %get-tuple-element.37.order_ref.before_rest, ...), custom_call_target="tpu_custom_call" | custom-call | flops 2000000000 | bytes 5000000 | tf_op jit(solution)/shard_map/pallas_call | solution.py:363
  27.4 0.3 collective-permute-done.6.refs_0_
  27.7 0.2 collective-permute-done.7.refs_1_
  27.9 3.2 %shard_map.63.outer_ref.own_ref = bf16[34,128,128]{2,1,0:T(8,128)(2,1)S(1)} custom-call(s32[128]{0:T(128)} %rad_ref.7, f32[128,48,128]{2,1,0:T(8,128)S(1)} %shard_map.62.dec_begun, f32[4760,128]{1,0:T(8,128)S(1)} %get-tuple-element.43.order_ref.ra_begun, bf16[18,256,128]{2,1,0:T(8,128)(2,1)S(1)} %get-tuple-element.39.dec_ref, ...), custom_call_target="tpu_custom_call" | custom-call | flops 10000000000 | bytes 5000000 | tf_op jit(solution)/shard_map/pallas_call | solution.py:420
  31.2 2.5 %shard_map.64 = (f32[72,128]{1,0:T(8,128)S(1)}, f32[128,128]{1,0:T(8,128)S(1)}, bf16[78,128,128]{2,1,0:T(8,128)(2,1)}) custom-call(bf16[44,128,128]{2,1,0:T(8,128)(2,1)S(1)} %get-tuple-element.42.own_ref, bf16[44,128,128]{2,1,0:T(8,128)(2,1)S(1)} %collective-permute-done.3.other_ref, bf16[34,128,128]{2,1,0:T(8,128)(2,1)S(1)} %shard_map.63.outer_ref.own_ref, ...), custom_call_target="tpu_custom_call" | custom-call | flops 1000000000 | bytes 3000000 | tf_op jit(solution)/shard_map/pallas_call | solution.py:491
  33.7 0.2 collective-permute-done.8.other_ref
  33.9 0.7 %shard_map.65 = f32[136,128]{1,0:T(8,128)S(1)} custom-call(f32[72,128]{1,0:T(8,128)S(1)} %get-tuple-element.51.folded_ref, f32[128,128]{1,0:T(8,128)S(1)} %get-tuple-element.52.cross_ref, bf16[34,128,128]{2,1,0:T(8,128)(2,1)S(1)} %shard_map.63.outer_ref.own_ref, bf16[34,128,128]{2,1,0:T(8,128)(2,1)S(1)} %collective-permute-done.8.other_ref, ...), custom_call_target="tpu_custom_call" | custom-call | tf_op jit(solution)/shard_map/pallas_call | solution.py:519
  34.7 1.4 %collective-permute-start.9 = (f32[136,128]{1,0:T(8,128)S(1)}, f32[136,128]{1,0:T(8,128)S(1)}, u32[]{:S(2)}, u32[]{:S(2)}) collective-permute-start(f32[136,128]{1,0:T(8,128)S(1)} %shard_map.65), channel_id=1, source_target_pairs={{0,2},{2,0},{1,3},{3,1},{4,6},{6,4},{5,7},{7,5},{8,10},{10,8},{9,1... | collective-permute-start | bytes 208904 | tf_op jit(solution)/shard_map/ppermute | solution.py:568
  36.1 3.0 %collective-permute-done.9 = f32[136,128]{1,0:T(8,128)S(1)} collective-permute-done((f32[136,128]{1,0:T(8,128)S(1)}, f32[136,128]{1,0:T(8,128)S(1)}, u32[]{:S(2)}, u32[]{:S(2)}) %collective-permute-start.9) | collective-permute-done | bytes 69664 | tf_op jit(solution)/shard_map/ppermute | solution.py:568
  39.1 1.2 %collective-permute-start.10 = (f32[136,128]{1,0:T(8,128)S(1)}, f32[136,128]{1,0:T(8,128)S(1)}, u32[]{:S(2)}, u32[]{:S(2)}) collective-permute-start(f32[136,128]{1,0:T(8,128)S(1)} %add.9), channel_id=1, source_target_pairs={{0,4},{4,0},{8,12},{12,8},{1,5},{5,1},{9,13},{13,9},{2,6},{6,2},{1... | collective-permute-start | bytes 208904 | tf_op jit(solution)/shard_map/ppermute | solution.py:568
  40.3 3.2 %collective-permute-done.10 = f32[136,128]{1,0:T(8,128)S(1)} collective-permute-done((f32[136,128]{1,0:T(8,128)S(1)}, f32[136,128]{1,0:T(8,128)S(1)}, u32[]{:S(2)}, u32[]{:S(2)}) %collective-permute-start.10) | collective-permute-done | bytes 69664 | tf_op jit(solution)/shard_map/ppermute | solution.py:568
  43.5 1.4 %collective-permute-start.11 = (f32[136,128]{1,0:T(8,128)S(1)}, f32[136,128]{1,0:T(8,128)S(1)}, u32[]{:S(2)}, u32[]{:S(2)}) collective-permute-start(f32[136,128]{1,0:T(8,128)S(1)} %add.10), channel_id=1, source_target_pairs={{0,8},{4,12},{8,0},{12,4},{1,9},{5,13},{9,1},{13,5},{2,10},{6,14},... | collective-permute-start | bytes 208904 | tf_op jit(solution)/shard_map/ppermute | solution.py:568
  44.9 4.6 %collective-permute-done.11 = f32[136,128]{1,0:T(8,128)S(1)} collective-permute-done((f32[136,128]{1,0:T(8,128)S(1)}, f32[136,128]{1,0:T(8,128)S(1)}, u32[]{:S(2)}, u32[]{:S(2)}) %collective-permute-start.11) | collective-permute-done | bytes 69664 | tf_op jit(solution)/shard_map/ppermute | solution.py:568
  49.6 1.2 %collective-permute-done.12.theirs_ref = f32[136,128]{1,0:T(8,128)S(1)} collective-permute-done((f32[136,128]{1,0:T(8,128)S(1)}, f32[136,128]{1,0:T(8,128)S(1)}, u32[]{:S(2)}, u32[]{:S(2)}) %collective-permute-start.12) | collective-permute-done | bytes 69664 | tf_op jit(solution)/shard_map/ppermute | solution.py:568
  50.9 0.9 %shard_map.66 = (f32[1,128]{1,0:T(1,128)}, f32[256,128]{1,0:T(8,128)}) custom-call(f32[136,128]{1,0:T(8,128)S(1)} %add.11.mine_ref, f32[136,128]{1,0:T(8,128)S(1)} %collective-permute-done.12.theirs_ref), custom_call_target="tpu_custom_call" | custom-call | tf_op jit(solution)/shard_map/pallas_call | solution.py:556
  (13 shorter events, 0.3 us)
Async XLA Ops:
  3.3 22.0 %collective-permute-start.4 = (bf16[1360,128]{1,0:T(8,128)(2,1)S(1)}, bf16[1360,128]{1,0:T(8,128)(2,1)S(1)}, u32[]{:S(2)}, u32[]{:S(2)}) collective-permute-start(bf16[1360,128]{1,0:T(8,128)(2,1)S(1)} %get-tuple-element.44), channel_id=1, source_target_pairs={{0,4},{4,8},{8,12},{12,0},{1,5},{5,9},{9,13},{13,1},{2,6},{6,10},{... | collective-permute-start | bytes 1044488 | tf_op jit(solution)/shard_map/ppermute | solution.py:597
  6.4 18.9 %collective-permute-start.5 = (bf16[1360,128]{1,0:T(8,128)(2,1)S(1)}, bf16[1360,128]{1,0:T(8,128)(2,1)S(1)}, u32[]{:S(2)}, u32[]{:S(2)}) collective-permute-start(bf16[1360,128]{1,0:T(8,128)(2,1)S(1)} %get-tuple-element.45), channel_id=1, source_target_pairs={{4,0},{8,4},{12,8},{0,12},{5,1},{9,5},{13,9},{1,13},{6,2},{10,6},{... | collective-permute-start | bytes 1044488 | tf_op jit(solution)/shard_map/ppermute | solution.py:597
  10.7 9.6 %collective-permute-start.2 = (bf16[1344,128]{1,0:T(8,128)(2,1)S(1)}, bf16[1344,128]{1,0:T(8,128)(2,1)S(1)}, u32[]{:S(2)}, u32[]{:S(2)}) collective-permute-start(bf16[1344,128]{1,0:T(8,128)(2,1)S(1)} %get-tuple-element.41), channel_id=1, source_target_pairs={{0,2},{2,0},{1,3},{3,1},{4,6},{6,4},{5,7},{7,5},{8,10},{10,8},{9,1... | collective-permute-start | bytes 1032200 | tf_op jit(solution)/shard_map/ppermute | solution.py:599
  12.4 15.3 %collective-permute-start.6 = (bf16[320,128]{1,0:T(8,128)(2,1)S(1)}, bf16[320,128]{1,0:T(8,128)(2,1)S(1)}, u32[]{:S(2)}, u32[]{:S(2)}) collective-permute-start(bf16[320,128]{1,0:T(8,128)(2,1)S(1)} %get-tuple-element.48), channel_id=1, source_target_pairs={{0,6},{2,4},{4,10},{6,8},{8,14},{10,12},{12,2},{14,0},{1,7},{3,5},... | collective-permute-start | bytes 245768 | tf_op jit(solution)/shard_map/ppermute | solution.py:576
  12.4 15.5 %collective-permute-start.7 = (bf16[320,128]{1,0:T(8,128)(2,1)S(1)}, bf16[320,128]{1,0:T(8,128)(2,1)S(1)}, u32[]{:S(2)}, u32[]{:S(2)}) collective-permute-start(bf16[320,128]{1,0:T(8,128)(2,1)S(1)} %get-tuple-element.49), channel_id=1, source_target_pairs={{0,14},{2,12},{4,2},{6,0},{8,6},{10,4},{12,10},{14,8},{1,15},{3,13... | collective-permute-start | bytes 245768 | tf_op jit(solution)/shard_map/ppermute | solution.py:576
  25.2 6.0 %collective-permute-start.3 = (bf16[44,128,128]{2,1,0:T(8,128)(2,1)S(1)}, bf16[44,128,128]{2,1,0:T(8,128)(2,1)S(1)}, u32[]{:S(2)}, u32[]{:S(2)}) collective-permute-start(bf16[44,128,128]{2,1,0:T(8,128)(2,1)S(1)} %get-tuple-element.42.own_ref), channel_id=1, source_target_pairs={{0,1},{1,0},{2,3},{3,2},{4,5},{5,4},{6,7},{7,6},{8,9},{9,8},{10,11... | collective-permute-start | bytes 4325384 | tf_op jit(solution)/shard_map/ppermute | solution.py:568
  27.9 3.3 %copy-start = (s32[78,128]{1,0:T(8,128)S(1)}, s32[78,128]{1,0:T(8,128)}, u32[]{:S(2)}) copy-start(s32[78,128]{1,0:T(8,128)} %valid_ref.3) | copy-start | bytes 119812
  31.1 2.8 %collective-permute-start.8 = (bf16[34,128,128]{2,1,0:T(8,128)(2,1)S(1)}, bf16[34,128,128]{2,1,0:T(8,128)(2,1)S(1)}, u32[]{:S(2)}, u32[]{:S(2)}) collective-permute-start(bf16[34,128,128]{2,1,0:T(8,128)(2,1)S(1)} %shard_map.63.outer_ref.own_ref), channel_id=1, source_target_pairs={{0,1},{1,0},{2,3},{3,2},{4,5},{5,4},{6,7},{7,6},{8,9},{9,8},{10,11... | collective-permute-start | bytes 3342344 | tf_op jit(solution)/shard_map/ppermute | solution.py:568
  34.7 4.4 %collective-permute-start.9 = (f32[136,128]{1,0:T(8,128)S(1)}, f32[136,128]{1,0:T(8,128)S(1)}, u32[]{:S(2)}, u32[]{:S(2)}) collective-permute-start(f32[136,128]{1,0:T(8,128)S(1)} %shard_map.65), channel_id=1, source_target_pairs={{0,2},{2,0},{1,3},{3,1},{4,6},{6,4},{5,7},{7,5},{8,10},{10,8},{9,1... | collective-permute-start | bytes 208904 | tf_op jit(solution)/shard_map/ppermute | solution.py:568
  39.1 4.4 %collective-permute-start.10 = (f32[136,128]{1,0:T(8,128)S(1)}, f32[136,128]{1,0:T(8,128)S(1)}, u32[]{:S(2)}, u32[]{:S(2)}) collective-permute-start(f32[136,128]{1,0:T(8,128)S(1)} %add.9), channel_id=1, source_target_pairs={{0,4},{4,0},{8,12},{12,8},{1,5},{5,1},{9,13},{13,9},{2,6},{6,2},{1... | collective-permute-start | bytes 208904 | tf_op jit(solution)/shard_map/ppermute | solution.py:568
  43.5 6.0 %collective-permute-start.11 = (f32[136,128]{1,0:T(8,128)S(1)}, f32[136,128]{1,0:T(8,128)S(1)}, u32[]{:S(2)}, u32[]{:S(2)}) collective-permute-start(f32[136,128]{1,0:T(8,128)S(1)} %add.10), channel_id=1, source_target_pairs={{0,8},{4,12},{8,0},{12,4},{1,9},{5,13},{9,1},{13,5},{2,10},{6,14},... | collective-permute-start | bytes 208904 | tf_op jit(solution)/shard_map/ppermute | solution.py:568
  49.5 1.3 %collective-permute-start.12 = (f32[136,128]{1,0:T(8,128)S(1)}, f32[136,128]{1,0:T(8,128)S(1)}, u32[]{:S(2)}, u32[]{:S(2)}) collective-permute-start(f32[136,128]{1,0:T(8,128)S(1)} %add.11.mine_ref), channel_id=1, source_target_pairs={{0,1},{1,0},{2,3},{3,2},{4,5},{5,4},{6,7},{7,6},{8,9},{9,8},{10,11... | collective-permute-start | bytes 208904 | tf_op jit(solution)/shard_map/ppermute | solution.py:568

commit v7 on v6

--- a/solution.py
+++ b/solution.py
@@ -78,7 +78,7 @@
             ref[index] = taps.astype(BF16)
         return carry
 
-    lax.fori_loop(1, RMAX + 1, one_radius, 0)
+    lax.fori_loop(1, RMAX + 1, one_radius, 0, unroll=True)
     pitch = chans + PAD
 
     def copy_row(i, carry):
@@ -86,7 +86,7 @@
         return carry
 
     load.wait()
-    lax.fori_loop(0, rows, copy_row, 0)
+    lax.fori_loop(0, rows, copy_row, 0, unroll=6)
     for i in range(rows, inner_ref.shape[2]):
         own[pl.ds(i * pitch, chans), :] = jnp.zeros((chans, cols), F32)
 
@@ -303,7 +303,7 @@
         out_ref[i] = result[pl.ds(i * pitch, chans), :].astype(BF16)
         return carry
 
-    lax.fori_loop(0, inner, store, 0)
+    lax.fori_loop(0, inner, store, 0, unroll=4)
 
 
 def smooth_inner(radii, rows, own, halos, dec_table, ra_table):
@@ -410,7 +410,7 @@
         out_ref[i] = (ra_begun[picked, :] + result[picked, :]).astype(BF16)
         return carry
 
-    lax.fori_loop(0, rows, store, 0)
+    lax.fori_loop(0, rows, store, 0, unroll=True)
 
 
 def smooth_outer(radii, dec_begun, ra_begun, dec_table, ra_table, corners):
@@ -449,7 +449,7 @@
             sums[...] += nt(jnp.broadcast_to(line, (16, line.shape[1])), own)[:SUM_ROWS]
         return carry
 
-    lax.fori_loop(0, rows // depth, body, 0)
+    lax.fori_loop(0, rows // depth, body, 0, unroll=True)
 
 
 def outer_row(image_rows):

time: 52.1 us -> 51.6 us (level)
  Pallas kernels: 22 us -> 20.5 us
  waiting for transfers between devices: 13.2 us -> 14.1 us
    pallas_call x1, Pallas kernels: 2.72 us -> 2.1 us  [tables(): pl.pallas_call(functools.partial(tables_kernel, sides), out_shape=[pltpu....]
    ppermute x1, waiting for transfers between devices: 0.42 us -> 1.04 us  [per_device(): lax.ppermute(p, 'dec', pairs)]
    pallas_call x1, Pallas kernels: 2.51 us -> 1.97 us  [own_gram(): pl.pallas_call(own_gram_kernel, out_shape=[pltpu.VMEM((chans // 2 + SUM_R...]
  transfers between devices with their start and end apart: 11 -> 11, of which waited for: 8 -> 8; matrix products, arithmetic and copies ran while one was open for 0% -> 0% of each run, Pallas kernels for 34% -> 32%
where the time goes in v7:
time: 51.6 us; the launch traced here: 51.3 us
  Pallas kernels  20.5 us (40%)
  starting transfers between devices  15.9 us (31%)
  waiting for transfers between devices  14.1 us (27%)
  between operations  0.74 us (1%)
    ppermute x6, waiting for transfers between devices, swap(): return lax.ppermute(array, axis, [(i, i ^ step) for i in range(size)])  12.7 us
    pallas_call x1, Pallas kernels, smooth_inner(): pl.pallas_call(functools.partial(inner_kernel, len(halos)), out_shape=[pl...  4.79 us
    ppermute x2, starting transfers between devices, diagonal(): return lax.ppermute(array, ('ra', 'dec'), pairs)  4.72 us
    ppermute x6, starting transfers between devices, swap(): return lax.ppermute(array, axis, [(i, i ^ step) for i in range(size)])  4.3 us
    ppermute x1, starting transfers between devices, per_device(): lax.ppermute(up_head, 'ra', up)  3.08 us
    pallas_call x1, Pallas kernels, smooth_outer(): pl.pallas_call(functools.partial(outer_kernel, len(corners)), out_shape=p...  2.98 us
    pallas_call x1, Pallas kernels, gather(): pl.pallas_call(gather_kernel, out_shape=[pltpu.SMEM((1,), jnp.int32), hea...  2.67 us
    pallas_call x1, Pallas kernels, outer_begin(): pl.pallas_call(outer_begin_kernel, out_shape=pltpu.VMEM((chans, 2 * HALO,...  2.31 us
  transfers between devices with their start and end apart: 11, of which 8 were waited for; matrix products, arithmetic and copies ran while one was open for 0% of the time, Pallas kernels for 32%

profile of v7, /device:TPU:0, one launch (start us, length us, event | category | flops | bytes accessed | tf_op | source)
XLA Modules:
  0.0 51.3 jit_solution(3925899970992593244)
XLA Ops:
  0.6 2.7 %shard_map.58 = (s32[1]{0:T(128)S(4)}, bf16[1360,128]{1,0:T(8,128)(2,1)S(1)}, bf16[816,128]{1,0:T(8,128)(2,1)S(1)}, bf16[1360,128]{1,0:T(8,128)(2,1)S(1)}, bf16[816,128]{1,0:T(8,128)(2,1)S(1)}) custom-call(s32[128]{0:T(128)} %rad_ref.7, bf16[78,128,128]{2,1,0:T(8,128)(2,1)} %bitcast.4), custom_call_target="tpu_custom_call" | custom-call | flops 1 | bytes 1 | tf_op jit(solution)/shard_map/pallas_call | solution.py:164
  3.3 3.1 %collective-permute-start.4 = (bf16[1360,128]{1,0:T(8,128)(2,1)S(1)}, bf16[1360,128]{1,0:T(8,128)(2,1)S(1)}, u32[]{:S(2)}, u32[]{:S(2)}) collective-permute-start(bf16[1360,128]{1,0:T(8,128)(2,1)S(1)} %get-tuple-element.44), channel_id=1, source_target_pairs={{0,4},{4,8},{8,12},{12,0},{1,5},{5,9},{9,13},{13,1},{2,6},{6,10},{... | collective-permute-start | bytes 1044488 | tf_op jit(solution)/shard_map/ppermute | solution.py:597
  6.4 2.1 %collective-permute-start.5 = (bf16[1360,128]{1,0:T(8,128)(2,1)S(1)}, bf16[1360,128]{1,0:T(8,128)(2,1)S(1)}, u32[]{:S(2)}, u32[]{:S(2)}) collective-permute-start(bf16[1360,128]{1,0:T(8,128)(2,1)S(1)} %get-tuple-element.45), channel_id=1, source_target_pairs={{4,0},{8,4},{12,8},{0,12},{5,1},{9,5},{13,9},{1,13},{6,2},{10,6},{... | collective-permute-start | bytes 1044488 | tf_op jit(solution)/shard_map/ppermute | solution.py:597
  8.5 2.2 %shard_map.60 = (bf16[1344,128]{1,0:T(8,128)(2,1)S(1)}, bf16[320,128]{1,0:T(8,128)(2,1)S(1)}, bf16[320,128]{1,0:T(8,128)(2,1)S(1)}) custom-call(s32[1]{0:T(128)S(4)} %get-tuple-element.34.order_ref, bf16[78,128,128]{2,1,0:T(8,128)(2,1)} %bitcast.5), custom_call_target="tpu_custom_call" | custom-call | flops 1 | bytes 1 | tf_op jit(solution)/shard_map/pallas_call | solution.py:239
  10.7 1.7 %collective-permute-start.2 = (bf16[1344,128]{1,0:T(8,128)(2,1)S(1)}, bf16[1344,128]{1,0:T(8,128)(2,1)S(1)}, u32[]{:S(2)}, u32[]{:S(2)}) collective-permute-start(bf16[1344,128]{1,0:T(8,128)(2,1)S(1)} %get-tuple-element.41), channel_id=1, source_target_pairs={{0,2},{2,0},{1,3},{3,1},{4,6},{6,4},{5,7},{7,5},{8,10},{10,8},{9,1... | collective-permute-start | bytes 1032200 | tf_op jit(solution)/shard_map/ppermute | solution.py:599
  12.4 4.7 %collective-permute-start.7 = (bf16[320,128]{1,0:T(8,128)(2,1)S(1)}, bf16[320,128]{1,0:T(8,128)(2,1)S(1)}, u32[]{:S(2)}, u32[]{:S(2)}) collective-permute-start(bf16[320,128]{1,0:T(8,128)(2,1)S(1)} %get-tuple-element.49), channel_id=1, source_target_pairs={{0,14},{2,12},{4,2},{6,0},{8,6},{10,4},{12,10},{14,8},{1,15},{3,13... | collective-permute-start | bytes 245768 | tf_op jit(solution)/shard_map/ppermute | solution.py:576
  17.2 2.1 %shard_map.59 = (bf16[18,256,128]{2,1,0:T(8,128)(2,1)S(1)}, bf16[18,96,80]{2,1,0:T(8,128)(2,1)S(1)}, bf16[18,48,48]{2,1,0:T(8,128)(2,1)S(1)}, f32[11016,128]{1,0:T(8,128)S(1)}) custom-call(bf16[816,128]{1,0:T(8,128)(2,1)S(1)} %get-tuple-element.37.order_ref.before_rest, bf16[78,128,128]{2,1,0:T(8,128)(2,1)} %bitcast.6), custom_call_target="tpu_custom_call" | custom-call | flops 100000 | bytes 100000 | tf_op jit(solution)/shard_map/pallas_call | solution.py:99
  19.3 1.0 %collective-permute-done.2.refs_0_ = bf16[1344,128]{1,0:T(8,128)(2,1)S(1)} collective-permute-done((bf16[1344,128]{1,0:T(8,128)(2,1)S(1)}, bf16[1344,128]{1,0:T(8,128)(2,1)S(1)}, u32[]{:S(2)}, u32[]{:S(2)}) %collective-permute-start.2) | collective-permute-done | bytes 344096 | tf_op jit(solution)/shard_map/ppermute | solution.py:599
  20.3 4.8 %shard_map.61 = (bf16[44,128,128]{2,1,0:T(8,128)(2,1)S(1)}, f32[4760,128]{1,0:T(8,128)S(1)}) custom-call(s32[128]{0:T(128)} %rad_ref.7, f32[11016,128]{1,0:T(8,128)S(1)} %get-tuple-element.38.own, bf16[18,256,128]{2,1,0:T(8,128)(2,1)S(1)} %get-tuple-element.39.dec_ref, bf16[18,96,80]{2,1,0:T(8,128)(2,1)S(1)} %get-tuple-element.40.ra_ref, ...), custom_call_target="tpu_custom_call" | custom-call | flops 1 | bytes 1 | tf_op jit(solution)/shard_map/pallas_call | solution.py:313
  25.2 2.3 %shard_map.62.dec_begun = f32[128,48,128]{2,1,0:T(8,128)S(1)} custom-call(s32[128]{0:T(128)} %rad_ref.7, f32[4760,128]{1,0:T(8,128)S(1)} %get-tuple-element.43.order_ref.ra_begun, bf16[1360,128]{1,0:T(8,128)(2,1)S(1)} %collective-permute-done.4.before_ref, bf16[816,128]{1,0:T(8,128)(2,1)S(1)} %get-tuple-element.37.order_ref.before_rest, ...), custom_call_target="tpu_custom_call" | custom-call | flops 2000000000 | bytes 5000000 | tf_op jit(solution)/shard_map/pallas_call | solution.py:363
  27.5 0.2 collective-permute-done.6.refs_0_
  27.9 3.0 %shard_map.63.outer_ref.own_ref = bf16[34,128,128]{2,1,0:T(8,128)(2,1)S(1)} custom-call(s32[128]{0:T(128)} %rad_ref.7, f32[128,48,128]{2,1,0:T(8,128)S(1)} %shard_map.62.dec_begun, f32[4760,128]{1,0:T(8,128)S(1)} %get-tuple-element.43.order_ref.ra_begun, bf16[18,256,128]{2,1,0:T(8,128)(2,1)S(1)} %get-tuple-element.39.dec_ref, ...), custom_call_target="tpu_custom_call" | custom-call | flops 10000000000 | bytes 5000000 | tf_op jit(solution)/shard_map/pallas_call | solution.py:420
  30.9 0.2 collective-permute-start.8
  31.1 2.0 %shard_map.64 = (f32[72,128]{1,0:T(8,128)S(1)}, f32[128,128]{1,0:T(8,128)S(1)}, bf16[78,128,128]{2,1,0:T(8,128)(2,1)}) custom-call(bf16[44,128,128]{2,1,0:T(8,128)(2,1)S(1)} %get-tuple-element.42.own_ref, bf16[44,128,128]{2,1,0:T(8,128)(2,1)S(1)} %collective-permute-done.3.other_ref, bf16[34,128,128]{2,1,0:T(8,128)(2,1)S(1)} %shard_map.63.outer_ref.own_ref, ...), custom_call_target="tpu_custom_call" | custom-call | flops 1000000000 | bytes 3000000 | tf_op jit(solution)/shard_map/pallas_call | solution.py:491
  33.1 0.6 %collective-permute-done.8.other_ref = bf16[34,128,128]{2,1,0:T(8,128)(2,1)S(1)} collective-permute-done((bf16[34,128,128]{2,1,0:T(8,128)(2,1)S(1)}, bf16[34,128,128]{2,1,0:T(8,128)(2,1)S(1)}, u32[]{:S(2)}, u32[]{:S(2)}) %collective-permute-start.8) | collective-permute-done | bytes 1114144 | tf_op jit(solution)/shard_map/ppermute | solution.py:568
  33.7 0.5 %shard_map.65 = f32[136,128]{1,0:T(8,128)S(1)} custom-call(f32[72,128]{1,0:T(8,128)S(1)} %get-tuple-element.51.folded_ref, f32[128,128]{1,0:T(8,128)S(1)} %get-tuple-element.52.cross_ref, bf16[34,128,128]{2,1,0:T(8,128)(2,1)S(1)} %shard_map.63.outer_ref.own_ref, bf16[34,128,128]{2,1,0:T(8,128)(2,1)S(1)} %collective-permute-done.8.other_ref, ...), custom_call_target="tpu_custom_call" | custom-call | tf_op jit(solution)/shard_map/pallas_call | solution.py:519
  34.2 1.3 %collective-permute-start.9 = (f32[136,128]{1,0:T(8,128)S(1)}, f32[136,128]{1,0:T(8,128)S(1)}, u32[]{:S(2)}, u32[]{:S(2)}) collective-permute-start(f32[136,128]{1,0:T(8,128)S(1)} %shard_map.65), channel_id=1, source_target_pairs={{0,2},{2,0},{1,3},{3,1},{4,6},{6,4},{5,7},{7,5},{8,10},{10,8},{9,1... | collective-permute-start | bytes 208904 | tf_op jit(solution)/shard_map/ppermute | solution.py:568
  35.6 3.0 %collective-permute-done.9 = f32[136,128]{1,0:T(8,128)S(1)} collective-permute-done((f32[136,128]{1,0:T(8,128)S(1)}, f32[136,128]{1,0:T(8,128)S(1)}, u32[]{:S(2)}, u32[]{:S(2)}) %collective-permute-start.9) | collective-permute-done | bytes 69664 | tf_op jit(solution)/shard_map/ppermute | solution.py:568
  38.6 1.2 %collective-permute-start.10 = (f32[136,128]{1,0:T(8,128)S(1)}, f32[136,128]{1,0:T(8,128)S(1)}, u32[]{:S(2)}, u32[]{:S(2)}) collective-permute-start(f32[136,128]{1,0:T(8,128)S(1)} %add.9), channel_id=1, source_target_pairs={{0,4},{4,0},{8,12},{12,8},{1,5},{5,1},{9,13},{13,9},{2,6},{6,2},{1... | collective-permute-start | bytes 208904 | tf_op jit(solution)/shard_map/ppermute | solution.py:568
  39.8 3.2 %collective-permute-done.10 = f32[136,128]{1,0:T(8,128)S(1)} collective-permute-done((f32[136,128]{1,0:T(8,128)S(1)}, f32[136,128]{1,0:T(8,128)S(1)}, u32[]{:S(2)}, u32[]{:S(2)}) %collective-permute-start.10) | collective-permute-done | bytes 69664 | tf_op jit(solution)/shard_map/ppermute | solution.py:568
  43.0 1.4 %collective-permute-start.11 = (f32[136,128]{1,0:T(8,128)S(1)}, f32[136,128]{1,0:T(8,128)S(1)}, u32[]{:S(2)}, u32[]{:S(2)}) collective-permute-start(f32[136,128]{1,0:T(8,128)S(1)} %add.10), channel_id=1, source_target_pairs={{0,8},{4,12},{8,0},{12,4},{1,9},{5,13},{9,1},{13,5},{2,10},{6,14},... | collective-permute-start | bytes 208904 | tf_op jit(solution)/shard_map/ppermute | solution.py:568
  44.4 4.6 %collective-permute-done.11 = f32[136,128]{1,0:T(8,128)S(1)} collective-permute-done((f32[136,128]{1,0:T(8,128)S(1)}, f32[136,128]{1,0:T(8,128)S(1)}, u32[]{:S(2)}, u32[]{:S(2)}) %collective-permute-start.11) | collective-permute-done | bytes 69664 | tf_op jit(solution)/shard_map/ppermute | solution.py:568
  49.1 1.2 %collective-permute-done.12.theirs_ref = f32[136,128]{1,0:T(8,128)S(1)} collective-permute-done((f32[136,128]{1,0:T(8,128)S(1)}, f32[136,128]{1,0:T(8,128)S(1)}, u32[]{:S(2)}, u32[]{:S(2)}) %collective-permute-start.12) | collective-permute-done | bytes 69664 | tf_op jit(solution)/shard_map/ppermute | solution.py:568
  50.4 0.9 %shard_map.66 = (f32[1,128]{1,0:T(1,128)}, f32[256,128]{1,0:T(8,128)}) custom-call(f32[136,128]{1,0:T(8,128)S(1)} %add.11.mine_ref, f32[136,128]{1,0:T(8,128)S(1)} %collective-permute-done.12.theirs_ref), custom_call_target="tpu_custom_call" | custom-call | tf_op jit(solution)/shard_map/pallas_call | solution.py:556
  (13 shorter events, 0.4 us)
Async XLA Ops:
  3.3 21.9 %collective-permute-start.4 = (bf16[1360,128]{1,0:T(8,128)(2,1)S(1)}, bf16[1360,128]{1,0:T(8,128)(2,1)S(1)}, u32[]{:S(2)}, u32[]{:S(2)}) collective-permute-start(bf16[1360,128]{1,0:T(8,128)(2,1)S(1)} %get-tuple-element.44), channel_id=1, source_target_pairs={{0,4},{4,8},{8,12},{12,0},{1,5},{5,9},{9,13},{13,1},{2,6},{6,10},{... | collective-permute-start | bytes 1044488 | tf_op jit(solution)/shard_map/ppermute | solution.py:597
  6.4 18.8 %collective-permute-start.5 = (bf16[1360,128]{1,0:T(8,128)(2,1)S(1)}, bf16[1360,128]{1,0:T(8,128)(2,1)S(1)}, u32[]{:S(2)}, u32[]{:S(2)}) collective-permute-start(bf16[1360,128]{1,0:T(8,128)(2,1)S(1)} %get-tuple-element.45), channel_id=1, source_target_pairs={{4,0},{8,4},{12,8},{0,12},{5,1},{9,5},{13,9},{1,13},{6,2},{10,6},{... | collective-permute-start | bytes 1044488 | tf_op jit(solution)/shard_map/ppermute | solution.py:597
  10.7 9.6 %collective-permute-start.2 = (bf16[1344,128]{1,0:T(8,128)(2,1)S(1)}, bf16[1344,128]{1,0:T(8,128)(2,1)S(1)}, u32[]{:S(2)}, u32[]{:S(2)}) collective-permute-start(bf16[1344,128]{1,0:T(8,128)(2,1)S(1)} %get-tuple-element.41), channel_id=1, source_target_pairs={{0,2},{2,0},{1,3},{3,1},{4,6},{6,4},{5,7},{7,5},{8,10},{10,8},{9,1... | collective-permute-start | bytes 1032200 | tf_op jit(solution)/shard_map/ppermute | solution.py:599
  12.4 15.3 %collective-permute-start.6 = (bf16[320,128]{1,0:T(8,128)(2,1)S(1)}, bf16[320,128]{1,0:T(8,128)(2,1)S(1)}, u32[]{:S(2)}, u32[]{:S(2)}) collective-permute-start(bf16[320,128]{1,0:T(8,128)(2,1)S(1)} %get-tuple-element.48), channel_id=1, source_target_pairs={{0,6},{2,4},{4,10},{6,8},{8,14},{10,12},{12,2},{14,0},{1,7},{3,5},... | collective-permute-start | bytes 245768 | tf_op jit(solution)/shard_map/ppermute | solution.py:576
  12.4 15.5 %collective-permute-start.7 = (bf16[320,128]{1,0:T(8,128)(2,1)S(1)}, bf16[320,128]{1,0:T(8,128)(2,1)S(1)}, u32[]{:S(2)}, u32[]{:S(2)}) collective-permute-start(bf16[320,128]{1,0:T(8,128)(2,1)S(1)} %get-tuple-element.49), channel_id=1, source_target_pairs={{0,14},{2,12},{4,2},{6,0},{8,6},{10,4},{12,10},{14,8},{1,15},{3,13... | collective-permute-start | bytes 245768 | tf_op jit(solution)/shard_map/ppermute | solution.py:576
  25.1 6.0 %collective-permute-start.3 = (bf16[44,128,128]{2,1,0:T(8,128)(2,1)S(1)}, bf16[44,128,128]{2,1,0:T(8,128)(2,1)S(1)}, u32[]{:S(2)}, u32[]{:S(2)}) collective-permute-start(bf16[44,128,128]{2,1,0:T(8,128)(2,1)S(1)} %get-tuple-element.42.own_ref), channel_id=1, source_target_pairs={{0,1},{1,0},{2,3},{3,2},{4,5},{5,4},{6,7},{7,6},{8,9},{9,8},{10,11... | collective-permute-start | bytes 4325384 | tf_op jit(solution)/shard_map/ppermute | solution.py:568
  27.9 3.2 %copy-start = (s32[78,128]{1,0:T(8,128)S(1)}, s32[78,128]{1,0:T(8,128)}, u32[]{:S(2)}) copy-start(s32[78,128]{1,0:T(8,128)} %valid_ref.3) | copy-start | bytes 119812
  30.9 2.8 %collective-permute-start.8 = (bf16[34,128,128]{2,1,0:T(8,128)(2,1)S(1)}, bf16[34,128,128]{2,1,0:T(8,128)(2,1)S(1)}, u32[]{:S(2)}, u32[]{:S(2)}) collective-permute-start(bf16[34,128,128]{2,1,0:T(8,128)(2,1)S(1)} %shard_map.63.outer_ref.own_ref), channel_id=1, source_target_pairs={{0,1},{1,0},{2,3},{3,2},{4,5},{5,4},{6,7},{7,6},{8,9},{9,8},{10,11... | collective-permute-start | bytes 3342344 | tf_op jit(solution)/shard_map/ppermute | solution.py:568
  34.2 4.4 %collective-permute-start.9 = (f32[136,128]{1,0:T(8,128)S(1)}, f32[136,128]{1,0:T(8,128)S(1)}, u32[]{:S(2)}, u32[]{:S(2)}) collective-permute-start(f32[136,128]{1,0:T(8,128)S(1)} %shard_map.65), channel_id=1, source_target_pairs={{0,2},{2,0},{1,3},{3,1},{4,6},{6,4},{5,7},{7,5},{8,10},{10,8},{9,1... | collective-permute-start | bytes 208904 | tf_op jit(solution)/shard_map/ppermute | solution.py:568
  38.6 4.4 %collective-permute-start.10 = (f32[136,128]{1,0:T(8,128)S(1)}, f32[136,128]{1,0:T(8,128)S(1)}, u32[]{:S(2)}, u32[]{:S(2)}) collective-permute-start(f32[136,128]{1,0:T(8,128)S(1)} %add.9), channel_id=1, source_target_pairs={{0,4},{4,0},{8,12},{12,8},{1,5},{5,1},{9,13},{13,9},{2,6},{6,2},{1... | collective-permute-start | bytes 208904 | tf_op jit(solution)/shard_map/ppermute | solution.py:568
  43.0 6.0 %collective-permute-start.11 = (f32[136,128]{1,0:T(8,128)S(1)}, f32[136,128]{1,0:T(8,128)S(1)}, u32[]{:S(2)}, u32[]{:S(2)}) collective-permute-start(f32[136,128]{1,0:T(8,128)S(1)} %add.10), channel_id=1, source_target_pairs={{0,8},{4,12},{8,0},{12,4},{1,9},{5,13},{9,1},{13,5},{2,10},{6,14},... | collective-permute-start | bytes 208904 | tf_op jit(solution)/shard_map/ppermute | solution.py:568
  49.1 1.3 %collective-permute-start.12 = (f32[136,128]{1,0:T(8,128)S(1)}, f32[136,128]{1,0:T(8,128)S(1)}, u32[]{:S(2)}, u32[]{:S(2)}) collective-permute-start(f32[136,128]{1,0:T(8,128)S(1)} %add.11.mine_ref), channel_id=1, source_target_pairs={{0,1},{1,0},{2,3},{3,2},{4,5},{5,4},{6,7},{7,6},{8,9},{9,8},{10,11... | collective-permute-start | bytes 208904 | tf_op jit(solution)/shard_map/ppermute | solution.py:568

commit v8 on v7

--- a/solution.py
+++ b/solution.py
@@ -11,7 +11,7 @@
 LANES = 128
 SLOTS = LANES // RMAX
 EDGE = -(-RMAX // SLOTS)
-PAD = 8
+PAD = 4
 HALO = 24
 VMEM_LIMIT = 32 * 1024 * 1024
 BF16, F32 = jnp.bfloat16, jnp.float32

time: 51.6 us -> 51.4 us (level)
  waiting for transfers between devices: 14.1 us -> 16.2 us
  Pallas kernels: 20.5 us -> 18.8 us
  starting transfers between devices: 15.9 us -> 15.3 us
    pallas_call x1, Pallas kernels: 4.79 us -> 3.47 us  [smooth_inner(): pl.pallas_call(functools.partial(inner_kernel, len(halos)), out_shape=[pl...]
    ppermute x1, waiting for transfers between devices: 0.01 us -> 1.32 us  [per_device(): lax.ppermute(down_head, 'ra', down)]
    ppermute x6, starting transfers between devices: 4.3 us -> 3.67 us  [swap(): return lax.ppermute(array, axis, [(i, i ^ step) for i in range(size)])]
    ppermute x6, waiting for transfers between devices: 12.7 us -> 13.3 us  [swap(): return lax.ppermute(array, axis, [(i, i ^ step) for i in range(size)])]
  transfers between devices with their start and end apart: 11 -> 11, of which waited for: 8 -> 9; matrix products, arithmetic and copies ran while one was open for 0% -> 0% of each run, Pallas kernels for 32% -> 29%
where the time goes in v8:
time: 51.4 us; the launch traced here: 51.1 us
  Pallas kernels  18.8 us (37%)
  waiting for transfers between devices  16.2 us (32%)
  starting transfers between devices  15.3 us (30%)
  between operations  0.75 us (1%)
    ppermute x6, waiting for transfers between devices, swap(): return lax.ppermute(array, axis, [(i, i ^ step) for i in range(size)])  13.3 us
    ppermute x2, starting transfers between devices, diagonal(): return lax.ppermute(array, ('ra', 'dec'), pairs)  4.72 us
    ppermute x6, starting transfers between devices, swap(): return lax.ppermute(array, axis, [(i, i ^ step) for i in range(size)])  3.67 us
    pallas_call x1, Pallas kernels, smooth_inner(): pl.pallas_call(functools.partial(inner_kernel, len(halos)), out_shape=[pl...  3.47 us
    ppermute x1, starting transfers between devices, per_device(): lax.ppermute(up_head, 'ra', up)  3.08 us
    pallas_call x1, Pallas kernels, smooth_outer(): pl.pallas_call(functools.partial(outer_kernel, len(corners)), out_shape=p...  2.89 us
    pallas_call x1, Pallas kernels, gather(): pl.pallas_call(gather_kernel, out_shape=[pltpu.SMEM((1,), jnp.int32), hea...  2.56 us
    pallas_call x1, Pallas kernels, pack(): pl.pallas_call(functools.partial(pack_kernel, sides), out_shape=packed *...  2.23 us
  transfers between devices with their start and end apart: 11, of which 9 were waited for; matrix products, arithmetic and copies ran while one was open for 0% of the time, Pallas kernels for 29%

profile of v8, /device:TPU:0, one launch (start us, length us, event | category | flops | bytes accessed | tf_op | source)
XLA Modules:
  0.0 51.1 jit_solution(5234813391393767096)
XLA Ops:
  0.6 2.6 %shard_map.58 = (s32[1]{0:T(128)S(4)}, bf16[1360,128]{1,0:T(8,128)(2,1)S(1)}, bf16[816,128]{1,0:T(8,128)(2,1)S(1)}, bf16[1360,128]{1,0:T(8,128)(2,1)S(1)}, bf16[816,128]{1,0:T(8,128)(2,1)S(1)}) custom-call(s32[128]{0:T(128)} %rad_ref.7, bf16[78,128,128]{2,1,0:T(8,128)(2,1)} %bitcast.4), custom_call_target="tpu_custom_call" | custom-call | flops 1 | bytes 1 | tf_op jit(solution)/shard_map/pallas_call | solution.py:164
  3.2 3.1 %collective-permute-start.4 = (bf16[1360,128]{1,0:T(8,128)(2,1)S(1)}, bf16[1360,128]{1,0:T(8,128)(2,1)S(1)}, u32[]{:S(2)}, u32[]{:S(2)}) collective-permute-start(bf16[1360,128]{1,0:T(8,128)(2,1)S(1)} %get-tuple-element.44), channel_id=1, source_target_pairs={{0,4},{4,8},{8,12},{12,0},{1,5},{5,9},{9,13},{13,1},{2,6},{6,10},{... | collective-permute-start | bytes 1044488 | tf_op jit(solution)/shard_map/ppermute | solution.py:597
  6.3 2.1 %collective-permute-start.5 = (bf16[1360,128]{1,0:T(8,128)(2,1)S(1)}, bf16[1360,128]{1,0:T(8,128)(2,1)S(1)}, u32[]{:S(2)}, u32[]{:S(2)}) collective-permute-start(bf16[1360,128]{1,0:T(8,128)(2,1)S(1)} %get-tuple-element.45), channel_id=1, source_target_pairs={{4,0},{8,4},{12,8},{0,12},{5,1},{9,5},{13,9},{1,13},{6,2},{10,6},{... | collective-permute-start | bytes 1044488 | tf_op jit(solution)/shard_map/ppermute | solution.py:597
  8.4 2.2 %shard_map.60 = (bf16[1344,128]{1,0:T(8,128)(2,1)S(1)}, bf16[320,128]{1,0:T(8,128)(2,1)S(1)}, bf16[320,128]{1,0:T(8,128)(2,1)S(1)}) custom-call(s32[1]{0:T(128)S(4)} %get-tuple-element.34.order_ref, bf16[78,128,128]{2,1,0:T(8,128)(2,1)} %bitcast.5), custom_call_target="tpu_custom_call" | custom-call | flops 1 | bytes 1 | tf_op jit(solution)/shard_map/pallas_call | solution.py:239
  10.6 1.7 %collective-permute-start.2 = (bf16[1344,128]{1,0:T(8,128)(2,1)S(1)}, bf16[1344,128]{1,0:T(8,128)(2,1)S(1)}, u32[]{:S(2)}, u32[]{:S(2)}) collective-permute-start(bf16[1344,128]{1,0:T(8,128)(2,1)S(1)} %get-tuple-element.41), channel_id=1, source_target_pairs={{0,2},{2,0},{1,3},{3,1},{4,6},{6,4},{5,7},{7,5},{8,10},{10,8},{9,1... | collective-permute-start | bytes 1032200 | tf_op jit(solution)/shard_map/ppermute | solution.py:599
  12.3 4.7 %collective-permute-start.7 = (bf16[320,128]{1,0:T(8,128)(2,1)S(1)}, bf16[320,128]{1,0:T(8,128)(2,1)S(1)}, u32[]{:S(2)}, u32[]{:S(2)}) collective-permute-start(bf16[320,128]{1,0:T(8,128)(2,1)S(1)} %get-tuple-element.49), channel_id=1, source_target_pairs={{0,14},{2,12},{4,2},{6,0},{8,6},{10,4},{12,10},{14,8},{1,15},{3,13... | collective-permute-start | bytes 245768 | tf_op jit(solution)/shard_map/ppermute | solution.py:576
  17.0 2.1 %shard_map.59 = (bf16[18,256,128]{2,1,0:T(8,128)(2,1)S(1)}, bf16[18,96,80]{2,1,0:T(8,128)(2,1)S(1)}, bf16[18,48,48]{2,1,0:T(8,128)(2,1)S(1)}, f32[10692,128]{1,0:T(8,128)S(1)}) custom-call(bf16[816,128]{1,0:T(8,128)(2,1)S(1)} %get-tuple-element.37.order_ref.before_rest, bf16[78,128,128]{2,1,0:T(8,128)(2,1)} %bitcast.6), custom_call_target="tpu_custom_call" | custom-call | flops 100000 | bytes 100000 | tf_op jit(solution)/shard_map/pallas_call | solution.py:99
  19.1 1.0 %collective-permute-done.2.refs_0_ = bf16[1344,128]{1,0:T(8,128)(2,1)S(1)} collective-permute-done((bf16[1344,128]{1,0:T(8,128)(2,1)S(1)}, bf16[1344,128]{1,0:T(8,128)(2,1)S(1)}, u32[]{:S(2)}, u32[]{:S(2)}) %collective-permute-start.2) | collective-permute-done | bytes 344096 | tf_op jit(solution)/shard_map/ppermute | solution.py:599
  20.2 3.5 %shard_map.61 = (bf16[44,128,128]{2,1,0:T(8,128)(2,1)S(1)}, f32[4620,128]{1,0:T(8,128)S(1)}) custom-call(s32[128]{0:T(128)} %rad_ref.7, f32[10692,128]{1,0:T(8,128)S(1)} %get-tuple-element.38.own, bf16[18,256,128]{2,1,0:T(8,128)(2,1)S(1)} %get-tuple-element.39.dec_ref, bf16[18,96,80]{2,1,0:T(8,128)(2,1)S(1)} %get-tuple-element.40.ra_ref, ...), custom_call_target="tpu_custom_call" | custom-call | flops 1 | bytes 1 | tf_op jit(solution)/shard_map/pallas_call | solution.py:313
  23.8 1.3 %collective-permute-done.5.after_ref = bf16[1360,128]{1,0:T(8,128)(2,1)S(1)} collective-permute-done((bf16[1360,128]{1,0:T(8,128)(2,1)S(1)}, bf16[1360,128]{1,0:T(8,128)(2,1)S(1)}, u32[]{:S(2)}, u32[]{:S(2)}) %collective-permute-start.5) | collective-permute-done | bytes 348192 | tf_op jit(solution)/shard_map/ppermute | solution.py:597
  25.1 2.1 %shard_map.62.dec_begun = f32[128,48,128]{2,1,0:T(8,128)S(1)} custom-call(s32[128]{0:T(128)} %rad_ref.7, f32[4620,128]{1,0:T(8,128)S(1)} %get-tuple-element.43.order_ref.ra_begun, bf16[1360,128]{1,0:T(8,128)(2,1)S(1)} %collective-permute-done.4.before_ref, bf16[816,128]{1,0:T(8,128)(2,1)S(1)} %get-tuple-element.37.order_ref.before_rest, ...), custom_call_target="tpu_custom_call" | custom-call | flops 2000000000 | bytes 5000000 | tf_op jit(solution)/shard_map/pallas_call | solution.py:363
  27.2 0.4 collective-permute-done.6.refs_0_
  27.8 2.9 %shard_map.63.outer_ref.own_ref = bf16[34,128,128]{2,1,0:T(8,128)(2,1)S(1)} custom-call(s32[128]{0:T(128)} %rad_ref.7, f32[128,48,128]{2,1,0:T(8,128)S(1)} %shard_map.62.dec_begun, f32[4620,128]{1,0:T(8,128)S(1)} %get-tuple-element.43.order_ref.ra_begun, bf16[18,256,128]{2,1,0:T(8,128)(2,1)S(1)} %get-tuple-element.39.dec_ref, ...), custom_call_target="tpu_custom_call" | custom-call | flops 10000000000 | bytes 5000000 | tf_op jit(solution)/shard_map/pallas_call | solution.py:420
  30.8 2.0 %shard_map.64 = (f32[72,128]{1,0:T(8,128)S(1)}, f32[128,128]{1,0:T(8,128)S(1)}, bf16[78,128,128]{2,1,0:T(8,128)(2,1)}) custom-call(bf16[44,128,128]{2,1,0:T(8,128)(2,1)S(1)} %get-tuple-element.42.own_ref, bf16[44,128,128]{2,1,0:T(8,128)(2,1)S(1)} %collective-permute-done.3.other_ref, bf16[34,128,128]{2,1,0:T(8,128)(2,1)S(1)} %shard_map.63.outer_ref.own_ref, ...), custom_call_target="tpu_custom_call" | custom-call | flops 1000000000 | bytes 3000000 | tf_op jit(solution)/shard_map/pallas_call | solution.py:491
  32.8 0.7 %collective-permute-done.8.other_ref = bf16[34,128,128]{2,1,0:T(8,128)(2,1)S(1)} collective-permute-done((bf16[34,128,128]{2,1,0:T(8,128)(2,1)S(1)}, bf16[34,128,128]{2,1,0:T(8,128)(2,1)S(1)}, u32[]{:S(2)}, u32[]{:S(2)}) %collective-permute-start.8) | collective-permute-done | bytes 1114144 | tf_op jit(solution)/shard_map/ppermute | solution.py:568
  33.5 0.5 %shard_map.65 = f32[136,128]{1,0:T(8,128)S(1)} custom-call(f32[72,128]{1,0:T(8,128)S(1)} %get-tuple-element.51.folded_ref, f32[128,128]{1,0:T(8,128)S(1)} %get-tuple-element.52.cross_ref, bf16[34,128,128]{2,1,0:T(8,128)(2,1)S(1)} %shard_map.63.outer_ref.own_ref, bf16[34,128,128]{2,1,0:T(8,128)(2,1)S(1)} %collective-permute-done.8.other_ref, ...), custom_call_target="tpu_custom_call" | custom-call | tf_op jit(solution)/shard_map/pallas_call | solution.py:519
  34.0 0.9 %collective-permute-start.9 = (f32[136,128]{1,0:T(8,128)S(1)}, f32[136,128]{1,0:T(8,128)S(1)}, u32[]{:S(2)}, u32[]{:S(2)}) collective-permute-start(f32[136,128]{1,0:T(8,128)S(1)} %shard_map.65), channel_id=1, source_target_pairs={{0,2},{2,0},{1,3},{3,1},{4,6},{6,4},{5,7},{7,5},{8,10},{10,8},{9,1... | collective-permute-start | bytes 208904 | tf_op jit(solution)/shard_map/ppermute | solution.py:568
  34.9 3.5 %collective-permute-done.9 = f32[136,128]{1,0:T(8,128)S(1)} collective-permute-done((f32[136,128]{1,0:T(8,128)S(1)}, f32[136,128]{1,0:T(8,128)S(1)}, u32[]{:S(2)}, u32[]{:S(2)}) %collective-permute-start.9) | collective-permute-done | bytes 69664 | tf_op jit(solution)/shard_map/ppermute | solution.py:568
  38.4 1.2 %collective-permute-start.10 = (f32[136,128]{1,0:T(8,128)S(1)}, f32[136,128]{1,0:T(8,128)S(1)}, u32[]{:S(2)}, u32[]{:S(2)}) collective-permute-start(f32[136,128]{1,0:T(8,128)S(1)} %add.9), channel_id=1, source_target_pairs={{0,4},{4,0},{8,12},{12,8},{1,5},{5,1},{9,13},{13,9},{2,6},{6,2},{1... | collective-permute-start | bytes 208904 | tf_op jit(solution)/shard_map/ppermute | solution.py:568
  39.6 3.2 %collective-permute-done.10 = f32[136,128]{1,0:T(8,128)S(1)} collective-permute-done((f32[136,128]{1,0:T(8,128)S(1)}, f32[136,128]{1,0:T(8,128)S(1)}, u32[]{:S(2)}, u32[]{:S(2)}) %collective-permute-start.10) | collective-permute-done | bytes 69664 | tf_op jit(solution)/shard_map/ppermute | solution.py:568
  42.8 1.4 %collective-permute-start.11 = (f32[136,128]{1,0:T(8,128)S(1)}, f32[136,128]{1,0:T(8,128)S(1)}, u32[]{:S(2)}, u32[]{:S(2)}) collective-permute-start(f32[136,128]{1,0:T(8,128)S(1)} %add.10), channel_id=1, source_target_pairs={{0,8},{4,12},{8,0},{12,4},{1,9},{5,13},{9,1},{13,5},{2,10},{6,14},... | collective-permute-start | bytes 208904 | tf_op jit(solution)/shard_map/ppermute | solution.py:568
  44.2 4.7 %collective-permute-done.11 = f32[136,128]{1,0:T(8,128)S(1)} collective-permute-done((f32[136,128]{1,0:T(8,128)S(1)}, f32[136,128]{1,0:T(8,128)S(1)}, u32[]{:S(2)}, u32[]{:S(2)}) %collective-permute-start.11) | collective-permute-done | bytes 69664 | tf_op jit(solution)/shard_map/ppermute | solution.py:568
  48.9 1.2 %collective-permute-done.12.theirs_ref = f32[136,128]{1,0:T(8,128)S(1)} collective-permute-done((f32[136,128]{1,0:T(8,128)S(1)}, f32[136,128]{1,0:T(8,128)S(1)}, u32[]{:S(2)}, u32[]{:S(2)}) %collective-permute-start.12) | collective-permute-done | bytes 69664 | tf_op jit(solution)/shard_map/ppermute | solution.py:568
  50.2 0.9 %shard_map.66 = (f32[1,128]{1,0:T(1,128)}, f32[256,128]{1,0:T(8,128)}) custom-call(f32[136,128]{1,0:T(8,128)S(1)} %add.11.mine_ref, f32[136,128]{1,0:T(8,128)S(1)} %collective-permute-done.12.theirs_ref), custom_call_target="tpu_custom_call" | custom-call | tf_op jit(solution)/shard_map/pallas_call | solution.py:556
  (13 shorter events, 0.4 us)
Async XLA Ops:
  3.2 20.6 %collective-permute-start.4 = (bf16[1360,128]{1,0:T(8,128)(2,1)S(1)}, bf16[1360,128]{1,0:T(8,128)(2,1)S(1)}, u32[]{:S(2)}, u32[]{:S(2)}) collective-permute-start(bf16[1360,128]{1,0:T(8,128)(2,1)S(1)} %get-tuple-element.44), channel_id=1, source_target_pairs={{0,4},{4,8},{8,12},{12,0},{1,5},{5,9},{9,13},{13,1},{2,6},{6,10},{... | collective-permute-start | bytes 1044488 | tf_op jit(solution)/shard_map/ppermute | solution.py:597
  6.3 18.8 %collective-permute-start.5 = (bf16[1360,128]{1,0:T(8,128)(2,1)S(1)}, bf16[1360,128]{1,0:T(8,128)(2,1)S(1)}, u32[]{:S(2)}, u32[]{:S(2)}) collective-permute-start(bf16[1360,128]{1,0:T(8,128)(2,1)S(1)} %get-tuple-element.45), channel_id=1, source_target_pairs={{4,0},{8,4},{12,8},{0,12},{5,1},{9,5},{13,9},{1,13},{6,2},{10,6},{... | collective-permute-start | bytes 1044488 | tf_op jit(solution)/shard_map/ppermute | solution.py:597
  10.6 9.6 %collective-permute-start.2 = (bf16[1344,128]{1,0:T(8,128)(2,1)S(1)}, bf16[1344,128]{1,0:T(8,128)(2,1)S(1)}, u32[]{:S(2)}, u32[]{:S(2)}) collective-permute-start(bf16[1344,128]{1,0:T(8,128)(2,1)S(1)} %get-tuple-element.41), channel_id=1, source_target_pairs={{0,2},{2,0},{1,3},{3,1},{4,6},{6,4},{5,7},{7,5},{8,10},{10,8},{9,1... | collective-permute-start | bytes 1032200 | tf_op jit(solution)/shard_map/ppermute | solution.py:599
  12.3 15.3 %collective-permute-start.6 = (bf16[320,128]{1,0:T(8,128)(2,1)S(1)}, bf16[320,128]{1,0:T(8,128)(2,1)S(1)}, u32[]{:S(2)}, u32[]{:S(2)}) collective-permute-start(bf16[320,128]{1,0:T(8,128)(2,1)S(1)} %get-tuple-element.48), channel_id=1, source_target_pairs={{0,6},{2,4},{4,10},{6,8},{8,14},{10,12},{12,2},{14,0},{1,7},{3,5},... | collective-permute-start | bytes 245768 | tf_op jit(solution)/shard_map/ppermute | solution.py:576
  12.3 15.5 %collective-permute-start.7 = (bf16[320,128]{1,0:T(8,128)(2,1)S(1)}, bf16[320,128]{1,0:T(8,128)(2,1)S(1)}, u32[]{:S(2)}, u32[]{:S(2)}) collective-permute-start(bf16[320,128]{1,0:T(8,128)(2,1)S(1)} %get-tuple-element.49), channel_id=1, source_target_pairs={{0,14},{2,12},{4,2},{6,0},{8,6},{10,4},{12,10},{14,8},{1,15},{3,13... | collective-permute-start | bytes 245768 | tf_op jit(solution)/shard_map/ppermute | solution.py:576
  23.7 7.1 %collective-permute-start.3 = (bf16[44,128,128]{2,1,0:T(8,128)(2,1)S(1)}, bf16[44,128,128]{2,1,0:T(8,128)(2,1)S(1)}, u32[]{:S(2)}, u32[]{:S(2)}) collective-permute-start(bf16[44,128,128]{2,1,0:T(8,128)(2,1)S(1)} %get-tuple-element.42.own_ref), channel_id=1, source_target_pairs={{0,1},{1,0},{2,3},{3,2},{4,5},{5,4},{6,7},{7,6},{8,9},{9,8},{10,11... | collective-permute-start | bytes 4325384 | tf_op jit(solution)/shard_map/ppermute | solution.py:568
  27.8 3.0 %copy-start = (s32[78,128]{1,0:T(8,128)S(1)}, s32[78,128]{1,0:T(8,128)}, u32[]{:S(2)}) copy-start(s32[78,128]{1,0:T(8,128)} %valid_ref.3) | copy-start | bytes 119812
  30.7 2.8 %collective-permute-start.8 = (bf16[34,128,128]{2,1,0:T(8,128)(2,1)S(1)}, bf16[34,128,128]{2,1,0:T(8,128)(2,1)S(1)}, u32[]{:S(2)}, u32[]{:S(2)}) collective-permute-start(bf16[34,128,128]{2,1,0:T(8,128)(2,1)S(1)} %shard_map.63.outer_ref.own_ref), channel_id=1, source_target_pairs={{0,1},{1,0},{2,3},{3,2},{4,5},{5,4},{6,7},{7,6},{8,9},{9,8},{10,11... | collective-permute-start | bytes 3342344 | tf_op jit(solution)/shard_map/ppermute | solution.py:568
  34.0 4.4 %collective-permute-start.9 = (f32[136,128]{1,0:T(8,128)S(1)}, f32[136,128]{1,0:T(8,128)S(1)}, u32[]{:S(2)}, u32[]{:S(2)}) collective-permute-start(f32[136,128]{1,0:T(8,128)S(1)} %shard_map.65), channel_id=1, source_target_pairs={{0,2},{2,0},{1,3},{3,1},{4,6},{6,4},{5,7},{7,5},{8,10},{10,8},{9,1... | collective-permute-start | bytes 208904 | tf_op jit(solution)/shard_map/ppermute | solution.py:568
  38.4 4.4 %collective-permute-start.10 = (f32[136,128]{1,0:T(8,128)S(1)}, f32[136,128]{1,0:T(8,128)S(1)}, u32[]{:S(2)}, u32[]{:S(2)}) collective-permute-start(f32[136,128]{1,0:T(8,128)S(1)} %add.9), channel_id=1, source_target_pairs={{0,4},{4,0},{8,12},{12,8},{1,5},{5,1},{9,13},{13,9},{2,6},{6,2},{1... | collective-permute-start | bytes 208904 | tf_op jit(solution)/shard_map/ppermute | solution.py:568
  42.8 6.0 %collective-permute-start.11 = (f32[136,128]{1,0:T(8,128)S(1)}, f32[136,128]{1,0:T(8,128)S(1)}, u32[]{:S(2)}, u32[]{:S(2)}) collective-permute-start(f32[136,128]{1,0:T(8,128)S(1)} %add.10), channel_id=1, source_target_pairs={{0,8},{4,12},{8,0},{12,4},{1,9},{5,13},{9,1},{13,5},{2,10},{6,14},... | collective-permute-start | bytes 208904 | tf_op jit(solution)/shard_map/ppermute | solution.py:568
  48.9 1.3 %collective-permute-start.12 = (f32[136,128]{1,0:T(8,128)S(1)}, f32[136,128]{1,0:T(8,128)S(1)}, u32[]{:S(2)}, u32[]{:S(2)}) collective-permute-start(f32[136,128]{1,0:T(8,128)S(1)} %add.11.mine_ref), channel_id=1, source_target_pairs={{0,1},{1,0},{2,3},{3,2},{4,5},{5,4},{6,7},{7,6},{8,9},{9,8},{10,11... | collective-permute-start | bytes 208904 | tf_op jit(solution)/shard_map/ppermute | solution.py:568

commit v9 on v8

--- a/solution.py
+++ b/solution.py
@@ -435,7 +435,7 @@
 
 
 def add_products(total, row_refs, own_ref, valid_ref, first_row, rows, sums=None):
-    depth = max(d for d in range(1, 27) if rows % d == 0)
+    depth = max(d for d in range(1, 65) if rows % d == 0)
 
     def nt(a, b):
         return lax.dot_general(a, b, (((1,), (1,)), ((), ())), preferred_element_type=F32)

time: 51.4 us -> 51.7 us (level)
  Pallas kernels: 18.8 us -> 19.6 us
    pallas_call x1, Pallas kernels: 1.97 us -> 2.78 us  [own_gram(): pl.pallas_call(own_gram_kernel, out_shape=[pltpu.VMEM((chans // 2 + SUM_R...]
  transfers between devices with their start and end apart: 11 -> 11, of which waited for: 9 -> 8; matrix products, arithmetic and copies ran while one was open for 0% -> 0% of each run, Pallas kernels for 29% -> 30%
where the time goes in v9:
time: 51.7 us; the launch traced here: 51.5 us
  Pallas kernels  19.6 us (38%)
  waiting for transfers between devices  15.8 us (31%)
  starting transfers between devices  15.3 us (30%)
  between operations  0.76 us (1%)
    ppermute x6, waiting for transfers between devices, swap(): return lax.ppermute(array, axis, [(i, i ^ step) for i in range(size)])  12.8 us
    ppermute x2, starting transfers between devices, diagonal(): return lax.ppermute(array, ('ra', 'dec'), pairs)  4.72 us
    ppermute x6, starting transfers between devices, swap(): return lax.ppermute(array, axis, [(i, i ^ step) for i in range(size)])  3.65 us
    pallas_call x1, Pallas kernels, smooth_inner(): pl.pallas_call(functools.partial(inner_kernel, len(halos)), out_shape=[pl...  3.47 us
    ppermute x1, starting transfers between devices, per_device(): lax.ppermute(up_head, 'ra', up)  3.08 us
    pallas_call x1, Pallas kernels, smooth_outer(): pl.pallas_call(functools.partial(outer_kernel, len(corners)), out_shape=p...  2.9 us
    pallas_call x1, Pallas kernels, own_gram(): pl.pallas_call(own_gram_kernel, out_shape=[pltpu.VMEM((chans // 2 + SUM_R...  2.78 us
    pallas_call x1, Pallas kernels, gather(): pl.pallas_call(gather_kernel, out_shape=[pltpu.SMEM((1,), jnp.int32), hea...  2.56 us
  transfers between devices with their start and end apart: 11, of which 8 were waited for; matrix products, arithmetic and copies ran while one was open for 0% of the time, Pallas kernels for 30%

profile of v9, /device:TPU:0, one launch (start us, length us, event | category | flops | bytes accessed | tf_op | source)
XLA Modules:
  0.0 51.5 jit_solution(2199388606123766359)
XLA Ops:
  0.6 2.6 %shard_map.58 = (s32[1]{0:T(128)S(4)}, bf16[1360,128]{1,0:T(8,128)(2,1)S(1)}, bf16[816,128]{1,0:T(8,128)(2,1)S(1)}, bf16[1360,128]{1,0:T(8,128)(2,1)S(1)}, bf16[816,128]{1,0:T(8,128)(2,1)S(1)}) custom-call(s32[128]{0:T(128)} %rad_ref.7, bf16[78,128,128]{2,1,0:T(8,128)(2,1)} %bitcast.4), custom_call_target="tpu_custom_call" | custom-call | flops 1 | bytes 1 | tf_op jit(solution)/shard_map/pallas_call | solution.py:164
  3.2 3.1 %collective-permute-start.4 = (bf16[1360,128]{1,0:T(8,128)(2,1)S(1)}, bf16[1360,128]{1,0:T(8,128)(2,1)S(1)}, u32[]{:S(2)}, u32[]{:S(2)}) collective-permute-start(bf16[1360,128]{1,0:T(8,128)(2,1)S(1)} %get-tuple-element.44), channel_id=1, source_target_pairs={{0,4},{4,8},{8,12},{12,0},{1,5},{5,9},{9,13},{13,1},{2,6},{6,10},{... | collective-permute-start | bytes 1044488 | tf_op jit(solution)/shard_map/ppermute | solution.py:597
  6.3 2.1 %collective-permute-start.5 = (bf16[1360,128]{1,0:T(8,128)(2,1)S(1)}, bf16[1360,128]{1,0:T(8,128)(2,1)S(1)}, u32[]{:S(2)}, u32[]{:S(2)}) collective-permute-start(bf16[1360,128]{1,0:T(8,128)(2,1)S(1)} %get-tuple-element.45), channel_id=1, source_target_pairs={{4,0},{8,4},{12,8},{0,12},{5,1},{9,5},{13,9},{1,13},{6,2},{10,6},{... | collective-permute-start | bytes 1044488 | tf_op jit(solution)/shard_map/ppermute | solution.py:597
  8.4 2.2 %shard_map.60 = (bf16[1344,128]{1,0:T(8,128)(2,1)S(1)}, bf16[320,128]{1,0:T(8,128)(2,1)S(1)}, bf16[320,128]{1,0:T(8,128)(2,1)S(1)}) custom-call(s32[1]{0:T(128)S(4)} %get-tuple-element.34.order_ref, bf16[78,128,128]{2,1,0:T(8,128)(2,1)} %bitcast.5), custom_call_target="tpu_custom_call" | custom-call | flops 1 | bytes 1 | tf_op jit(solution)/shard_map/pallas_call | solution.py:239
  10.6 1.7 %collective-permute-start.2 = (bf16[1344,128]{1,0:T(8,128)(2,1)S(1)}, bf16[1344,128]{1,0:T(8,128)(2,1)S(1)}, u32[]{:S(2)}, u32[]{:S(2)}) collective-permute-start(bf16[1344,128]{1,0:T(8,128)(2,1)S(1)} %get-tuple-element.41), channel_id=1, source_target_pairs={{0,2},{2,0},{1,3},{3,1},{4,6},{6,4},{5,7},{7,5},{8,10},{10,8},{9,1... | collective-permute-start | bytes 1032200 | tf_op jit(solution)/shard_map/ppermute | solution.py:599
  12.3 4.7 %collective-permute-start.7 = (bf16[320,128]{1,0:T(8,128)(2,1)S(1)}, bf16[320,128]{1,0:T(8,128)(2,1)S(1)}, u32[]{:S(2)}, u32[]{:S(2)}) collective-permute-start(bf16[320,128]{1,0:T(8,128)(2,1)S(1)} %get-tuple-element.49), channel_id=1, source_target_pairs={{0,14},{2,12},{4,2},{6,0},{8,6},{10,4},{12,10},{14,8},{1,15},{3,13... | collective-permute-start | bytes 245768 | tf_op jit(solution)/shard_map/ppermute | solution.py:576
  17.0 2.1 %shard_map.59 = (bf16[18,256,128]{2,1,0:T(8,128)(2,1)S(1)}, bf16[18,96,80]{2,1,0:T(8,128)(2,1)S(1)}, bf16[18,48,48]{2,1,0:T(8,128)(2,1)S(1)}, f32[10692,128]{1,0:T(8,128)S(1)}) custom-call(bf16[816,128]{1,0:T(8,128)(2,1)S(1)} %get-tuple-element.37.order_ref.before_rest, bf16[78,128,128]{2,1,0:T(8,128)(2,1)} %bitcast.6), custom_call_target="tpu_custom_call" | custom-call | flops 100000 | bytes 100000 | tf_op jit(solution)/shard_map/pallas_call | solution.py:99
  19.1 1.0 %collective-permute-done.2.refs_0_ = bf16[1344,128]{1,0:T(8,128)(2,1)S(1)} collective-permute-done((bf16[1344,128]{1,0:T(8,128)(2,1)S(1)}, bf16[1344,128]{1,0:T(8,128)(2,1)S(1)}, u32[]{:S(2)}, u32[]{:S(2)}) %collective-permute-start.2) | collective-permute-done | bytes 344096 | tf_op jit(solution)/shard_map/ppermute | solution.py:599
  20.2 3.5 %shard_map.61 = (bf16[44,128,128]{2,1,0:T(8,128)(2,1)S(1)}, f32[4620,128]{1,0:T(8,128)S(1)}) custom-call(s32[128]{0:T(128)} %rad_ref.7, f32[10692,128]{1,0:T(8,128)S(1)} %get-tuple-element.38.own, bf16[18,256,128]{2,1,0:T(8,128)(2,1)S(1)} %get-tuple-element.39.dec_ref, bf16[18,96,80]{2,1,0:T(8,128)(2,1)S(1)} %get-tuple-element.40.ra_ref, ...), custom_call_target="tpu_custom_call" | custom-call | flops 1 | bytes 1 | tf_op jit(solution)/shard_map/pallas_call | solution.py:313
  23.8 1.3 %collective-permute-done.5.after_ref = bf16[1360,128]{1,0:T(8,128)(2,1)S(1)} collective-permute-done((bf16[1360,128]{1,0:T(8,128)(2,1)S(1)}, bf16[1360,128]{1,0:T(8,128)(2,1)S(1)}, u32[]{:S(2)}, u32[]{:S(2)}) %collective-permute-start.5) | collective-permute-done | bytes 348192 | tf_op jit(solution)/shard_map/ppermute | solution.py:597
  25.1 2.1 %shard_map.62.dec_begun = f32[128,48,128]{2,1,0:T(8,128)S(1)} custom-call(s32[128]{0:T(128)} %rad_ref.7, f32[4620,128]{1,0:T(8,128)S(1)} %get-tuple-element.43.order_ref.ra_begun, bf16[1360,128]{1,0:T(8,128)(2,1)S(1)} %collective-permute-done.4.before_ref, bf16[816,128]{1,0:T(8,128)(2,1)S(1)} %get-tuple-element.37.order_ref.before_rest, ...), custom_call_target="tpu_custom_call" | custom-call | flops 2000000000 | bytes 5000000 | tf_op jit(solution)/shard_map/pallas_call | solution.py:363
  27.2 0.4 collective-permute-done.6.refs_0_
  27.6 0.2 collective-permute-done.7.refs_1_
  27.8 2.9 %shard_map.63.outer_ref.own_ref = bf16[34,128,128]{2,1,0:T(8,128)(2,1)S(1)} custom-call(s32[128]{0:T(128)} %rad_ref.7, f32[128,48,128]{2,1,0:T(8,128)S(1)} %shard_map.62.dec_begun, f32[4620,128]{1,0:T(8,128)S(1)} %get-tuple-element.43.order_ref.ra_begun, bf16[18,256,128]{2,1,0:T(8,128)(2,1)S(1)} %get-tuple-element.39.dec_ref, ...), custom_call_target="tpu_custom_call" | custom-call | flops 10000000000 | bytes 5000000 | tf_op jit(solution)/shard_map/pallas_call | solution.py:420
  30.8 2.8 %shard_map.64 = (f32[72,128]{1,0:T(8,128)S(1)}, f32[128,128]{1,0:T(8,128)S(1)}, bf16[78,128,128]{2,1,0:T(8,128)(2,1)}) custom-call(bf16[44,128,128]{2,1,0:T(8,128)(2,1)S(1)} %get-tuple-element.42.own_ref, bf16[44,128,128]{2,1,0:T(8,128)(2,1)S(1)} %collective-permute-done.3.other_ref, bf16[34,128,128]{2,1,0:T(8,128)(2,1)S(1)} %shard_map.63.outer_ref.own_ref, ...), custom_call_target="tpu_custom_call" | custom-call | flops 1000000000 | bytes 3000000 | tf_op jit(solution)/shard_map/pallas_call | solution.py:491
  33.6 0.5 %shard_map.65 = f32[136,128]{1,0:T(8,128)S(1)} custom-call(f32[72,128]{1,0:T(8,128)S(1)} %get-tuple-element.51.folded_ref, f32[128,128]{1,0:T(8,128)S(1)} %get-tuple-element.52.cross_ref, bf16[34,128,128]{2,1,0:T(8,128)(2,1)S(1)} %shard_map.63.outer_ref.own_ref, bf16[34,128,128]{2,1,0:T(8,128)(2,1)S(1)} %collective-permute-done.8.other_ref, ...), custom_call_target="tpu_custom_call" | custom-call | tf_op jit(solution)/shard_map/pallas_call | solution.py:519
  34.1 0.9 %collective-permute-start.9 = (f32[136,128]{1,0:T(8,128)S(1)}, f32[136,128]{1,0:T(8,128)S(1)}, u32[]{:S(2)}, u32[]{:S(2)}) collective-permute-start(f32[136,128]{1,0:T(8,128)S(1)} %shard_map.65), channel_id=1, source_target_pairs={{0,2},{2,0},{1,3},{3,1},{4,6},{6,4},{5,7},{7,5},{8,10},{10,8},{9,1... | collective-permute-start | bytes 208904 | tf_op jit(solution)/shard_map/ppermute | solution.py:568
  35.0 3.8 %collective-permute-done.9 = f32[136,128]{1,0:T(8,128)S(1)} collective-permute-done((f32[136,128]{1,0:T(8,128)S(1)}, f32[136,128]{1,0:T(8,128)S(1)}, u32[]{:S(2)}, u32[]{:S(2)}) %collective-permute-start.9) | collective-permute-done | bytes 69664 | tf_op jit(solution)/shard_map/ppermute | solution.py:568
  38.8 1.2 %collective-permute-start.10 = (f32[136,128]{1,0:T(8,128)S(1)}, f32[136,128]{1,0:T(8,128)S(1)}, u32[]{:S(2)}, u32[]{:S(2)}) collective-permute-start(f32[136,128]{1,0:T(8,128)S(1)} %add.9), channel_id=1, source_target_pairs={{0,4},{4,0},{8,12},{12,8},{1,5},{5,1},{9,13},{13,9},{2,6},{6,2},{1... | collective-permute-start | bytes 208904 | tf_op jit(solution)/shard_map/ppermute | solution.py:568
  40.0 3.2 %collective-permute-done.10 = f32[136,128]{1,0:T(8,128)S(1)} collective-permute-done((f32[136,128]{1,0:T(8,128)S(1)}, f32[136,128]{1,0:T(8,128)S(1)}, u32[]{:S(2)}, u32[]{:S(2)}) %collective-permute-start.10) | collective-permute-done | bytes 69664 | tf_op jit(solution)/shard_map/ppermute | solution.py:568
  43.2 1.4 %collective-permute-start.11 = (f32[136,128]{1,0:T(8,128)S(1)}, f32[136,128]{1,0:T(8,128)S(1)}, u32[]{:S(2)}, u32[]{:S(2)}) collective-permute-start(f32[136,128]{1,0:T(8,128)S(1)} %add.10), channel_id=1, source_target_pairs={{0,8},{4,12},{8,0},{12,4},{1,9},{5,13},{9,1},{13,5},{2,10},{6,14},... | collective-permute-start | bytes 208904 | tf_op jit(solution)/shard_map/ppermute | solution.py:568
  44.5 4.7 %collective-permute-done.11 = f32[136,128]{1,0:T(8,128)S(1)} collective-permute-done((f32[136,128]{1,0:T(8,128)S(1)}, f32[136,128]{1,0:T(8,128)S(1)}, u32[]{:S(2)}, u32[]{:S(2)}) %collective-permute-start.11) | collective-permute-done | bytes 69664 | tf_op jit(solution)/shard_map/ppermute | solution.py:568
  49.3 1.2 %collective-permute-done.12.theirs_ref = f32[136,128]{1,0:T(8,128)S(1)} collective-permute-done((f32[136,128]{1,0:T(8,128)S(1)}, f32[136,128]{1,0:T(8,128)S(1)}, u32[]{:S(2)}, u32[]{:S(2)}) %collective-permute-start.12) | collective-permute-done | bytes 69664 | tf_op jit(solution)/shard_map/ppermute | solution.py:568
  50.5 0.9 %shard_map.66 = (f32[1,128]{1,0:T(1,128)}, f32[256,128]{1,0:T(8,128)}) custom-call(f32[136,128]{1,0:T(8,128)S(1)} %add.11.mine_ref, f32[136,128]{1,0:T(8,128)S(1)} %collective-permute-done.12.theirs_ref), custom_call_target="tpu_custom_call" | custom-call | tf_op jit(solution)/shard_map/pallas_call | solution.py:556
  (13 shorter events, 0.3 us)
Async XLA Ops:
  3.2 20.6 %collective-permute-start.4 = (bf16[1360,128]{1,0:T(8,128)(2,1)S(1)}, bf16[1360,128]{1,0:T(8,128)(2,1)S(1)}, u32[]{:S(2)}, u32[]{:S(2)}) collective-permute-start(bf16[1360,128]{1,0:T(8,128)(2,1)S(1)} %get-tuple-element.44), channel_id=1, source_target_pairs={{0,4},{4,8},{8,12},{12,0},{1,5},{5,9},{9,13},{13,1},{2,6},{6,10},{... | collective-permute-start | bytes 1044488 | tf_op jit(solution)/shard_map/ppermute | solution.py:597
  6.3 18.8 %collective-permute-start.5 = (bf16[1360,128]{1,0:T(8,128)(2,1)S(1)}, bf16[1360,128]{1,0:T(8,128)(2,1)S(1)}, u32[]{:S(2)}, u32[]{:S(2)}) collective-permute-start(bf16[1360,128]{1,0:T(8,128)(2,1)S(1)} %get-tuple-element.45), channel_id=1, source_target_pairs={{4,0},{8,4},{12,8},{0,12},{5,1},{9,5},{13,9},{1,13},{6,2},{10,6},{... | collective-permute-start | bytes 1044488 | tf_op jit(solution)/shard_map/ppermute | solution.py:597
  10.6 9.6 %collective-permute-start.2 = (bf16[1344,128]{1,0:T(8,128)(2,1)S(1)}, bf16[1344,128]{1,0:T(8,128)(2,1)S(1)}, u32[]{:S(2)}, u32[]{:S(2)}) collective-permute-start(bf16[1344,128]{1,0:T(8,128)(2,1)S(1)} %get-tuple-element.41), channel_id=1, source_target_pairs={{0,2},{2,0},{1,3},{3,1},{4,6},{6,4},{5,7},{7,5},{8,10},{10,8},{9,1... | collective-permute-start | bytes 1032200 | tf_op jit(solution)/shard_map/ppermute | solution.py:599
  12.3 15.3 %collective-permute-start.6 = (bf16[320,128]{1,0:T(8,128)(2,1)S(1)}, bf16[320,128]{1,0:T(8,128)(2,1)S(1)}, u32[]{:S(2)}, u32[]{:S(2)}) collective-permute-start(bf16[320,128]{1,0:T(8,128)(2,1)S(1)} %get-tuple-element.48), channel_id=1, source_target_pairs={{0,6},{2,4},{4,10},{6,8},{8,14},{10,12},{12,2},{14,0},{1,7},{3,5},... | collective-permute-start | bytes 245768 | tf_op jit(solution)/shard_map/ppermute | solution.py:576
  12.3 15.5 %collective-permute-start.7 = (bf16[320,128]{1,0:T(8,128)(2,1)S(1)}, bf16[320,128]{1,0:T(8,128)(2,1)S(1)}, u32[]{:S(2)}, u32[]{:S(2)}) collective-permute-start(bf16[320,128]{1,0:T(8,128)(2,1)S(1)} %get-tuple-element.49), channel_id=1, source_target_pairs={{0,14},{2,12},{4,2},{6,0},{8,6},{10,4},{12,10},{14,8},{1,15},{3,13... | collective-permute-start | bytes 245768 | tf_op jit(solution)/shard_map/ppermute | solution.py:576
  23.7 7.1 %collective-permute-start.3 = (bf16[44,128,128]{2,1,0:T(8,128)(2,1)S(1)}, bf16[44,128,128]{2,1,0:T(8,128)(2,1)S(1)}, u32[]{:S(2)}, u32[]{:S(2)}) collective-permute-start(bf16[44,128,128]{2,1,0:T(8,128)(2,1)S(1)} %get-tuple-element.42.own_ref), channel_id=1, source_target_pairs={{0,1},{1,0},{2,3},{3,2},{4,5},{5,4},{6,7},{7,6},{8,9},{9,8},{10,11... | collective-permute-start | bytes 4325384 | tf_op jit(solution)/shard_map/ppermute | solution.py:568
  27.8 3.0 %copy-start = (s32[78,128]{1,0:T(8,128)S(1)}, s32[78,128]{1,0:T(8,128)}, u32[]{:S(2)}) copy-start(s32[78,128]{1,0:T(8,128)} %valid_ref.3) | copy-start | bytes 119812
  30.7 2.9 %collective-permute-start.8 = (bf16[34,128,128]{2,1,0:T(8,128)(2,1)S(1)}, bf16[34,128,128]{2,1,0:T(8,128)(2,1)S(1)}, u32[]{:S(2)}, u32[]{:S(2)}) collective-permute-start(bf16[34,128,128]{2,1,0:T(8,128)(2,1)S(1)} %shard_map.63.outer_ref.own_ref), channel_id=1, source_target_pairs={{0,1},{1,0},{2,3},{3,2},{4,5},{5,4},{6,7},{7,6},{8,9},{9,8},{10,11... | collective-permute-start | bytes 3342344 | tf_op jit(solution)/shard_map/ppermute | solution.py:568
  34.1 4.6 %collective-permute-start.9 = (f32[136,128]{1,0:T(8,128)S(1)}, f32[136,128]{1,0:T(8,128)S(1)}, u32[]{:S(2)}, u32[]{:S(2)}) collective-permute-start(f32[136,128]{1,0:T(8,128)S(1)} %shard_map.65), channel_id=1, source_target_pairs={{0,2},{2,0},{1,3},{3,1},{4,6},{6,4},{5,7},{7,5},{8,10},{10,8},{9,1... | collective-permute-start | bytes 208904 | tf_op jit(solution)/shard_map/ppermute | solution.py:568
  38.8 4.4 %collective-permute-start.10 = (f32[136,128]{1,0:T(8,128)S(1)}, f32[136,128]{1,0:T(8,128)S(1)}, u32[]{:S(2)}, u32[]{:S(2)}) collective-permute-start(f32[136,128]{1,0:T(8,128)S(1)} %add.9), channel_id=1, source_target_pairs={{0,4},{4,0},{8,12},{12,8},{1,5},{5,1},{9,13},{13,9},{2,6},{6,2},{1... | collective-permute-start | bytes 208904 | tf_op jit(solution)/shard_map/ppermute | solution.py:568
  43.2 6.0 %collective-permute-start.11 = (f32[136,128]{1,0:T(8,128)S(1)}, f32[136,128]{1,0:T(8,128)S(1)}, u32[]{:S(2)}, u32[]{:S(2)}) collective-permute-start(f32[136,128]{1,0:T(8,128)S(1)} %add.10), channel_id=1, source_target_pairs={{0,8},{4,12},{8,0},{12,4},{1,9},{5,13},{9,1},{13,5},{2,10},{6,14},... | collective-permute-start | bytes 208904 | tf_op jit(solution)/shard_map/ppermute | solution.py:568
  49.2 1.3 %collective-permute-start.12 = (f32[136,128]{1,0:T(8,128)S(1)}, f32[136,128]{1,0:T(8,128)S(1)}, u32[]{:S(2)}, u32[]{:S(2)}) collective-permute-start(f32[136,128]{1,0:T(8,128)S(1)} %add.11.mine_ref), channel_id=1, source_target_pairs={{0,1},{1,0},{2,3},{3,2},{4,5},{5,4},{6,7},{7,6},{8,9},{9,8},{10,11... | collective-permute-start | bytes 208904 | tf_op jit(solution)/shard_map/ppermute | solution.py:568
